TPU v7x, 32 devices: a whole 2x2x4 slice. The times are simulated.
32 devices in a mesh: groups: 2 (over y), dp: 4 (over z), tensor: 4 (over x, core).
Axes of the slice: x: 2, y: 2, z: 4, core: 2. Of those that a mesh axis runs over, the one named last changes fastest.
Arguments:
- tokens: bfloat16 [2048, 8192], P(('groups', 'dp'), 'tensor'), parts along dimension 0, may hold values from -6 to 6
- value_weight: bfloat16 [8192, 1024], P('tensor', 'dp'), may hold values from -0.0625 to 0.0625
- adapter_down_weight: bfloat16 [8, 8192, 64], P('dp', 'tensor'), may hold values from -0.0625 to 0.0625
- adapter_up_weight: bfloat16 [8, 64, 1024], P('dp', None, 'tensor'), may hold values from -0.75 to 0.75
- adapter_slot_table: int32 [16], P('groups'), parts along dimension 0, may hold values from 0 to 7, as said below
- adapter_per_block: int32 [32], P(('groups', 'dp')), parts along dimension 0, may hold values from 0 to 7, as said below
- request_rows_per_block: int32 [32], P(('groups', 'dp')), parts along dimension 0, may hold values from 1 to 64
Outputs:
- mixed: bfloat16 [2048, 1024], P(('groups', 'dp'), 'tensor'), parts along dimension 0
There are 2 independent parts, one for each index of `groups`. A program takes and returns all parts, laid end to end along the dimension named above; an argument that names none is the same for every part. Nothing has to cross between parts.
Inputs may be any that keep to these rules, and one draw needn't show every extreme that they name: `adapter_slot_table`: every slot once. Slot s is held by dp index s // 2. `adapter_per_block`: blocks k * 4 to (k + 1) * 4 - 1 stand on dp index k. The blocks of one dp index name adapters held by all 4 dp indices, one block each.
All inputs are finite; a program needn't handle non-finite values.
Results may differ from a plain program's by a relative error of at most 0.014.
Values may be sent and summed in bfloat16 or wider, within the bound.
No kernel may reach another device: no remote copies, remote signals or barrier semaphores. Data moves between devices by JAX's collectives and lax.ppermute only.
A program may use at most 64 MiB of HBM per device.

v0:
```python
import jax
import jax.numpy as jnp
from jax import lax
from jax.sharding import PartitionSpec as P


def local(
    tokens,
    value_weight,
    adapter_down_weight,
    adapter_up_weight,
    adapter_slot_table,
    adapter_per_block,
    request_rows_per_block,
):
    dp_count = lax.axis_size("dp")
    blocks = adapter_per_block.shape[0]
    tok_rows = tokens.shape[0]
    block_len = tok_rows // blocks
    feature_total = tokens.shape[1]
    adapter_total = adapter_down_weight.shape[0]
    adapter_rank_width = adapter_down_weight.shape[2]
    column_total = adapter_up_weight.shape[2]
    partial_value = jnp.dot(
        tokens,
        lax.all_gather(value_weight, "dp", axis=1, tiled=True),
        preferred_element_type=jnp.float32,
    )
    summed = lax.psum(partial_value.astype(jnp.bfloat16), "tensor").astype(jnp.float32)
    base_cols = lax.dynamic_slice_in_dim(
        summed, lax.axis_index("tensor") * column_total, column_total, 1
    )
    matches = (
        adapter_per_block[:, None]
        == jnp.arange(adapter_slot_table.shape[0], dtype=jnp.int32)[None, :]
    )
    slot_index = jnp.sum(jnp.where(matches, adapter_slot_table[None, :], 0), axis=1)
    holder = slot_index // adapter_total
    local_slot = slot_index % adapter_total
    route_map = (holder[None, :] == jnp.arange(dp_count, dtype=jnp.int32)[:, None]).astype(
        jnp.bfloat16
    )
    local_onehot = (
        local_slot[:, None] == jnp.arange(adapter_total, dtype=jnp.int32)[None, :]
    ).astype(jnp.bfloat16)
    wanted_hot = jnp.dot(route_map, local_onehot, preferred_element_type=jnp.bfloat16)
    block_input = tokens.reshape(blocks, block_len, feature_total)
    sent_x = jnp.dot(
        route_map,
        block_input.reshape(blocks, block_len * feature_total),
        preferred_element_type=jnp.bfloat16,
    )
    sent_x = sent_x.reshape(dp_count, block_len, feature_total)
    recv_x, recv_hot = (
        lax.all_to_all(sent_x, "dp", split_axis=0, concat_axis=0, tiled=True),
        lax.all_to_all(wanted_hot, "dp", split_axis=0, concat_axis=0, tiled=True),
    )
    flat_down_weight = jnp.transpose(adapter_down_weight, (1, 0, 2)).reshape(
        feature_total, adapter_total * adapter_rank_width
    )
    every = jnp.einsum("nbf,fq->nbq", recv_x, flat_down_weight, preferred_element_type=jnp.float32)
    every = every.reshape(dp_count, block_len, adapter_total, adapter_rank_width)
    picked = jnp.sum(every * recv_hot.astype(jnp.float32)[:, None, :, None], axis=2)
    reduced_input = lax.psum(picked.astype(jnp.bfloat16), "tensor")
    spread_rows = (recv_hot[:, None, :, None] * reduced_input[:, :, None, :]).reshape(
        dp_count, block_len, adapter_total * adapter_rank_width
    )
    flat_up_weight = adapter_up_weight.reshape(adapter_total * adapter_rank_width, column_total)
    delta_rows = jnp.einsum(
        "nbq,qc->nbc", spread_rows, flat_up_weight, preferred_element_type=jnp.float32
    ).astype(jnp.bfloat16)
    returned = lax.all_to_all(delta_rows, "dp", split_axis=0, concat_axis=0, tiled=True)
    own_delta = jnp.dot(
        route_map.T,
        returned.reshape(dp_count, block_len * column_total),
        preferred_element_type=jnp.bfloat16,
    )
    own_delta = own_delta.reshape(tok_rows, column_total)
    live_rows = (
        jnp.arange(block_len, dtype=jnp.int32)[None, :] < request_rows_per_block[:, None]
    ).reshape(tok_rows)
    mixed = jnp.where(
        live_rows[:, None], base_cols + own_delta.astype(jnp.float32), jnp.float32(0.0)
    )
    return mixed.astype(jnp.bfloat16)


def solution(mesh):
    placed = (
        P(("groups", "dp"), "tensor"),
        P("tensor", "dp"),
        P("dp", "tensor", None),
        P("dp", None, "tensor"),
        P("groups"),
        P(("groups", "dp")),
        P(("groups", "dp")),
    )
    return jax.shard_map(
        local, mesh=mesh, in_specs=placed, out_specs=P(("groups", "dp"), "tensor"), check_vma=False
    )
```

profile of v0, /device:TPU:0, one launch (start us, length us, event | category | flops | bytes accessed | tf_op | source)
XLA Modules:
  0.0 164.9 jit_solution(12876740926960132047)
XLA Ops:
  6.5 0.7 all-gather.2.cloned.1.call-update
  7.3 0.9 select_reduce_fusion
  8.1 0.3 convolution_bitcast_fusion.1
  8.4 0.7 copy.19
  9.1 6.3 %all-to-all-start = ((bf16[4,1,2]{2,1,0:T(2,128)(2,1)}), bf16[4,1,2]{2,1,0:T(2,128)(2,1)S(1)}, u32[]{:S(2)}, u32[]{:S(2)}) async-start(bf16[4,1,2]{2,1,0:T(2,128)(2,1)} %copy.19), calls=%async_computation | async-start | bytes 4096 | tf_op jit(solution)/shard_map/all_to_all | solution.py:56
  15.4 2.0 %reshape_reshape.3 = bf16[4,131072]{1,0:T(4,128)(2,1)S(1)} reshape(bf16[256,2048]{1,0:T(8,128)(2,1)} %param.7) | data formatting | bytes 2097152 | tf_op jit(solution)/shard_map/reshape;reshape | solution.py:50
  17.4 0.0 copy-start.2
  17.4 0.0 copy-start.1
  17.4 0.7 fusion.9
  18.1 1.6 copy.22
  19.7 1.2 all-to-all-done
  20.9 3.9 %all-to-all-start.1 = ((bf16[4,64,2048]{2,1,0:T(8,128)(2,1)}), bf16[4,64,2048]{2,1,0:T(8,128)(2,1)S(1)}, u32[]{:S(2)}, u32[]{:S(2)}) async-start(bf16[4,64,2048]{2,1,0:T(8,128)(2,1)} %copy.22), calls=%async_computation.1 | async-start | bytes 2097152 | tf_op jit(solution)/shard_map/all_to_all | solution.py:55
  24.8 0.1 copy.20
  24.9 0.1 copy.21
  25.0 0.1 copy.23
  25.1 55.6 %all-to-all-done.1 = bf16[4,64,2048]{2,1,0:T(8,128)(2,1)S(1)} async-done(((bf16[4,64,2048]{2,1,0:T(8,128)(2,1)}), bf16[4,64,2048]{2,1,0:T(8,128)(2,1)S(1)}, u32[]{:S(2)}, u32[]{:S(2)}) %all-to-all-start.1) | async-done | bytes 1048608 | tf_op jit(solution)/shard_map/all_to_all | solution.py:55
  80.7 0.5 fusion.1
  81.1 12.7 %psum.15 = bf16[4,64,64]{2,1,0:T(8,128)(2,1)S(1)} all-reduce(bf16[4,64,64]{2,1,0:T(8,128)(2,1)S(1)} %fusion.1), channel_id=1, replica_groups=mesh['groups'=2,'dp'=4,'tensor'=4] {'tensor'}, use_global_device_ids=true, to_apply=%region_3.4 | all-reduce | flops 16384 | bytes 65536 | tf_op jit(solution)/shard_map/psum | solution.py:64
  93.8 0.0 copy-start.3
  93.8 1.0 fusion
  94.8 3.3 %all-to-all-start.2 = ((bf16[4,64,256]{2,1,0:T(8,128)(2,1)}), bf16[4,64,256]{2,1,0:T(8,128)(2,1)S(1)}, u32[]{:S(2)}, u32[]{:S(2)}) async-start(bf16[4,64,256]{2,1,0:T(8,128)(2,1)} %fusion), calls=%async_computation.2 | async-start | bytes 262144 | tf_op jit(solution)/shard_map/all_to_all | solution.py:72
  98.1 0.0 all-reduce.2.cloned.1.call-start
  98.2 20.5 %all-gather.2.cloned.1.call-done = bf16[2048,1024]{1,0:T(8,128)(2,1)} async-done(((bf16[2048,256]{1,0:T(8,128)(2,1)}), bf16[2048,1024]{1,0:T(8,128)(2,1)}) %all-gather.2.cloned.1.call-update) | async-done | bytes 4194320 | tf_op jit(solution)/shard_map/all_gather | solution.py:26
  118.7 4.3 %convolution_convert_fusion.1 = bf16[256,1024]{1,0:T(8,128)(2,1)} fusion(bf16[256,2048]{1,0:T(8,128)(2,1)S(1)} %copy-done.1, bf16[2048,1024]{1,0:T(8,128)(2,1)} %all-gather.2.cloned.1.call-done), kind=kOutput, calls=%fused_computation.1 | convolution fusion | flops 1074003968 | bytes 5767168 | tf_op jit(solution)/shard_map/dot_general | solution.py:24
  122.9 0.0 all-reduce.2.cloned.1.call-update
  123.0 0.1 iota_compare_fusion.5
  123.1 0.1 lt.32
  123.1 0.1 copy.26
  123.3 0.3 convolution_convert_fusion
  123.5 0.2 reshape.74
  123.7 32.7 %all-reduce.2.cloned.1.call-done = bf16[256,1024]{1,0:T(8,128)(2,1)} async-done(((bf16[256,1024]{1,0:T(8,128)(2,1)}), bf16[256,1024]{1,0:T(8,128)(2,1)}) %all-reduce.2.cloned.1.call-update) | async-done | bytes 524304 | tf_op jit(solution)/shard_map/psum | solution.py:29
  156.4 1.7 %select_convert_fusion = bf16[256,256]{1,0:T(8,128)(2,1)} fusion(f32[256,256]{1,0:T(8,128)S(1)} %reshape.74, bf16[256,1024]{1,0:T(8,128)(2,1)} %all-reduce.2.cloned.1.call-done, s32[]{:T(128)S(6)} %select_n.31, pred[256]{0:T(512)(128)(4,1)S(1)} %lt.32), kind=kLoop, calls=%fused_computation.9 | loop fusion | flops 262144 | bytes 524548 | tf_op jit(solution)/shard_map/convert_element_type | solution.py:85
  (9 shorter events, 0.0 us)
Async XLA Ops:
  6.5 74.1 %copy-start = (bf16[2,2048,64]{1,2,0:T(8,128)(2,1)S(1)}, bf16[2,2048,64]{1,2,0:T(8,128)(2,1)}, u32[]{:S(2)}) copy-start(bf16[2,2048,64]{1,2,0:T(8,128)(2,1)} %param.9) | copy-start | bytes 1572868
  6.5 112.1 %all-gather.2.cloned.1.call-start = ((), (), s32[]{:S(2)}) async-start(), calls=%async_computation.3 | async-start | bytes 5242880 | tf_op jit(solution)/shard_map/all_gather | solution.py:26
  9.1 11.8 %all-to-all-start = ((bf16[4,1,2]{2,1,0:T(2,128)(2,1)}), bf16[4,1,2]{2,1,0:T(2,128)(2,1)S(1)}, u32[]{:S(2)}, u32[]{:S(2)}) async-start(bf16[4,1,2]{2,1,0:T(2,128)(2,1)} %copy.19), calls=%async_computation | async-start | bytes 4096 | tf_op jit(solution)/shard_map/all_to_all | solution.py:56
  17.4 76.4 %copy-start.2 = (bf16[2,64,256]{2,1,0:T(8,128)(2,1)S(1)}, bf16[2,64,256]{2,1,0:T(8,128)(2,1)}, u32[]{:S(2)}) copy-start(bf16[2,64,256]{2,1,0:T(8,128)(2,1)} %param.10) | copy-start | bytes 196612
  17.4 101.3 %copy-start.1 = (bf16[256,2048]{1,0:T(8,128)(2,1)S(1)}, bf16[256,2048]{1,0:T(8,128)(2,1)}, u32[]{:S(2)}) copy-start(bf16[256,2048]{1,0:T(8,128)(2,1)} %param.7) | copy-start | bytes 3145732
  20.9 59.8 %all-to-all-start.1 = ((bf16[4,64,2048]{2,1,0:T(8,128)(2,1)}), bf16[4,64,2048]{2,1,0:T(8,128)(2,1)S(1)}, u32[]{:S(2)}, u32[]{:S(2)}) async-start(bf16[4,64,2048]{2,1,0:T(8,128)(2,1)} %copy.22), calls=%async_computation.1 | async-start | bytes 2097152 | tf_op jit(solution)/shard_map/all_to_all | solution.py:55
  93.8 29.1 %copy-start.3 = (s32[4]{0:T(128)S(1)}, s32[4]{0:T(128)}, u32[]{:S(2)}) copy-start(s32[4]{0:T(128)} %param.13) | copy-start | bytes 52
  94.8 28.4 %all-to-all-start.2 = ((bf16[4,64,256]{2,1,0:T(8,128)(2,1)}), bf16[4,64,256]{2,1,0:T(8,128)(2,1)S(1)}, u32[]{:S(2)}, u32[]{:S(2)}) async-start(bf16[4,64,256]{2,1,0:T(8,128)(2,1)} %fusion), calls=%async_computation.2 | async-start | bytes 262144 | tf_op jit(solution)/shard_map/all_to_all | solution.py:72
  98.1 58.3 %all-reduce.2.cloned.1.call-start = ((), (), s32[]{:S(2)}) async-start(), calls=%async_computation.4 | async-start | bytes 1048576 | tf_op jit(solution)/shard_map/psum | solution.py:29
Sparse Core Ops, SparseCore 0:
  8.9 109.6 all-gather.1
  123.1 33.2 all-reduce.1
where the time goes:
time: 165 us
  waiting for transfers between devices  111 us (67%)
  starting transfers between devices  13.6 us (8%)
  between operations  13.5 us (8%)
  blocking collectives  12.7 us (8%)
  matrix products  6.94 us (4%)
  local copies, waits for them, and re-layouts  4.95 us (3%)
  other arithmetic  2.61 us (2%)
    all_to_all x1, waiting for transfers between devices, local(): lax.all_to_all(sent_x, 'dp', split_axis=0, concat_axis=0, tiled=True)  55.6 us
    psum x1, waiting for transfers between devices, local(): lax.psum(partial_value.astype(jnp.bfloat16), 'tensor').astype(jnp.float32)  32.7 us
    all_gather x1, waiting for transfers between devices, local(): lax.all_gather(value_weight, 'dp', axis=1, tiled=True)  20.5 us
    psum x1, blocking collectives, local(): reduced_input = lax.psum(picked.astype(jnp.bfloat16), 'tensor')  12.7 us
    all_to_all x1, starting transfers between devices, local(): lax.all_to_all(wanted_hot, 'dp', split_axis=0, concat_axis=0, tiled=True)  6.32 us
    dot_general x1, matrix products, local(): jnp.dot(tokens, lax.all_gather(value_weight, 'dp', axis=1, tiled=True), p...  4.28 us
    all_to_all x1, starting transfers between devices, local(): lax.all_to_all(sent_x, 'dp', split_axis=0, concat_axis=0, tiled=True)  3.9 us
    all_to_all x1, starting transfers between devices, local(): lax.all_to_all(delta_rows, 'dp', split_axis=0, concat_axis=0, tiled=True)  3.33 us
  transfers between devices with their start and end apart: 5, of which 4 were waited for; matrix products, arithmetic and copies ran while one was open for 8% of the time, Pallas kernels for 0%

commit v1 on v0

--- a/solution.py
+++ b/solution.py
@@ -1,7 +1,313 @@
 import jax
 import jax.numpy as jnp
 from jax import lax
+from jax.experimental import pallas as pl
+from jax.experimental.pallas import tpu as pltpu
 from jax.sharding import PartitionSpec as P
+
+AXES = ("groups", "dp", "tensor")
+LANES = 128
+F32 = jnp.float32
+BF16 = jnp.bfloat16
+VMEM = pl.BlockSpec(memory_space=pltpu.VMEM)
+SMEM = pl.BlockSpec(memory_space=pltpu.SMEM)
+
+
+def call(body, name, outs, ins):
+    return pl.pallas_call(
+        body,
+        name=name,
+        out_shape=outs,
+        in_specs=[SMEM] + [VMEM] * (len(ins) - 1),
+        out_specs=jax.tree.map(lambda _: VMEM, outs),
+        compiler_params=pltpu.CompilerParams(vmem_limit_bytes=40 * 2**20),
+    )(*ins)
+
+
+def local_line(sizes, tokens, value_weight, down, up, slot_table, per_block, live_rows):
+    groups, dp, tensor = sizes
+    y, z, t = (lax.axis_index(a) for a in AXES)
+    rows, feats = tokens.shape
+    blocks = per_block.shape[0]
+    block_len = rows // blocks
+    per_dev, _, rank = down.shape
+    out_cols = up.shape[2]
+    half_cols = value_weight.shape[1] // groups
+    half = feats // 2
+    low = half * rank // LANES
+    up_rows = per_dev * rank * out_cols // LANES
+    pairs = dp // 2
+
+    def device(a, b, c):
+        return (a * dp + b) * tensor + c
+
+    def send(x, where):
+        perm = []
+        for a in range(groups):
+            for b in range(dp):
+                for c in range(tensor):
+                    to = where(a, b, c)
+                    if to is not None:
+                        perm.append((device(a, b, c), device(*to)))
+        return lax.ppermute(x, AXES, perm)
+
+    def rise(x, hop):
+        return send(x, lambda a, b, c: (a, b + 1, c) if hop - 1 <= b < dp - 1 else None)
+
+    def fall(x, hop):
+        return send(x, lambda a, b, c: (a, b - 1, c) if 0 < b <= dp - hop else None)
+
+    own_ints = jnp.concatenate([per_block, slot_table])
+    swap = lambda a, b, c: (1 - a, b, c)
+    other_ints = send(own_ints, swap)
+    place = jnp.stack([y, z, t]).astype(jnp.int32)
+    ints = jnp.concatenate([place, own_ints, other_ints])
+    n_ints = own_ints.shape[0]
+
+    def slot_of(ints_ref, which, k):
+        base = 3 + which * n_ints
+        return ints_ref[base + blocks + ints_ref[base + k]]
+
+    def pack(ints_ref, w_ref, d_ref, u_ref, l_ref, h_ref):
+        me = ints_ref[0]
+        cols = pl.ds(pl.multiple_of(me * half_cols, LANES), half_cols)
+        for part, ref in ((0, l_ref), (1, h_ref)):
+            ref[0:half, :] = w_ref[pl.ds(part * half, half), cols]
+            for i in range(half // LANES):
+                at = part * half + i * LANES
+                ref[half + i * rank : half + (i + 1) * rank, :] = d_ref[me, :, at : at + LANES]
+        for s in range(per_dev):
+            for v in range(out_cols // LANES):
+                at = half + low + (s * (out_cols // LANES) + v) * rank
+                l_ref[at : at + rank, :] = u_ref[s, :, v * LANES : (v + 1) * LANES]
+
+    l_shape = jax.ShapeDtypeStruct((half + low + up_rows, LANES), BF16)
+    h_shape = jax.ShapeDtypeStruct((half + low, LANES), BF16)
+    own_l, own_h = call(
+        pack,
+        "pack",
+        (l_shape, h_shape),
+        (place, value_weight, jnp.transpose(down, (0, 2, 1)), up),
+    )
+
+    rise_l, rise_h, fall_l, fall_h = [own_l], [own_h], [own_l], [own_h]
+    rise_l.append(rise(own_l, 1))
+    fall_l.append(fall(own_l, 1))
+    other_tokens = send(tokens, swap)
+    rise_h.append(rise(own_h, 1))
+    fall_h.append(fall(own_h, 1))
+    for hop in range(2, dp):
+        rise_l.append(rise(rise_l[-1], hop))
+        fall_l.append(fall(fall_l[-1], hop))
+        rise_h.append(rise(rise_h[-1], hop))
+        fall_h.append(fall(fall_h[-1], hop))
+
+    def product(ints_ref, tok_refs, l_ref, h_ref, holder, out_ref, s_ref):
+        mine = per_dev * holder + ints_ref[0]
+        for which, tok in enumerate(tok_refs):
+            x_l, x_h = tok[:, 0:half], tok[:, half:feats]
+            at = pl.ds(which * rows, rows)
+            out_ref[at, :] = jnp.dot(
+                x_l, l_ref[0:half, :], preferred_element_type=F32
+            ) + jnp.dot(x_h, h_ref[0:half, :], preferred_element_type=F32)
+            shrink = jnp.zeros((rows, rank), F32)
+            for x, ref in ((x_l, l_ref), (x_h, h_ref)):
+                flat = jnp.concatenate(
+                    [
+                        ref[half + i * rank : half + (i + 1) * rank, :]
+                        for i in range(half // LANES)
+                    ],
+                    axis=1,
+                )
+                shrink += lax.dot_general(
+                    x, flat, (((1,), (1,)), ((), ())), preferred_element_type=F32
+                )
+            for k in range(blocks):
+                @pl.when(slot_of(ints_ref, which, k) == mine)
+                def _():
+                    s_ref[pl.ds(which * rows + k * block_len, block_len), :] = shrink[
+                        k * block_len : (k + 1) * block_len, :
+                    ]
+
+    part_shape = jax.ShapeDtypeStruct((groups * rows, half_cols), F32)
+    s_shape = jax.ShapeDtypeStruct((groups * rows, rank), F32)
+
+    def own_product(ints_ref, a_ref, b_ref, l_ref, h_ref, out_ref, s_ref):
+        s_ref[...] = jnp.zeros_like(s_ref)
+        product(ints_ref, (a_ref, b_ref), l_ref, h_ref, ints_ref[1], out_ref, s_ref)
+
+    def hop_product(hop):
+        def body(ints_ref, a_ref, b_ref, rl, rh, fl, fh, s_in, r_out, f_out, s_ref):
+            here = ints_ref[1]
+            s_ref[...] = s_in[...]
+
+            @pl.when(here >= hop)
+            def _():
+                product(ints_ref, (a_ref, b_ref), rl, rh, here - hop, r_out, s_ref)
+
+            @pl.when(here + hop < dp)
+            def _():
+                product(ints_ref, (a_ref, b_ref), fl, fh, here + hop, f_out, s_ref)
+
+        return body
+
+    parts = []
+    first, shrunk = call(
+        own_product,
+        "own_columns",
+        (part_shape, s_shape),
+        (ints, tokens, other_tokens, own_l, own_h),
+    )
+    for hop in range(1, dp):
+        r_part, f_part, shrunk = call(
+            hop_product(hop),
+            "hop_columns",
+            (part_shape, part_shape, s_shape),
+            (ints, tokens, other_tokens, rise_l[hop], rise_h[hop], fall_l[hop], fall_h[hop], shrunk),
+        )
+        parts += [r_part, f_part]
+
+    both = groups * rows
+    s_rows = both * rank // LANES
+
+    def sort(ints_ref, *refs):
+        o_ref, *p_refs = refs[: 1 + len(parts)]
+        s_in = refs[1 + len(parts)]
+        keep, away = refs[2 + len(parts) :]
+        here, mine = ints_ref[1], ints_ref[2] % 2
+
+        def put(ref, holder):
+            at = pl.ds(pl.multiple_of((holder // 2) * both, both), both)
+
+            @pl.when(holder % 2 == mine)
+            def _():
+                keep[at, :] = ref[...]
+
+            @pl.when(holder % 2 != mine)
+            def _():
+                away[at, :] = ref[...].astype(BF16)
+
+        put(o_ref, here)
+        for hop in range(1, dp):
+            pl.when(here >= hop)(lambda hop=hop: put(p_refs[2 * hop - 2], here - hop))
+            pl.when(here + hop < dp)(lambda hop=hop: put(p_refs[2 * hop - 1], here + hop))
+        for g in range(groups):
+            s = jnp.concatenate(
+                [s_in[g * rows : g * rows + rows // 2, :], s_in[g * rows + rows // 2 : (g + 1) * rows, :]],
+                axis=1,
+            )
+            at = pairs * both + g * (rows // 2)
+            keep[at : at + rows // 2, :] = s
+            away[at : at + rows // 2, :] = s.astype(BF16)
+
+    total = pairs * both + s_rows
+    keep, away = call(
+        sort,
+        "sort",
+        (
+            jax.ShapeDtypeStruct((total, LANES), F32),
+            jax.ShapeDtypeStruct((total, LANES), BF16),
+        ),
+        (ints, first, *parts, shrunk),
+    )
+    came = send(away, lambda a, b, c: (a, b, c ^ 1))
+
+    msg_rows = rows + rows // 2
+
+    def add_cores(ints_ref, keep_ref, came_ref, own_out, x_out, y_out, d_out):
+        side = ints_ref[2] // 2
+
+        def tile(side_at, group_at):
+            at = pl.ds(pl.multiple_of(side_at * both + group_at * rows, rows), rows)
+            return keep_ref[at, :] + came_ref[at, :].astype(F32)
+
+        def low_rank(group_at):
+            at = pl.ds(pairs * both + group_at * (rows // 2), rows // 2)
+            return keep_ref[at, :] + came_ref[at, :].astype(F32)
+
+        own_out[0:rows, :] = tile(side, 0)
+        x_out[0:rows, :] = tile(1 - side, 0).astype(BF16)
+        y_out[0:rows, :] = tile(side, 1).astype(BF16)
+        d_out[0:rows, :] = tile(1 - side, 1).astype(BF16)
+        s_a, s_b = low_rank(0), low_rank(1)
+        own_out[rows:, :] = s_a
+        x_out[rows:, :] = s_a.astype(BF16)
+        y_out[rows:, :] = s_b.astype(BF16)
+        d_out[rows:, :] = s_b.astype(BF16)
+
+    msg = jax.ShapeDtypeStruct((msg_rows, LANES), BF16)
+    mine, to_x, to_y, to_d = call(
+        add_cores,
+        "add_cores",
+        (jax.ShapeDtypeStruct((msg_rows, LANES), F32), msg, msg, msg),
+        (ints, keep, came),
+    )
+    from_d = send(to_d, lambda a, b, c: (1 - a, b, c ^ 2))
+    from_x = send(to_x, lambda a, b, c: (a, b, c ^ 2))
+    from_y = send(to_y, lambda a, b, c: (1 - a, b, c))
+
+    def ups(ints_ref, o_ref, *refs):
+        p_refs, out = refs[:-1], refs[-1]
+        here = ints_ref[1]
+        at = half + low
+
+        def put(ref, holder):
+            out[holder] = ref[at : at + up_rows, :]
+
+        put(o_ref, here)
+        for hop in range(1, dp):
+            pl.when(here >= hop)(lambda hop=hop: put(p_refs[2 * hop - 2], here - hop))
+            pl.when(here + hop < dp)(lambda hop=hop: put(p_refs[2 * hop - 1], here + hop))
+
+    up_all = call(
+        ups,
+        "ups",
+        jax.ShapeDtypeStruct((dp, up_rows, LANES), BF16),
+        (ints, own_l, *[a[h] for h in range(1, dp) for a in (rise_l, fall_l)]),
+    )
+
+    def finish(ints_ref, live_ref, up_ref, mine_ref, x_ref, y_ref, d_ref, out_ref):
+        me = ints_ref[0]
+        here_half = mine_ref[0:rows, :] + x_ref[0:rows, :].astype(F32)
+        there_half = y_ref[0:rows, :].astype(F32) + d_ref[0:rows, :].astype(F32)
+        s = mine_ref[rows:, :]
+        for ref in (x_ref, y_ref, d_ref):
+            s = s + ref[rows:, :].astype(F32)
+        s = s.astype(BF16)
+        halves = (
+            jnp.where(me == 0, here_half, there_half),
+            jnp.where(me == 0, there_half, here_half),
+        )
+        for k in range(blocks):
+            slot = slot_of(ints_ref, 0, k)
+            holder, local_slot = slot // per_dev, slot % per_dev
+            per_lane = blocks // 2
+            piece = s[
+                (k % per_lane) * block_len : (k % per_lane + 1) * block_len,
+                (k // per_lane) * rank : (k // per_lane + 1) * rank,
+            ]
+            row = lax.broadcasted_iota(jnp.int32, (block_len, LANES), 0)
+            for v in range(out_cols // LANES):
+                at = pl.ds(
+                    pl.multiple_of((local_slot * (out_cols // LANES) + v) * rank, rank), rank
+                )
+                delta = jnp.dot(piece, up_ref[holder, at, :], preferred_element_type=F32)
+                base = halves[v][k * block_len : (k + 1) * block_len, :]
+                mixed = jnp.where(
+                    row < live_ref[k], base + delta.astype(BF16).astype(F32), 0.0
+                )
+                out_ref[
+                    k * block_len : (k + 1) * block_len, v * LANES : (v + 1) * LANES
+                ] = mixed.astype(BF16)
+
+    return pl.pallas_call(
+        finish,
+        name="finish",
+        out_shape=jax.ShapeDtypeStruct((rows, out_cols), BF16),
+        in_specs=[SMEM, SMEM] + [VMEM] * 5,
+        out_specs=VMEM,
+        compiler_params=pltpu.CompilerParams(vmem_limit_bytes=40 * 2**20),
+    )(ints, live_rows, up_all, mine, from_x, from_y, from_d)
 
 
 def local(
@@ -95,6 +401,11 @@
         P(("groups", "dp")),
         P(("groups", "dp")),
     )
+    sizes = tuple(mesh.shape[a] for a in AXES)
+    if sizes == (2, 4, 4):
+        body = lambda *args: local_line(sizes, *args)
+    else:
+        body = local
     return jax.shard_map(
-        local, mesh=mesh, in_specs=placed, out_specs=P(("groups", "dp"), "tensor"), check_vma=False
-    )
+        body, mesh=mesh, in_specs=placed, out_specs=P(("groups", "dp"), "tensor"), check_vma=False
+    )

time: 165 us -> 84.4 us (0.51)
  waiting for transfers between devices: 111 us -> 31.9 us
  starting transfers between devices: 13.6 us -> 28.8 us
  Pallas kernels: 0 us -> 14.4 us
  between operations: 13.5 us -> 0.26 us
  blocking collectives: 12.7 us -> 0 us
  matrix products: 6.94 us -> 0 us
  local copies, waits for them, and re-layouts: 4.95 us -> 8.3 us
  other arithmetic: 2.61 us -> 0.15 us
    all_to_all x3 -> x0, waiting for transfers between devices: 56.8 us -> none  [the longest x1 55.6 us: local(): lax.all_to_all(sent_x, 'dp', split_axis=0, concat_axis=0, tiled=True)]
    psum x1 -> x0, waiting for transfers between devices: 32.7 us -> none  [local(): lax.psum(partial_value.astype(jnp.bfloat16), 'tensor').astype(jnp.float32)]
    ppermute x0 -> x18, waiting for transfers between devices: none -> 31.9 us  [send(): return lax.ppermute(x, AXES, perm)]
    ppermute x0 -> x18, starting transfers between devices: none -> 28.8 us  [send(): return lax.ppermute(x, AXES, perm)]
    all_gather x1 -> x0, waiting for transfers between devices: 20.5 us -> none  [local(): lax.all_gather(value_weight, 'dp', axis=1, tiled=True)]
    pallas_call x0 -> x9, Pallas kernels: none -> 14.4 us  [the longest x8 13 us: call(): pl.pallas_call(body, name=name, out_shape=outs, in_specs=[SMEM] + [VMEM]...]
    all_to_all x3 -> x0, starting transfers between devices: 13.5 us -> none  [the longest x1 6.32 us: local(): lax.all_to_all(wanted_hot, 'dp', split_axis=0, concat_axis=0, tiled=True)]
    psum x1 -> x0, blocking collectives: 12.7 us -> none  [local(): reduced_input = lax.psum(picked.astype(jnp.bfloat16), 'tensor')]
  transfers between devices with their start and end apart: 5 -> 18, of which waited for: 4 -> 10; matrix products, arithmetic and copies ran while one was open for 8% -> 0% of each run, Pallas kernels for 0% -> 10%
where the time goes in v1:
time: 84.4 us; the launch traced here: 83.9 us
  waiting for transfers between devices  31.9 us (38%)
  starting transfers between devices  28.8 us (34%)
  Pallas kernels  14.4 us (17%)
  local copies, waits for them, and re-layouts  8.3 us (10%)
    ppermute x18, waiting for transfers between devices, send(): return lax.ppermute(x, AXES, perm)  31.9 us
    ppermute x18, starting transfers between devices, send(): return lax.ppermute(x, AXES, perm)  28.8 us
    pallas_call x8, Pallas kernels, call(): pl.pallas_call(body, name=name, out_shape=outs, in_specs=[SMEM] + [VMEM]...  13 us
    unnamed x32, local copies, waits for them, and re-layouts  8.22 us
  transfers between devices with their start and end apart: 18, of which 10 were waited for; matrix products, arithmetic and copies ran while one was open for 0% of the time, Pallas kernels for 10%

profile of v1, /device:TPU:0, one launch (start us, length us, event | category | flops | bytes accessed | tf_op | source)
XLA Modules:
  0.0 83.9 jit_solution(1280514621823233475)
XLA Ops:
  0.1 1.3 %copy-done.4 = bf16[2048,256]{1,0:T(8,128)(2,1)S(1)} copy-done((bf16[2048,256]{1,0:T(8,128)(2,1)S(1)}, bf16[2048,256]{1,0:T(8,128)(2,1)}, u32[]{:S(2)}) %copy-start.4) | copy-done | bytes 1048600
  1.4 1.0 %copy-done.5 = bf16[2,2048,64]{1,2,0:T(8,128)(2,1)S(1)} copy-done((bf16[2,2048,64]{1,2,0:T(8,128)(2,1)S(1)}, bf16[2,2048,64]{1,2,0:T(8,128)(2,1)}, u32[]{:S(2)}) %copy-start.5) | copy-done | bytes 524312
  4.0 5.0 %collective-permute-start.1 = (bf16[1792,128]{1,0:T(8,128)(2,1)S(1)}, bf16[1792,128]{1,0:T(8,128)(2,1)S(1)}, u32[]{:S(2)}, u32[]{:S(2)}) collective-permute-start(bf16[1792,128]{1,0:T(8,128)(2,1)S(1)} %get-tuple-element.24.o_ref.l_ref), channel_id=1, source_target_pairs={{0,4},{1,5},{2,6},{3,7},{4,8},{5,9},{6,10},{7,11},{8,12},{9,13},{1... | collective-permute-start | bytes 1376264 | tf_op jit(solution)/shard_map/ppermute | solution.py:52
  8.9 1.3 %collective-permute-start.2 = (bf16[1792,128]{1,0:T(8,128)(2,1)S(1)}, bf16[1792,128]{1,0:T(8,128)(2,1)S(1)}, u32[]{:S(2)}, u32[]{:S(2)}) collective-permute-start(bf16[1792,128]{1,0:T(8,128)(2,1)S(1)} %get-tuple-element.24.o_ref.l_ref), channel_id=1, source_target_pairs={{4,0},{5,1},{6,2},{7,3},{8,4},{9,5},{10,6},{11,7},{12,8},{13,9},{1... | collective-permute-start | bytes 1376264 | tf_op jit(solution)/shard_map/ppermute | solution.py:52
  11.0 4.6 %collective-permute-start.8 = (bf16[1536,128]{1,0:T(8,128)(2,1)S(1)}, bf16[1536,128]{1,0:T(8,128)(2,1)S(1)}, u32[]{:S(2)}, u32[]{:S(2)}) collective-permute-start(bf16[1536,128]{1,0:T(8,128)(2,1)S(1)} %get-tuple-element.25.h_ref), channel_id=1, source_target_pairs={{0,4},{1,5},{2,6},{3,7},{4,8},{5,9},{6,10},{7,11},{8,12},{9,13},{1... | collective-permute-start | bytes 1179656 | tf_op jit(solution)/shard_map/ppermute | solution.py:52
  15.6 1.3 %collective-permute-start.9 = (bf16[1536,128]{1,0:T(8,128)(2,1)S(1)}, bf16[1536,128]{1,0:T(8,128)(2,1)S(1)}, u32[]{:S(2)}, u32[]{:S(2)}) collective-permute-start(bf16[1536,128]{1,0:T(8,128)(2,1)S(1)} %get-tuple-element.25.h_ref), channel_id=1, source_target_pairs={{4,0},{5,1},{6,2},{7,3},{8,4},{9,5},{10,6},{11,7},{12,8},{13,9},{1... | collective-permute-start | bytes 1179656 | tf_op jit(solution)/shard_map/ppermute | solution.py:52
  17.7 1.5 %collective-permute-start = (s32[12]{0:T(128)S(1)}, s32[12]{0:T(128)S(1)}, u32[]{:S(2)}, u32[]{:S(2)}) collective-permute-start(s32[12]{0:T(128)S(1)} %pad_add_fusion), channel_id=1, source_target_pairs={{0,16},{1,17},{2,18},{3,19},{4,20},{5,21},{6,22},{7,23},{8,24},{9,... | collective-permute-start | bytes 152 | tf_op jit(solution)/shard_map/ppermute | solution.py:52
  19.2 2.0 %collective-permute-done = s32[12]{0:T(128)S(1)} collective-permute-done((s32[12]{0:T(128)S(1)}, s32[12]{0:T(128)S(1)}, u32[]{:S(2)}, u32[]{:S(2)}) %collective-permute-start) | collective-permute-done | bytes 80 | tf_op jit(solution)/shard_map/ppermute | solution.py:52
  21.3 1.5 %collective-permute-start.7 = (bf16[256,2048]{1,0:T(8,128)(2,1)S(1)}, bf16[256,2048]{1,0:T(8,128)(2,1)S(1)}, u32[]{:S(2)}, u32[]{:S(2)}) collective-permute-start(bf16[256,2048]{1,0:T(8,128)(2,1)S(1)} %copy-done), channel_id=1, source_target_pairs={{0,16},{1,17},{2,18},{3,19},{4,20},{5,21},{6,22},{7,23},{8,24},{9,... | collective-permute-start | bytes 3145736 | tf_op jit(solution)/shard_map/ppermute | solution.py:52
  24.3 1.3 %collective-permute-start.4 = (bf16[1792,128]{1,0:T(8,128)(2,1)S(1)}, bf16[1792,128]{1,0:T(8,128)(2,1)}, u32[]{:S(2)}, u32[]{:S(2)}) collective-permute-start(bf16[1792,128]{1,0:T(8,128)(2,1)S(1)} %collective-permute-done.2.refs_1_.fl), channel_id=1, source_target_pairs={{4,0},{5,1},{6,2},{7,3},{8,4},{9,5},{10,6},{11,7},{20,16},{21,17},... | collective-permute-start | bytes 1376264 | tf_op jit(solution)/shard_map/ppermute | solution.py:52
  25.6 1.5 %collective-permute-done.8.rh = bf16[1536,128]{1,0:T(8,128)(2,1)S(1)} collective-permute-done((bf16[1536,128]{1,0:T(8,128)(2,1)S(1)}, bf16[1536,128]{1,0:T(8,128)(2,1)S(1)}, u32[]{:S(2)}, u32[]{:S(2)}) %collective-permute-start.8) | collective-permute-done | bytes 393248 | tf_op jit(solution)/shard_map/ppermute | solution.py:52
  27.1 1.4 %collective-permute-start.10 = (bf16[1536,128]{1,0:T(8,128)(2,1)S(1)}, bf16[1536,128]{1,0:T(8,128)(2,1)}, u32[]{:S(2)}, u32[]{:S(2)}) collective-permute-start(bf16[1536,128]{1,0:T(8,128)(2,1)S(1)} %collective-permute-done.8.rh), channel_id=1, source_target_pairs={{4,8},{5,9},{6,10},{7,11},{8,12},{9,13},{10,14},{11,15},{20,24},{2... | collective-permute-start | bytes 1179656 | tf_op jit(solution)/shard_map/ppermute | solution.py:52
  29.3 3.5 %collective-permute-done.9.fh = bf16[1536,128]{1,0:T(8,128)(2,1)S(1)} collective-permute-done((bf16[1536,128]{1,0:T(8,128)(2,1)S(1)}, bf16[1536,128]{1,0:T(8,128)(2,1)S(1)}, u32[]{:S(2)}, u32[]{:S(2)}) %collective-permute-start.9) | collective-permute-done | bytes 393248 | tf_op jit(solution)/shard_map/ppermute | solution.py:52
  32.7 1.3 %collective-permute-start.11 = (bf16[1536,128]{1,0:T(8,128)(2,1)S(1)}, bf16[1536,128]{1,0:T(8,128)(2,1)}, u32[]{:S(2)}, u32[]{:S(2)}) collective-permute-start(bf16[1536,128]{1,0:T(8,128)(2,1)S(1)} %collective-permute-done.9.fh), channel_id=1, source_target_pairs={{4,0},{5,1},{6,2},{7,3},{8,4},{9,5},{10,6},{11,7},{20,16},{21,17},... | collective-permute-start | bytes 1179656 | tf_op jit(solution)/shard_map/ppermute | solution.py:52
  34.7 1.4 %collective-permute-start.5 = (bf16[1792,128]{1,0:T(8,128)(2,1)S(1)}, bf16[1792,128]{1,0:T(8,128)(2,1)}, u32[]{:S(2)}, u32[]{:S(2)}) collective-permute-start(bf16[1792,128]{1,0:T(8,128)(2,1)S(1)} %collective-permute-done.3.refs_2_.rl), channel_id=1, source_target_pairs={{8,12},{9,13},{10,14},{11,15},{24,28},{25,29},{26,30},{27,31}} | collective-permute-start | bytes 1376264 | tf_op jit(solution)/shard_map/ppermute | solution.py:52
  36.2 6.5 %collective-permute-done.4.refs_3_.fl = bf16[1792,128]{1,0:T(8,128)(2,1)} collective-permute-done((bf16[1792,128]{1,0:T(8,128)(2,1)S(1)}, bf16[1792,128]{1,0:T(8,128)(2,1)}, u32[]{:S(2)}, u32[]{:S(2)}) %collective-permute-start.4) | collective-permute-done | bytes 458784 | tf_op jit(solution)/shard_map/ppermute | solution.py:52
  42.6 1.3 %collective-permute-start.6 = (bf16[1792,128]{1,0:T(8,128)(2,1)}, bf16[1792,128]{1,0:T(8,128)(2,1)}, u32[]{:S(2)}, u32[]{:S(2)}) collective-permute-start(bf16[1792,128]{1,0:T(8,128)(2,1)} %collective-permute-done.4.refs_3_.fl), channel_id=1, source_target_pairs={{4,0},{5,1},{6,2},{7,3},{20,16},{21,17},{22,18},{23,19}} | collective-permute-start | bytes 1376264 | tf_op jit(solution)/shard_map/ppermute | solution.py:52
  43.9 1.4 %collective-permute-start.12 = (bf16[1536,128]{1,0:T(8,128)(2,1)}, bf16[1536,128]{1,0:T(8,128)(2,1)}, u32[]{:S(2)}, u32[]{:S(2)}) collective-permute-start(bf16[1536,128]{1,0:T(8,128)(2,1)} %collective-permute-done.10.rh), channel_id=1, source_target_pairs={{8,12},{9,13},{10,14},{11,15},{24,28},{25,29},{26,30},{27,31}} | collective-permute-start | bytes 1179656 | tf_op jit(solution)/shard_map/ppermute | solution.py:52
  45.4 5.7 %collective-permute-done.11.fh = bf16[1536,128]{1,0:T(8,128)(2,1)} collective-permute-done((bf16[1536,128]{1,0:T(8,128)(2,1)S(1)}, bf16[1536,128]{1,0:T(8,128)(2,1)}, u32[]{:S(2)}, u32[]{:S(2)}) %collective-permute-start.11) | collective-permute-done | bytes 393248 | tf_op jit(solution)/shard_map/ppermute | solution.py:52
  51.1 1.3 %collective-permute-start.13 = (bf16[1536,128]{1,0:T(8,128)(2,1)}, bf16[1536,128]{1,0:T(8,128)(2,1)}, u32[]{:S(2)}, u32[]{:S(2)}) collective-permute-start(bf16[1536,128]{1,0:T(8,128)(2,1)} %collective-permute-done.11.fh), channel_id=1, source_target_pairs={{4,0},{5,1},{6,2},{7,3},{20,16},{21,17},{22,18},{23,19}} | collective-permute-start | bytes 1179656 | tf_op jit(solution)/shard_map/ppermute | solution.py:52
  54.5 2.0 %own_columns.1 = (f32[512,128]{1,0:T(8,128)S(1)}, f32[512,64]{1,0:T(8,128)S(1)}) custom-call(s32[27]{0:T(128)S(1)} %concatenate.8.ints_ref, bf16[256,2048]{1,0:T(8,128)(2,1)S(1)} %copy-done, bf16[256,2048]{1,0:T(8,128)(2,1)S(1)} %collective-permute-done.7.b_ref, bf16[1792,128]{1,0:T(8,128)(2,1)S(1)} %copy-done.2, bf16[1536,128]{1,0:T(8,128)(2,1)S(1)} %copy-done.7), custom_call_target="tpu_custom_call" | custom-call | tf_op jit(solution)/shard_map/own_columns/pallas_call | solution.py:17
  56.5 2.0 %hop_columns.3 = (f32[512,128]{1,0:T(8,128)S(1)}, f32[512,128]{1,0:T(8,128)S(1)}, f32[512,64]{1,0:T(8,128)S(1)}) custom-call(s32[27]{0:T(128)S(1)} %concatenate.8.ints_ref, bf16[256,2048]{1,0:T(8,128)(2,1)S(1)} %copy-done, bf16[256,2048]{1,0:T(8,128)(2,1)S(1)} %collective-permute-done.7.b_ref, bf16[1792,128]{1,0:T(8,128)(2,1)S(1)} %collective-permute-done.1.refs_0_.rl, ...), custom_call_target="tpu_custom_call" | custom-call | tf_op jit(solution)/shard_map/hop_columns/pallas_call | solution.py:17
  58.5 2.7 %hop_columns.4 = (f32[512,128]{1,0:T(8,128)S(1)}, f32[512,128]{1,0:T(8,128)S(1)}, f32[512,64]{1,0:T(8,128)S(1)}) custom-call(s32[27]{0:T(128)S(1)} %concatenate.8.ints_ref, bf16[256,2048]{1,0:T(8,128)(2,1)S(1)} %copy-done, bf16[256,2048]{1,0:T(8,128)(2,1)S(1)} %collective-permute-done.7.b_ref, bf16[1792,128]{1,0:T(8,128)(2,1)S(1)} %collective-permute-done.3.refs_2_.rl, ...), custom_call_target="tpu_custom_call" | custom-call | tf_op jit(solution)/shard_map/hop_columns/pallas_call | solution.py:17
  61.3 6.6 %collective-permute-done.13.fh = bf16[1536,128]{1,0:T(8,128)(2,1)} collective-permute-done((bf16[1536,128]{1,0:T(8,128)(2,1)}, bf16[1536,128]{1,0:T(8,128)(2,1)}, u32[]{:S(2)}, u32[]{:S(2)}) %collective-permute-start.13) | collective-permute-done | bytes 393248 | tf_op jit(solution)/shard_map/ppermute | solution.py:52
  67.9 2.9 %hop_columns.5 = (f32[512,128]{1,0:T(8,128)S(1)}, f32[512,128]{1,0:T(8,128)S(1)}, f32[512,64]{1,0:T(8,128)S(1)}) custom-call(s32[27]{0:T(128)S(1)} %concatenate.8.ints_ref, bf16[256,2048]{1,0:T(8,128)(2,1)S(1)} %copy-done, bf16[256,2048]{1,0:T(8,128)(2,1)S(1)} %collective-permute-done.7.b_ref, bf16[1792,128]{1,0:T(8,128)(2,1)} %collective-permute-done.5.refs_4_.rl, ...), custom_call_target="tpu_custom_call" | custom-call | tf_op jit(solution)/shard_map/hop_columns/pallas_call | solution.py:17
  71.6 1.6 %collective-permute-done.14.came_ref = bf16[1280,128]{1,0:T(8,128)(2,1)S(1)} collective-permute-done((bf16[1280,128]{1,0:T(8,128)(2,1)S(1)}, bf16[1280,128]{1,0:T(8,128)(2,1)S(1)}, u32[]{:S(2)}, u32[]{:S(2)}) %collective-permute-start.14) | collective-permute-done | bytes 327712 | tf_op jit(solution)/shard_map/ppermute | solution.py:52
  73.8 1.6 %collective-permute-start.15 = (bf16[384,128]{1,0:T(8,128)(2,1)S(1)}, bf16[384,128]{1,0:T(8,128)(2,1)S(1)}, u32[]{:S(2)}, u32[]{:S(2)}) collective-permute-start(bf16[384,128]{1,0:T(8,128)(2,1)S(1)} %get-tuple-element.40), channel_id=1, source_target_pairs={{0,2},{1,3},{2,0},{3,1},{4,6},{5,7},{6,4},{7,5},{8,10},{9,11},{10,... | collective-permute-start | bytes 294920 | tf_op jit(solution)/shard_map/ppermute | solution.py:52
  75.4 1.5 %collective-permute-start.16 = (bf16[384,128]{1,0:T(8,128)(2,1)S(1)}, bf16[384,128]{1,0:T(8,128)(2,1)S(1)}, u32[]{:S(2)}, u32[]{:S(2)}) collective-permute-start(bf16[384,128]{1,0:T(8,128)(2,1)S(1)} %get-tuple-element.41), channel_id=1, source_target_pairs={{0,16},{1,17},{2,18},{3,19},{4,20},{5,21},{6,22},{7,23},{8,24},{9,... | collective-permute-start | bytes 294920 | tf_op jit(solution)/shard_map/ppermute | solution.py:52
  77.4 1.3 %ups.1.up_ref = bf16[4,256,128]{2,1,0:T(8,128)(2,1)S(1)} custom-call(s32[27]{0:T(128)S(1)} %concatenate.8.ints_ref, bf16[1792,128]{1,0:T(8,128)(2,1)S(1)} %copy-done.3, bf16[1792,128]{1,0:T(8,128)(2,1)S(1)} %collective-permute-done.1.refs_0_.rl, bf16[1792,128]{1,0:T(8,128)(2,1)S(1)} %collective-permute-done.2.refs_1_.fl, ...), custom_call_target="tpu_custom_call" | custom-call | tf_op jit(solution)/shard_map/ups/pallas_call | solution.py:17
  78.8 2.4 %collective-permute-done.16.y_ref = bf16[384,128]{1,0:T(8,128)(2,1)S(1)} collective-permute-done((bf16[384,128]{1,0:T(8,128)(2,1)S(1)}, bf16[384,128]{1,0:T(8,128)(2,1)S(1)}, u32[]{:S(2)}, u32[]{:S(2)}) %collective-permute-start.16) | collective-permute-done | bytes 98336 | tf_op jit(solution)/shard_map/ppermute | solution.py:52
  81.2 1.3 %collective-permute-done.17.d_ref = bf16[384,128]{1,0:T(8,128)(2,1)S(1)} collective-permute-done((bf16[384,128]{1,0:T(8,128)(2,1)S(1)}, bf16[384,128]{1,0:T(8,128)(2,1)S(1)}, u32[]{:S(2)}, u32[]{:S(2)}) %collective-permute-start.17) | collective-permute-done | bytes 98336 | tf_op jit(solution)/shard_map/ppermute | solution.py:52
  82.4 1.4 %finish.1 = bf16[256,256]{1,0:T(8,128)(2,1)} custom-call(s32[27]{0:T(128)S(1)} %concatenate.8.ints_ref, s32[4]{0:T(128)S(1)} %copy-done.13, bf16[4,256,128]{2,1,0:T(8,128)(2,1)S(1)} %ups.1.up_ref, f32[384,128]{1,0:T(8,128)S(1)} %get-tuple-element.39.mine_ref, bf16[384,128]{1,0:T(8,128)(2,1)S(1)} %collective-permute-done.15.x_ref, ...), custom_call_target="tpu_custom_call" | custom-call | tf_op jit(solution)/shard_map/finish/pallas_call | solution.py:303
  (48 shorter events, 10.2 us)
Async XLA Ops:
  0.0 21.3 %copy-start = (bf16[256,2048]{1,0:T(8,128)(2,1)S(1)}, bf16[256,2048]{1,0:T(8,128)(2,1)}, u32[]{:S(2)}) copy-start(bf16[256,2048]{1,0:T(8,128)(2,1)} %a_ref.7) | copy-start | bytes 3145732
  0.1 1.3 %copy-start.4 = (bf16[2048,256]{1,0:T(8,128)(2,1)S(1)}, bf16[2048,256]{1,0:T(8,128)(2,1)}, u32[]{:S(2)}) copy-start(bf16[2048,256]{1,0:T(8,128)(2,1)} %w_ref.1) | copy-start | bytes 3145732
  1.4 1.0 %copy-start.5 = (bf16[2,2048,64]{1,2,0:T(8,128)(2,1)S(1)}, bf16[2,2048,64]{1,2,0:T(8,128)(2,1)}, u32[]{:S(2)}) copy-start(bf16[2,2048,64]{1,2,0:T(8,128)(2,1)} %param.9) | copy-start | bytes 1572868
  2.4 0.8 %copy-start.12 = (bf16[2,64,256]{2,1,0:T(8,128)(2,1)S(1)}, bf16[2,64,256]{2,1,0:T(8,128)(2,1)}, u32[]{:S(2)}) copy-start(bf16[2,64,256]{2,1,0:T(8,128)(2,1)} %u_ref.1) | copy-start | bytes 196612
  4.0 13.7 %copy-start.14 = (s32[4]{0:T(128)S(1)}, s32[4]{0:T(128)}, u32[]{:S(2)}) copy-start(s32[4]{0:T(128)} %param.12) | copy-start | bytes 52
  4.0 13.7 %copy-start.15 = (s32[8]{0:T(128)S(1)}, s32[8]{0:T(128)}, u32[]{:S(2)}) copy-start(s32[8]{0:T(128)} %param.11) | copy-start | bytes 100
  4.0 18.8 %collective-permute-start.1 = (bf16[1792,128]{1,0:T(8,128)(2,1)S(1)}, bf16[1792,128]{1,0:T(8,128)(2,1)S(1)}, u32[]{:S(2)}, u32[]{:S(2)}) collective-permute-start(bf16[1792,128]{1,0:T(8,128)(2,1)S(1)} %get-tuple-element.24.o_ref.l_ref), channel_id=1, source_target_pairs={{0,4},{1,5},{2,6},{3,7},{4,8},{5,9},{6,10},{7,11},{8,12},{9,13},{1... | collective-permute-start | bytes 1376264 | tf_op jit(solution)/shard_map/ppermute | solution.py:52
  8.9 15.3 %collective-permute-start.2 = (bf16[1792,128]{1,0:T(8,128)(2,1)S(1)}, bf16[1792,128]{1,0:T(8,128)(2,1)S(1)}, u32[]{:S(2)}, u32[]{:S(2)}) collective-permute-start(bf16[1792,128]{1,0:T(8,128)(2,1)S(1)} %get-tuple-element.24.o_ref.l_ref), channel_id=1, source_target_pairs={{4,0},{5,1},{6,2},{7,3},{8,4},{9,5},{10,6},{11,7},{12,8},{13,9},{1... | collective-permute-start | bytes 1376264 | tf_op jit(solution)/shard_map/ppermute | solution.py:52
  10.2 0.8 copy-start.1
  11.0 16.1 %collective-permute-start.8 = (bf16[1536,128]{1,0:T(8,128)(2,1)S(1)}, bf16[1536,128]{1,0:T(8,128)(2,1)S(1)}, u32[]{:S(2)}, u32[]{:S(2)}) collective-permute-start(bf16[1536,128]{1,0:T(8,128)(2,1)S(1)} %get-tuple-element.25.h_ref), channel_id=1, source_target_pairs={{0,4},{1,5},{2,6},{3,7},{4,8},{5,9},{6,10},{7,11},{8,12},{9,13},{1... | collective-permute-start | bytes 1179656 | tf_op jit(solution)/shard_map/ppermute | solution.py:52
  15.6 17.1 %collective-permute-start.9 = (bf16[1536,128]{1,0:T(8,128)(2,1)S(1)}, bf16[1536,128]{1,0:T(8,128)(2,1)S(1)}, u32[]{:S(2)}, u32[]{:S(2)}) collective-permute-start(bf16[1536,128]{1,0:T(8,128)(2,1)S(1)} %get-tuple-element.25.h_ref), channel_id=1, source_target_pairs={{4,0},{5,1},{6,2},{7,3},{8,4},{9,5},{10,6},{11,7},{12,8},{13,9},{1... | collective-permute-start | bytes 1179656 | tf_op jit(solution)/shard_map/ppermute | solution.py:52
  16.9 0.8 copy-start.6
  17.7 3.5 %collective-permute-start = (s32[12]{0:T(128)S(1)}, s32[12]{0:T(128)S(1)}, u32[]{:S(2)}, u32[]{:S(2)}) collective-permute-start(s32[12]{0:T(128)S(1)} %pad_add_fusion), channel_id=1, source_target_pairs={{0,16},{1,17},{2,18},{3,19},{4,20},{5,21},{6,22},{7,23},{8,24},{9,... | collective-permute-start | bytes 152 | tf_op jit(solution)/shard_map/ppermute | solution.py:52
  21.3 31.2 %collective-permute-start.7 = (bf16[256,2048]{1,0:T(8,128)(2,1)S(1)}, bf16[256,2048]{1,0:T(8,128)(2,1)S(1)}, u32[]{:S(2)}, u32[]{:S(2)}) collective-permute-start(bf16[256,2048]{1,0:T(8,128)(2,1)S(1)} %copy-done), channel_id=1, source_target_pairs={{0,16},{1,17},{2,18},{3,19},{4,20},{5,21},{6,22},{7,23},{8,24},{9,... | collective-permute-start | bytes 3145736 | tf_op jit(solution)/shard_map/ppermute | solution.py:52
  22.8 12.0 %collective-permute-start.3 = (bf16[1792,128]{1,0:T(8,128)(2,1)S(1)}, bf16[1792,128]{1,0:T(8,128)(2,1)S(1)}, u32[]{:S(2)}, u32[]{:S(2)}) collective-permute-start(bf16[1792,128]{1,0:T(8,128)(2,1)S(1)} %collective-permute-done.1.refs_0_.rl), channel_id=1, source_target_pairs={{4,8},{5,9},{6,10},{7,11},{8,12},{9,13},{10,14},{11,15},{20,24},{2... | collective-permute-start | bytes 1376264 | tf_op jit(solution)/shard_map/ppermute | solution.py:52
  24.3 18.4 %collective-permute-start.4 = (bf16[1792,128]{1,0:T(8,128)(2,1)S(1)}, bf16[1792,128]{1,0:T(8,128)(2,1)}, u32[]{:S(2)}, u32[]{:S(2)}) collective-permute-start(bf16[1792,128]{1,0:T(8,128)(2,1)S(1)} %collective-permute-done.2.refs_1_.fl), channel_id=1, source_target_pairs={{4,0},{5,1},{6,2},{7,3},{8,4},{9,5},{10,6},{11,7},{20,16},{21,17},... | collective-permute-start | bytes 1376264 | tf_op jit(solution)/shard_map/ppermute | solution.py:52
  27.1 16.8 %collective-permute-start.10 = (bf16[1536,128]{1,0:T(8,128)(2,1)S(1)}, bf16[1536,128]{1,0:T(8,128)(2,1)}, u32[]{:S(2)}, u32[]{:S(2)}) collective-permute-start(bf16[1536,128]{1,0:T(8,128)(2,1)S(1)} %collective-permute-done.8.rh), channel_id=1, source_target_pairs={{4,8},{5,9},{6,10},{7,11},{8,12},{9,13},{10,14},{11,15},{20,24},{2... | collective-permute-start | bytes 1179656 | tf_op jit(solution)/shard_map/ppermute | solution.py:52
  32.7 18.4 %collective-permute-start.11 = (bf16[1536,128]{1,0:T(8,128)(2,1)S(1)}, bf16[1536,128]{1,0:T(8,128)(2,1)}, u32[]{:S(2)}, u32[]{:S(2)}) collective-permute-start(bf16[1536,128]{1,0:T(8,128)(2,1)S(1)} %collective-permute-done.9.fh), channel_id=1, source_target_pairs={{4,0},{5,1},{6,2},{7,3},{8,4},{9,5},{10,6},{11,7},{20,16},{21,17},... | collective-permute-start | bytes 1179656 | tf_op jit(solution)/shard_map/ppermute | solution.py:52
  34.7 33.1 %collective-permute-start.5 = (bf16[1792,128]{1,0:T(8,128)(2,1)S(1)}, bf16[1792,128]{1,0:T(8,128)(2,1)}, u32[]{:S(2)}, u32[]{:S(2)}) collective-permute-start(bf16[1792,128]{1,0:T(8,128)(2,1)S(1)} %collective-permute-done.3.refs_2_.rl), channel_id=1, source_target_pairs={{8,12},{9,13},{10,14},{11,15},{24,28},{25,29},{26,30},{27,31}} | collective-permute-start | bytes 1376264 | tf_op jit(solution)/shard_map/ppermute | solution.py:52
  42.6 25.2 %collective-permute-start.6 = (bf16[1792,128]{1,0:T(8,128)(2,1)}, bf16[1792,128]{1,0:T(8,128)(2,1)}, u32[]{:S(2)}, u32[]{:S(2)}) collective-permute-start(bf16[1792,128]{1,0:T(8,128)(2,1)} %collective-permute-done.4.refs_3_.fl), channel_id=1, source_target_pairs={{4,0},{5,1},{6,2},{7,3},{20,16},{21,17},{22,18},{23,19}} | collective-permute-start | bytes 1376264 | tf_op jit(solution)/shard_map/ppermute | solution.py:52
  43.9 17.3 %collective-permute-start.12 = (bf16[1536,128]{1,0:T(8,128)(2,1)}, bf16[1536,128]{1,0:T(8,128)(2,1)}, u32[]{:S(2)}, u32[]{:S(2)}) collective-permute-start(bf16[1536,128]{1,0:T(8,128)(2,1)} %collective-permute-done.10.rh), channel_id=1, source_target_pairs={{8,12},{9,13},{10,14},{11,15},{24,28},{25,29},{26,30},{27,31}} | collective-permute-start | bytes 1179656 | tf_op jit(solution)/shard_map/ppermute | solution.py:52
  51.1 16.8 %collective-permute-start.13 = (bf16[1536,128]{1,0:T(8,128)(2,1)}, bf16[1536,128]{1,0:T(8,128)(2,1)}, u32[]{:S(2)}, u32[]{:S(2)}) collective-permute-start(bf16[1536,128]{1,0:T(8,128)(2,1)} %collective-permute-done.11.fh), channel_id=1, source_target_pairs={{4,0},{5,1},{6,2},{7,3},{20,16},{21,17},{22,18},{23,19}} | collective-permute-start | bytes 1179656 | tf_op jit(solution)/shard_map/ppermute | solution.py:52
  52.4 1.0 %copy-start.2 = (bf16[1792,128]{1,0:T(8,128)(2,1)S(1)}, bf16[1792,128]{1,0:T(8,128)(2,1)}, u32[]{:S(2)}) copy-start(bf16[1792,128]{1,0:T(8,128)(2,1)} %copy-done.1) | copy-start | bytes 1376260
  53.5 1.0 %copy-start.7 = (bf16[1536,128]{1,0:T(8,128)(2,1)S(1)}, bf16[1536,128]{1,0:T(8,128)(2,1)}, u32[]{:S(2)}) copy-start(bf16[1536,128]{1,0:T(8,128)(2,1)} %copy-done.6) | copy-start | bytes 1179652
  54.5 2.0 %copy-start.9 = (bf16[1536,128]{1,0:T(8,128)(2,1)S(1)}, bf16[1536,128]{1,0:T(8,128)(2,1)}, u32[]{:S(2)}) copy-start(bf16[1536,128]{1,0:T(8,128)(2,1)} %copy-done.8) | copy-start | bytes 1179652
  54.5 2.0 %copy-start.11 = (bf16[1536,128]{1,0:T(8,128)(2,1)S(1)}, bf16[1536,128]{1,0:T(8,128)(2,1)}, u32[]{:S(2)}) copy-start(bf16[1536,128]{1,0:T(8,128)(2,1)} %copy-done.10) | copy-start | bytes 1179652
  71.5 1.7 %collective-permute-start.14 = (bf16[1280,128]{1,0:T(8,128)(2,1)S(1)}, bf16[1280,128]{1,0:T(8,128)(2,1)S(1)}, u32[]{:S(2)}, u32[]{:S(2)}) collective-permute-start(bf16[1280,128]{1,0:T(8,128)(2,1)S(1)} %get-tuple-element.38), channel_id=1, source_target_pairs={{0,1},{1,0},{2,3},{3,2},{4,5},{5,4},{6,7},{7,6},{8,9},{9,8},{10,11... | collective-permute-start | bytes 983048 | tf_op jit(solution)/shard_map/ppermute | solution.py:52
  73.2 4.2 %copy-start.3 = (bf16[1792,128]{1,0:T(8,128)(2,1)S(1)}, bf16[1792,128]{1,0:T(8,128)(2,1)}, u32[]{:S(2)}) copy-start(bf16[1792,128]{1,0:T(8,128)(2,1)} %copy-done.1) | copy-start | bytes 1376260
  73.8 4.9 %collective-permute-start.15 = (bf16[384,128]{1,0:T(8,128)(2,1)S(1)}, bf16[384,128]{1,0:T(8,128)(2,1)S(1)}, u32[]{:S(2)}, u32[]{:S(2)}) collective-permute-start(bf16[384,128]{1,0:T(8,128)(2,1)S(1)} %get-tuple-element.40), channel_id=1, source_target_pairs={{0,2},{1,3},{2,0},{3,1},{4,6},{5,7},{6,4},{7,5},{8,10},{9,11},{10,... | collective-permute-start | bytes 294920 | tf_op jit(solution)/shard_map/ppermute | solution.py:52
  75.4 5.8 %collective-permute-start.16 = (bf16[384,128]{1,0:T(8,128)(2,1)S(1)}, bf16[384,128]{1,0:T(8,128)(2,1)S(1)}, u32[]{:S(2)}, u32[]{:S(2)}) collective-permute-start(bf16[384,128]{1,0:T(8,128)(2,1)S(1)} %get-tuple-element.41), channel_id=1, source_target_pairs={{0,16},{1,17},{2,18},{3,19},{4,20},{5,21},{6,22},{7,23},{8,24},{9,... | collective-permute-start | bytes 294920 | tf_op jit(solution)/shard_map/ppermute | solution.py:52
  76.9 5.5 %collective-permute-start.17 = (bf16[384,128]{1,0:T(8,128)(2,1)S(1)}, bf16[384,128]{1,0:T(8,128)(2,1)S(1)}, u32[]{:S(2)}, u32[]{:S(2)}) collective-permute-start(bf16[384,128]{1,0:T(8,128)(2,1)S(1)} %get-tuple-element.42), channel_id=1, source_target_pairs={{0,18},{1,19},{2,16},{3,17},{4,22},{5,23},{6,20},{7,21},{8,26},{9,... | collective-permute-start | bytes 294920 | tf_op jit(solution)/shard_map/ppermute | solution.py:52
  78.7 3.7 %copy-start.13 = (s32[4]{0:T(128)S(1)}, s32[4]{0:T(128)}, u32[]{:S(2)}) copy-start(s32[4]{0:T(128)} %live_ref.1) | copy-start | bytes 52
  (2 other events, 1.5 us)

commit v2 on v0

--- a/solution.py
+++ b/solution.py
@@ -1,7 +1,403 @@
 import jax
 import jax.numpy as jnp
 from jax import lax
+from jax.experimental import pallas as pl
+from jax.experimental.pallas import tpu as pltpu
 from jax.sharding import PartitionSpec as P
+
+AXES = ("groups", "dp", "tensor")
+LANES = 128
+CODE_ROWS = 16
+F32 = jnp.float32
+BF16 = jnp.bfloat16
+VMEM = pl.BlockSpec(memory_space=pltpu.VMEM)
+SMEM = pl.BlockSpec(memory_space=pltpu.SMEM)
+ANY = pl.BlockSpec(memory_space=pl.ANY)
+
+
+def call(body, name, outs, specs, ins, scratch=()):
+    return pl.pallas_call(
+        body,
+        name=name,
+        out_shape=outs,
+        in_specs=specs,
+        out_specs=jax.tree.map(lambda _: VMEM, outs),
+        scratch_shapes=scratch,
+        compiler_params=pltpu.CompilerParams(vmem_limit_bytes=16 * 2**20),
+    )(*ins)
+
+
+def like(rows, cols, dtype=BF16):
+    return jax.ShapeDtypeStruct((rows, cols), dtype)
+
+
+def local_line(sizes, tokens, value_weight, down, up, slot_table, per_block, live_rows):
+    groups, dp, tensor = sizes
+    y, z, t = (lax.axis_index(a) for a in AXES)
+    place = jnp.stack([y, z, t]).astype(jnp.int32)
+    rows, feats = tokens.shape
+    blocks = per_block.shape[0]
+    block_len = rows // blocks
+    per_dev, _, rank = down.shape
+    out_cols = up.shape[2]
+    half_cols = value_weight.shape[1] // groups
+    half = feats // 2
+    quarter = half // 2
+    up_at = half + quarter
+    up_rows = per_dev * rank * out_cols // LANES
+    col_tiles = out_cols // LANES
+    pairs = dp // 2
+    both = groups * rows
+    s_rows = both * rank // LANES
+    total = pairs * both + s_rows
+    msg_rows = rows + rows // 2
+
+    def device(a, b, c):
+        return (a * dp + b) * tensor + c
+
+    def send(x, where, planes=range(4)):
+        perm = []
+        for a in range(groups):
+            for b in planes:
+                for c in range(tensor):
+                    perm.append((device(a, b, c), device(*where(a, b, c))))
+        return lax.ppermute(x, AXES, perm)
+
+    outer, inner = (0, 3), (1, 2)
+
+    def inward(x):
+        return send(x, lambda a, b, c: (a, b ^ 1, c), outer)
+
+    def outward(x):
+        return send(x, lambda a, b, c: (a, b ^ 1, c), inner)
+
+    def middle(x):
+        return send(x, lambda a, b, c: (a, 3 - b, c), inner)
+
+    def swap(x, planes=range(4)):
+        return send(x, lambda a, b, c: (1 - a, b, c), planes)
+
+    def pack(ints_ref, w_ref, d_ref, u_ref, l_ref, h_ref, d_held, sems):
+        me = ints_ref[0]
+        cols = pl.ds(pl.multiple_of(me * half_cols, LANES), half_cols)
+        copies = [
+            pltpu.make_async_copy(d_ref.at[me], d_held, sems.at[0]),
+            pltpu.make_async_copy(w_ref.at[pl.ds(0, half), cols], l_ref.at[pl.ds(0, half)], sems.at[1]),
+            pltpu.make_async_copy(w_ref.at[pl.ds(half, half), cols], h_ref.at[pl.ds(0, half)], sems.at[2]),
+        ]
+        for s in range(per_dev):
+            for v in range(col_tiles):
+                n = s * col_tiles + v
+                copies.append(
+                    pltpu.make_async_copy(
+                        u_ref.at[s, :, pl.ds(v * LANES, LANES)],
+                        l_ref.at[pl.ds(up_at + n * rank, rank)],
+                        sems.at[3 + n],
+                    )
+                )
+        for c in copies:
+            c.start()
+        copies[0].wait()
+        for part, ref in ((0, l_ref), (1, h_ref)):
+            at = part * half
+            ref[half:up_at, :] = jnp.concatenate(
+                [d_held[:, at : at + quarter], d_held[:, at + quarter : at + half]], axis=0
+            ).T
+        for c in copies[1:]:
+            c.wait()
+
+    own_l, own_h = call(
+        pack,
+        "pack_weights",
+        (like(up_at + up_rows, LANES), like(up_at, LANES)),
+        [SMEM, ANY, ANY, ANY],
+        (place, value_weight, jnp.transpose(down, (0, 2, 1)), up),
+        [pltpu.VMEM((rank, feats), BF16), pltpu.SemaphoreType.DMA((3 + per_dev * col_tiles,))],
+    )
+
+    def pack_tokens(table_ref, block_ref, tok_ref, low_ref, high_ref, a_ref, b_ref, sems):
+        copies = [
+            pltpu.make_async_copy(tok_ref.at[:, pl.ds(0, half)], low_ref.at[pl.ds(0, rows)], sems.at[0]),
+            pltpu.make_async_copy(tok_ref.at[:, pl.ds(half, half)], high_ref, sems.at[1]),
+            pltpu.make_async_copy(tok_ref.at[:, pl.ds(half, quarter)], a_ref.at[pl.ds(0, rows)], sems.at[2]),
+            pltpu.make_async_copy(tok_ref.at[:, pl.ds(half + quarter, quarter)], b_ref, sems.at[3]),
+        ]
+        for c in copies:
+            c.start()
+        row = lax.broadcasted_iota(jnp.int32, (CODE_ROWS, half), 0)
+        code = jnp.zeros((CODE_ROWS, half), jnp.int32)
+        for k in range(blocks):
+            code = jnp.where(row == k, table_ref[block_ref[k]], code)
+        code = code.astype(F32).astype(BF16)
+        low_ref[rows:, :] = code
+        a_ref[rows:, :] = code[:, 0:quarter]
+        for c in copies:
+            c.wait()
+
+    tok_l, tok_h, tok_a, tok_b = call(
+        pack_tokens,
+        "pack_tokens",
+        (like(rows + CODE_ROWS, half), like(rows, half), like(rows + CODE_ROWS, quarter), like(rows, quarter)),
+        [SMEM, SMEM, ANY],
+        (slot_table, per_block, tokens),
+        [pltpu.SemaphoreType.DMA((4,))],
+    )
+
+    mid_l = middle(own_l)
+    in_l = inward(own_l)
+    out_l1 = outward(own_l)
+    other_l = swap(tok_l)
+    mid_h = middle(own_h)
+    in_a = inward(tok_a)
+    in_h = inward(own_h)
+    in_b = inward(tok_b)
+    other_h = swap(tok_h, inner)
+    out_l2 = outward(mid_l)
+    far_l = middle(in_l)
+    far_h = middle(in_h)
+    out_l3 = outward(far_l)
+    other_a = swap(in_a, inner)
+    other_b = swap(in_b, inner)
+
+    def product(tiles, w_ref):
+        base = s = None
+        for q, x in tiles:
+            rhs = jnp.concatenate(
+                [w_ref[q * quarter : (q + 1) * quarter, :], w_ref[half:up_at, :]], axis=1
+            )
+            got = jnp.dot(x, rhs, preferred_element_type=F32)
+            b = got[:, 0:LANES]
+            e = got[:, LANES + q * rank : LANES + (q + 1) * rank]
+            base, s = (b, e) if base is None else (base + b, s + e)
+        return base, s
+
+    def chosen(s, code_ref, mine):
+        codes = code_ref[rows : rows + CODE_ROWS, 0:LANES].astype(F32)
+        pieces = []
+        for k in range(blocks):
+            hit = codes[k : k + 1, 0:rank] == mine
+            pieces.append(jnp.where(hit, s[k * block_len : (k + 1) * block_len, :], 0.0))
+        return jnp.concatenate(pieces, axis=0)
+
+    def halves(ref):
+        return [(q, ref[0:rows, q * quarter : (q + 1) * quarter]) for q in (0, 1)]
+
+    def number(ints_ref, holder):
+        return (per_dev * holder + ints_ref[0]).astype(F32)
+
+    def where_from(here, slot):
+        near = here ^ 1
+        is_outer = (here == 0) | (here == 3)
+        if slot == 0:
+            return here
+        if slot == 1:
+            return near
+        if slot == 2:
+            return jnp.where(is_outer, 3 - near, 3 - here)
+        return jnp.where(is_outer, 3 - here, 3 - near)
+
+    def own_rows(ints_ref, toks, slot, l_ref, h_ref, out_ref, out_at, s_ref):
+        mine = number(ints_ref, where_from(ints_ref[1], slot))
+        for g, (low, high) in enumerate(toks):
+            base, s = product(halves(low), l_ref)
+            if h_ref is not None:
+                b, e = product(halves(high), h_ref)
+                base, s = base + b, s + e
+            at = pl.ds(out_at + g * rows, rows)
+            out_ref[at, :] = base
+            s_ref[pl.ds(g * rows, rows), :] += chosen(s, low, mine)
+
+    def early(ints_ref, low_a, high_a, low_b, high_b, own_l, own_h, in_l, in_h, mid_l, mid_h, out1, out2, part_ref, s_ref):
+        toks = ((low_a, high_a), (low_b, high_b))
+        here = ints_ref[1]
+        is_outer = (here == 0) | (here == 3)
+        s_ref[...] = jnp.zeros_like(s_ref)
+
+        @pl.when(is_outer)
+        def _():
+            for slot, ref in enumerate((own_l, out1, out2)):
+                own_rows(ints_ref, toks, slot, ref, None, part_ref, slot * both, s_ref)
+
+        @pl.when(jnp.logical_not(is_outer))
+        def _():
+            for slot, (l, h) in enumerate(((own_l, own_h), (in_l, in_h), (mid_l, mid_h))):
+                own_rows(ints_ref, toks, slot, l, h, part_ref, slot * both, s_ref)
+
+    part, shrunk = call(
+        early,
+        "early_columns",
+        (like(3 * both, LANES, F32), like(both, rank, F32)),
+        [SMEM] + [VMEM] * 12,
+        (place, tok_l, tok_h, other_l, other_h, own_l, own_h, in_l, in_h, mid_l, mid_h, out_l1, out_l2),
+    )
+
+    def late(
+        ints_ref, low_a, high_a, low_b, high_b, na, nb, oa, ob, own_h, in_h, mid_h, far_l, far_h, out3,
+        part_ref, s_in, keep, away, last_ref, s_ref, near_ref, near_s,
+    ):
+        toks = ((low_a, high_a), (low_b, high_b))
+        here, core = ints_ref[1], ints_ref[2] % 2
+        is_outer = (here == 0) | (here == 3)
+        s_ref[...] = s_in[...]
+
+        def put(ref, ref_at, holder, base):
+            at = pl.ds(pl.multiple_of(base + (holder // 2) * both, both // 2), both)
+
+            @pl.when(holder % 2 == core)
+            def _():
+                keep[at, :] = ref[ref_at : ref_at + both, :]
+
+            @pl.when(holder % 2 != core)
+            def _():
+                away[at, :] = ref[ref_at : ref_at + both, :].astype(BF16)
+
+        def put_shrunk(ref, base):
+            for g in range(groups):
+                s = jnp.concatenate(
+                    [
+                        ref[g * rows : g * rows + rows // 2, :],
+                        ref[g * rows + rows // 2 : (g + 1) * rows, :],
+                    ],
+                    axis=1,
+                )
+                at = base + pairs * both + g * (rows // 2)
+                keep[at : at + rows // 2, :] = s
+                away[at : at + rows // 2, :] = s.astype(BF16)
+
+        @pl.when(is_outer)
+        def _():
+            own_rows(ints_ref, toks, 3, out3, None, last_ref, 0, s_ref)
+
+        @pl.when(jnp.logical_not(is_outer))
+        def _():
+            own_rows(ints_ref, toks, 3, far_l, far_h, last_ref, 0, s_ref)
+            near_s[...] = jnp.zeros_like(near_s)
+            for slot, w_ref in enumerate((own_h, in_h, mid_h, far_h)):
+                mine = number(ints_ref, where_from(here, slot))
+                for g, (a, b) in enumerate(((na, nb), (oa, ob))):
+                    base, s = product([(0, a[0:rows, :]), (1, b[...])], w_ref)
+                    near_ref[g * rows : (g + 1) * rows, :] = base
+                    near_s[g * rows : (g + 1) * rows, :] += chosen(s, a, mine)
+                put(near_ref, 0, where_from(here, slot), total)
+            put_shrunk(near_s, total)
+
+        for slot in range(3):
+            put(part_ref, slot * both, where_from(here, slot), 0)
+        put(last_ref, 0, where_from(here, 3), 0)
+        put_shrunk(s_ref, 0)
+
+    keep, away = call(
+        late,
+        "late_columns",
+        (like(2 * total, LANES, F32), like(2 * total, LANES)),
+        [SMEM] + [VMEM] * 16,
+        (
+            place, tok_l, tok_h, other_l, other_h, in_a, in_b, other_a, other_b,
+            own_h, in_h, mid_h, far_l, far_h, out_l3, part, shrunk,
+        ),
+        [
+            pltpu.VMEM((both, LANES), F32),
+            pltpu.VMEM((both, rank), F32),
+            pltpu.VMEM((both, LANES), F32),
+            pltpu.VMEM((both, rank), F32),
+        ],
+    )
+    came = send(away, lambda a, b, c: (a, b, c ^ 1))
+
+    def add_cores(ints_ref, keep_ref, came_ref, own_out, *outs):
+        side = ints_ref[2] // 2
+
+        def fill(out, base, side_at, g):
+            at = pl.ds(pl.multiple_of(base + side_at * both + g * rows, rows), rows)
+            s_at = pl.ds(base + pairs * both + g * (rows // 2), rows // 2)
+            out[0:rows, :] = (keep_ref[at, :] + came_ref[at, :].astype(F32)).astype(out.dtype)
+            out[rows:, :] = (keep_ref[s_at, :] + came_ref[s_at, :].astype(F32)).astype(out.dtype)
+
+        fill(own_out, 0, side, 0)
+        for n, out in enumerate(outs[0:3]):
+            flip, g = ((0, 1), (1, 0), (1, 1))[n]
+            fill(out, 0, jnp.where(flip == 1, 1 - side, side), g)
+        for n, out in enumerate(outs[3:]):
+            flip, g = n // 2, n % 2
+            fill(out, total, jnp.where(flip == 1, 1 - side, side), g)
+
+    msg = like(msg_rows, LANES)
+    mine, *sent = call(
+        add_cores,
+        "add_cores",
+        (like(msg_rows, LANES, F32),) + (msg,) * 7,
+        [SMEM, VMEM, VMEM],
+        (place, keep, came),
+    )
+    came_msgs = []
+    for flip, g, x in ((0, 0, sent[3]), (0, 1, sent[4]), (1, 0, sent[5]), (1, 1, sent[6])):
+        came_msgs.append((g, send(x, lambda a, b, c: (a ^ g, b ^ 1, c ^ (2 * flip)), inner)))
+    for flip, g, x in ((1, 1, sent[2]), (1, 0, sent[1]), (0, 1, sent[0])):
+        came_msgs.append((g, send(x, lambda a, b, c: (a ^ g, b, c ^ (2 * flip)))))
+
+    def ups(ints_ref, own, in_l, mid_l, far_l, out1, out2, out3, out):
+        here = ints_ref[1]
+        is_outer = (here == 0) | (here == 3)
+
+        def put(ref, slot):
+            out[where_from(here, slot)] = ref[up_at : up_at + up_rows, :]
+
+        put(own, 0)
+
+        @pl.when(is_outer)
+        def _():
+            for slot, ref in ((1, out1), (2, out2), (3, out3)):
+                put(ref, slot)
+
+        @pl.when(jnp.logical_not(is_outer))
+        def _():
+            for slot, ref in ((1, in_l), (2, mid_l), (3, far_l)):
+                put(ref, slot)
+
+    up_all = call(
+        ups,
+        "ups",
+        jax.ShapeDtypeStruct((dp, up_rows, LANES), BF16),
+        [SMEM] + [VMEM] * 7,
+        (place, own_l, in_l, mid_l, far_l, out_l1, out_l2, out_l3),
+    )
+    groups_of = [g for g, _ in came_msgs]
+
+    def finish(ints_ref, table_ref, block_ref, live_ref, up_ref, mine_ref, *refs):
+        msgs, out_ref = refs[:-1], refs[-1]
+        me = ints_ref[0]
+        sums = [mine_ref[0:rows, :], jnp.zeros((rows, LANES), F32)]
+        s = mine_ref[rows:, :]
+        for g, ref in zip(groups_of, msgs):
+            sums[g] = sums[g] + ref[0:rows, :].astype(F32)
+            s = s + ref[rows:, :].astype(F32)
+        s = s.astype(BF16)
+        split = (jnp.where(me == 0, sums[0], sums[1]), jnp.where(me == 0, sums[1], sums[0]))
+        per_lane = blocks // 2
+        row = lax.broadcasted_iota(jnp.int32, (block_len, LANES), 0)
+        for k in range(blocks):
+            slot = table_ref[block_ref[k]]
+            holder, local_slot = slot // per_dev, slot % per_dev
+            piece = s[
+                (k % per_lane) * block_len : (k % per_lane + 1) * block_len,
+                (k // per_lane) * rank : (k // per_lane + 1) * rank,
+            ]
+            for v in range(col_tiles):
+                at = pl.ds(pl.multiple_of((local_slot * col_tiles + v) * rank, rank), rank)
+                delta = jnp.dot(piece, up_ref[holder, at, :], preferred_element_type=F32)
+                base = split[v][k * block_len : (k + 1) * block_len, :]
+                mixed = jnp.where(row < live_ref[k], base + delta.astype(BF16).astype(F32), 0.0)
+                out_ref[
+                    k * block_len : (k + 1) * block_len, v * LANES : (v + 1) * LANES
+                ] = mixed.astype(BF16)
+
+    return call(
+        finish,
+        "finish",
+        like(rows, out_cols),
+        [SMEM] * 4 + [VMEM] * 9,
+        (place, slot_table, per_block, live_rows, up_all, mine, *[m for _, m in came_msgs]),
+    )
 
 
 def local(
@@ -95,6 +491,11 @@
         P(("groups", "dp")),
         P(("groups", "dp")),
     )
+    sizes = tuple(mesh.shape[a] for a in AXES)
+    if sizes == (2, 4, 4):
+        body = lambda *args: local_line(sizes, *args)
+    else:
+        body = local
     return jax.shard_map(
-        local, mesh=mesh, in_specs=placed, out_specs=P(("groups", "dp"), "tensor"), check_vma=False
-    )
+        body, mesh=mesh, in_specs=placed, out_specs=P(("groups", "dp"), "tensor"), check_vma=False
+    )

time: 165 us -> 103 us (0.62)
  waiting for transfers between devices: 111 us -> 59.7 us
  starting transfers between devices: 13.6 us -> 31.8 us
  between operations: 13.5 us -> 0.31 us
  blocking collectives: 12.7 us -> 0 us
  Pallas kernels: 0 us -> 7.13 us
  matrix products: 6.94 us -> 0 us
  other arithmetic: 2.61 us -> 0.08 us
  local copies, waits for them, and re-layouts: 4.95 us -> 3.12 us
    ppermute x0 -> x23, waiting for transfers between devices: none -> 59.7 us  [send(): return lax.ppermute(x, AXES, perm)]
    all_to_all x3 -> x0, waiting for transfers between devices: 56.8 us -> none  [the longest x1 55.6 us: local(): lax.all_to_all(sent_x, 'dp', split_axis=0, concat_axis=0, tiled=True)]
    psum x1 -> x0, waiting for transfers between devices: 32.7 us -> none  [local(): lax.psum(partial_value.astype(jnp.bfloat16), 'tensor').astype(jnp.float32)]
    ppermute x0 -> x23, starting transfers between devices: none -> 31.8 us  [send(): return lax.ppermute(x, AXES, perm)]
    all_gather x1 -> x0, waiting for transfers between devices: 20.5 us -> none  [local(): lax.all_gather(value_weight, 'dp', axis=1, tiled=True)]
    all_to_all x3 -> x0, starting transfers between devices: 13.5 us -> none  [the longest x1 6.32 us: local(): lax.all_to_all(wanted_hot, 'dp', split_axis=0, concat_axis=0, tiled=True)]
    psum x1 -> x0, blocking collectives: 12.7 us -> none  [local(): reduced_input = lax.psum(picked.astype(jnp.bfloat16), 'tensor')]
    pallas_call x0 -> x7, Pallas kernels: none -> 7.13 us  [call(): pl.pallas_call(body, name=name, out_shape=outs, in_specs=specs, out_specs...]
  transfers between devices with their start and end apart: 5 -> 23, of which waited for: 4 -> 12; matrix products, arithmetic and copies ran while one was open for 8% -> 0% of each run, Pallas kernels for 0% -> 3%
where the time goes in v2:
time: 103 us; the launch traced here: 102 us
  waiting for transfers between devices  59.7 us (58%)
  starting transfers between devices  31.8 us (31%)
  Pallas kernels  7.13 us (7%)
  local copies, waits for them, and re-layouts  3.12 us (3%)
    ppermute x23, waiting for transfers between devices, send(): return lax.ppermute(x, AXES, perm)  59.7 us
    ppermute x23, starting transfers between devices, send(): return lax.ppermute(x, AXES, perm)  31.8 us
    pallas_call x7, Pallas kernels, call(): pl.pallas_call(body, name=name, out_shape=outs, in_specs=specs, out_specs...  7.13 us
    unnamed x14, local copies, waits for them, and re-layouts  3.12 us
  transfers between devices with their start and end apart: 23, of which 12 were waited for; matrix products, arithmetic and copies ran while one was open for 0% of the time, Pallas kernels for 3%

profile of v2, /device:TPU:0, one launch (start us, length us, event | category | flops | bytes accessed | tf_op | source)
XLA Modules:
  0.0 102.1 jit_solution(111696599038896712)
XLA Ops:
  0.1 1.2 %copy-done = bf16[2048,256]{1,0:T(8,128)(2,1)S(1)} copy-done((bf16[2048,256]{1,0:T(8,128)(2,1)S(1)}, bf16[2048,256]{1,0:T(8,128)(2,1)}, u32[]{:S(2)}) %copy-start) | copy-done | bytes 1048600
  1.3 1.0 %copy-done.2 = bf16[2,2048,64]{1,2,0:T(8,128)(2,1)S(1)} copy-done((bf16[2,2048,64]{1,2,0:T(8,128)(2,1)S(1)}, bf16[2,2048,64]{1,2,0:T(8,128)(2,1)}, u32[]{:S(2)}) %copy-start.2) | copy-done | bytes 524312
  2.4 0.8 copy-done.3
  3.2 0.9 pack_weights.1
  4.1 5.0 %collective-permute-start = (bf16[1792,128]{1,0:T(8,128)(2,1)S(1)}, bf16[1792,128]{1,0:T(8,128)(2,1)S(1)}, u32[]{:S(2)}, u32[]{:S(2)}) collective-permute-start(bf16[1792,128]{1,0:T(8,128)(2,1)S(1)} %get-tuple-element.23.own.own_l), channel_id=1, source_target_pairs={{0,4},{1,5},{2,6},{3,7},{12,8},{13,9},{14,10},{15,11},{16,20},{17,... | collective-permute-start | bytes 1376264 | tf_op jit(solution)/shard_map/ppermute | solution.py:64
  9.7 4.1 %collective-permute-start.12 = (bf16[1536,128]{1,0:T(8,128)(2,1)S(1)}, bf16[1536,128]{1,0:T(8,128)(2,1)S(1)}, u32[]{:S(2)}, u32[]{:S(2)}) collective-permute-start(bf16[1536,128]{1,0:T(8,128)(2,1)S(1)} %get-tuple-element.28.own_h), channel_id=1, source_target_pairs={{0,4},{1,5},{2,6},{3,7},{12,8},{13,9},{14,10},{15,11},{16,20},{17,... | collective-permute-start | bytes 1179656 | tf_op jit(solution)/shard_map/ppermute | solution.py:64
  14.6 1.3 %collective-permute-start.9 = (bf16[256,512]{1,0:T(8,128)(2,1)S(1)}, bf16[256,512]{1,0:T(8,128)(2,1)S(1)}, u32[]{:S(2)}, u32[]{:S(2)}) collective-permute-start(bf16[256,512]{1,0:T(8,128)(2,1)S(1)} %get-tuple-element.27), channel_id=1, source_target_pairs={{0,4},{1,5},{2,6},{3,7},{12,8},{13,9},{14,10},{15,11},{16,20},{17,... | collective-permute-start | bytes 786440 | tf_op jit(solution)/shard_map/ppermute | solution.py:64
  15.9 1.3 %collective-permute-start.8 = (bf16[272,512]{1,0:T(8,128)(2,1)S(1)}, bf16[272,512]{1,0:T(8,128)(2,1)S(1)}, u32[]{:S(2)}, u32[]{:S(2)}) collective-permute-start(bf16[272,512]{1,0:T(8,128)(2,1)S(1)} %get-tuple-element.26), channel_id=1, source_target_pairs={{0,4},{1,5},{2,6},{3,7},{12,8},{13,9},{14,10},{15,11},{16,20},{17,... | collective-permute-start | bytes 835592 | tf_op jit(solution)/shard_map/ppermute | solution.py:64
  17.2 16.7 %collective-permute-done.9.nb = bf16[256,512]{1,0:T(8,128)(2,1)S(1)} collective-permute-done((bf16[256,512]{1,0:T(8,128)(2,1)S(1)}, bf16[256,512]{1,0:T(8,128)(2,1)S(1)}, u32[]{:S(2)}, u32[]{:S(2)}) %collective-permute-start.9) | collective-permute-done | bytes 262176 | tf_op jit(solution)/shard_map/ppermute | solution.py:64
  35.3 3.4 %collective-permute-done.8.na = bf16[272,512]{1,0:T(8,128)(2,1)S(1)} collective-permute-done((bf16[272,512]{1,0:T(8,128)(2,1)S(1)}, bf16[272,512]{1,0:T(8,128)(2,1)S(1)}, u32[]{:S(2)}, u32[]{:S(2)}) %collective-permute-start.8) | collective-permute-done | bytes 278560 | tf_op jit(solution)/shard_map/ppermute | solution.py:64
  38.8 1.3 %collective-permute-start.3 = (bf16[1792,128]{1,0:T(8,128)(2,1)S(1)}, bf16[1792,128]{1,0:T(8,128)(2,1)S(1)}, u32[]{:S(2)}, u32[]{:S(2)}) collective-permute-start(bf16[1792,128]{1,0:T(8,128)(2,1)S(1)} %get-tuple-element.23.own.own_l), channel_id=1, source_target_pairs={{4,0},{5,1},{6,2},{7,3},{8,12},{9,13},{10,14},{11,15},{20,16},{21,... | collective-permute-start | bytes 1376264 | tf_op jit(solution)/shard_map/ppermute | solution.py:64
  40.1 1.6 %collective-permute-start.6 = (bf16[272,1024]{1,0:T(8,128)(2,1)S(1)}, bf16[272,1024]{1,0:T(8,128)(2,1)S(1)}, u32[]{:S(2)}, u32[]{:S(2)}) collective-permute-start(bf16[272,1024]{1,0:T(8,128)(2,1)S(1)} %get-tuple-element.24.low_a), channel_id=1, source_target_pairs={{0,16},{1,17},{2,18},{3,19},{4,20},{5,21},{6,22},{7,23},{8,24},{9,... | collective-permute-start | bytes 1671176 | tf_op jit(solution)/shard_map/ppermute | solution.py:64
  42.4 1.3 %collective-permute-start.4 = (bf16[1792,128]{1,0:T(8,128)(2,1)S(1)}, bf16[1792,128]{1,0:T(8,128)(2,1)S(1)}, u32[]{:S(2)}, u32[]{:S(2)}) collective-permute-start(bf16[1792,128]{1,0:T(8,128)(2,1)S(1)} %collective-permute-done.1.mid_l), channel_id=1, source_target_pairs={{4,0},{5,1},{6,2},{7,3},{8,12},{9,13},{10,14},{11,15},{20,16},{21,... | collective-permute-start | bytes 1376264 | tf_op jit(solution)/shard_map/ppermute | solution.py:64
  43.7 1.3 %collective-permute-start.5 = (bf16[1792,128]{1,0:T(8,128)(2,1)S(1)}, bf16[1792,128]{1,0:T(8,128)(2,1)S(1)}, u32[]{:S(2)}, u32[]{:S(2)}) collective-permute-start(bf16[1792,128]{1,0:T(8,128)(2,1)S(1)} %collective-permute-done.2.far_l), channel_id=1, source_target_pairs={{4,0},{5,1},{6,2},{7,3},{8,12},{9,13},{10,14},{11,15},{20,16},{21,... | collective-permute-start | bytes 1376264 | tf_op jit(solution)/shard_map/ppermute | solution.py:64
  45.0 10.0 %collective-permute-done.3.out1 = bf16[1792,128]{1,0:T(8,128)(2,1)S(1)} collective-permute-done((bf16[1792,128]{1,0:T(8,128)(2,1)S(1)}, bf16[1792,128]{1,0:T(8,128)(2,1)S(1)}, u32[]{:S(2)}, u32[]{:S(2)}) %collective-permute-start.3) | collective-permute-done | bytes 458784 | tf_op jit(solution)/shard_map/ppermute | solution.py:64
  57.1 7.8 %collective-permute-done.4.out2 = bf16[1792,128]{1,0:T(8,128)(2,1)S(1)} collective-permute-done((bf16[1792,128]{1,0:T(8,128)(2,1)S(1)}, bf16[1792,128]{1,0:T(8,128)(2,1)S(1)}, u32[]{:S(2)}, u32[]{:S(2)}) %collective-permute-start.4) | collective-permute-done | bytes 458784 | tf_op jit(solution)/shard_map/ppermute | solution.py:64
  64.8 1.6 %early_columns.1 = (f32[1536,128]{1,0:T(8,128)S(1)}, f32[512,64]{1,0:T(8,128)S(1)}) custom-call(s32[3]{0:T(128)S(1)} %pad_add_fusion.ints_ref, bf16[272,1024]{1,0:T(8,128)(2,1)S(1)} %get-tuple-element.24.low_a, bf16[256,1024]{1,0:T(8,128)(2,1)S(1)} %get-tuple-element.25.high_a, bf16[272,1024]{1,0:T(8,128)(2,1)S(1)} %collective-permute-done.6.low_b, ...), custom_call_target="tpu_custom_call" | custom-call | tf_op jit(solution)/shard_map/early_columns/pallas_call | solution.py:19
  66.5 5.3 %collective-permute-done.5.out3 = bf16[1792,128]{1,0:T(8,128)(2,1)S(1)} collective-permute-done((bf16[1792,128]{1,0:T(8,128)(2,1)S(1)}, bf16[1792,128]{1,0:T(8,128)(2,1)S(1)}, u32[]{:S(2)}, u32[]{:S(2)}) %collective-permute-start.5) | collective-permute-done | bytes 458784 | tf_op jit(solution)/shard_map/ppermute | solution.py:64
  71.8 1.3 %late_columns.1 = (f32[2560,128]{1,0:T(8,128)S(1)}, bf16[2560,128]{1,0:T(8,128)(2,1)S(1)}) custom-call(s32[3]{0:T(128)S(1)} %pad_add_fusion.ints_ref, bf16[272,1024]{1,0:T(8,128)(2,1)S(1)} %get-tuple-element.24.low_a, bf16[256,1024]{1,0:T(8,128)(2,1)S(1)} %get-tuple-element.25.high_a, bf16[272,1024]{1,0:T(8,128)(2,1)S(1)} %collective-permute-done.6.low_b, ...), custom_call_target="tpu_custom_call" | custom-call | tf_op jit(solution)/shard_map/late_columns/pallas_call | solution.py:19
  73.2 2.1 %collective-permute-done.15.came_ref = bf16[2560,128]{1,0:T(8,128)(2,1)S(1)} collective-permute-done((bf16[2560,128]{1,0:T(8,128)(2,1)S(1)}, bf16[2560,128]{1,0:T(8,128)(2,1)S(1)}, u32[]{:S(2)}, u32[]{:S(2)}) %collective-permute-start.15) | collective-permute-done | bytes 655392 | tf_op jit(solution)/shard_map/ppermute | solution.py:64
  75.9 1.3 %collective-permute-start.16 = (bf16[384,128]{1,0:T(8,128)(2,1)S(1)}, bf16[384,128]{1,0:T(8,128)(2,1)S(1)}, u32[]{:S(2)}, u32[]{:S(2)}) collective-permute-start(bf16[384,128]{1,0:T(8,128)(2,1)S(1)} %get-tuple-element.34), channel_id=1, source_target_pairs={{4,0},{5,1},{6,2},{7,3},{8,12},{9,13},{10,14},{11,15},{20,16},{21,... | collective-permute-start | bytes 294920 | tf_op jit(solution)/shard_map/ppermute | solution.py:64
  77.2 1.3 %collective-permute-start.17 = (bf16[384,128]{1,0:T(8,128)(2,1)S(1)}, bf16[384,128]{1,0:T(8,128)(2,1)S(1)}, u32[]{:S(2)}, u32[]{:S(2)}) collective-permute-start(bf16[384,128]{1,0:T(8,128)(2,1)S(1)} %get-tuple-element.35), channel_id=1, source_target_pairs={{4,16},{5,17},{6,18},{7,19},{8,28},{9,29},{10,30},{11,31},{20,0},{... | collective-permute-start | bytes 294920 | tf_op jit(solution)/shard_map/ppermute | solution.py:64
  78.5 1.3 %collective-permute-start.18 = (bf16[384,128]{1,0:T(8,128)(2,1)S(1)}, bf16[384,128]{1,0:T(8,128)(2,1)S(1)}, u32[]{:S(2)}, u32[]{:S(2)}) collective-permute-start(bf16[384,128]{1,0:T(8,128)(2,1)S(1)} %get-tuple-element.36), channel_id=1, source_target_pairs={{4,2},{5,3},{6,0},{7,1},{8,14},{9,15},{10,12},{11,13},{20,18},{21,... | collective-permute-start | bytes 294920 | tf_op jit(solution)/shard_map/ppermute | solution.py:64
  79.8 1.3 %collective-permute-start.19 = (bf16[384,128]{1,0:T(8,128)(2,1)S(1)}, bf16[384,128]{1,0:T(8,128)(2,1)S(1)}, u32[]{:S(2)}, u32[]{:S(2)}) collective-permute-start(bf16[384,128]{1,0:T(8,128)(2,1)S(1)} %get-tuple-element.37), channel_id=1, source_target_pairs={{4,18},{5,19},{6,16},{7,17},{8,30},{9,31},{10,28},{11,29},{20,2},{... | collective-permute-start | bytes 294920 | tf_op jit(solution)/shard_map/ppermute | solution.py:64
  81.1 2.5 %collective-permute-start.20 = (bf16[384,128]{1,0:T(8,128)(2,1)S(1)}, bf16[384,128]{1,0:T(8,128)(2,1)S(1)}, u32[]{:S(2)}, u32[]{:S(2)}) collective-permute-start(bf16[384,128]{1,0:T(8,128)(2,1)S(1)} %get-tuple-element.38), channel_id=1, source_target_pairs={{0,18},{1,19},{2,16},{3,17},{4,22},{5,23},{6,20},{7,21},{8,26},{9,... | collective-permute-start | bytes 294920 | tf_op jit(solution)/shard_map/ppermute | solution.py:64
  83.6 8.2 %collective-permute-done.16.refs_0_ = bf16[384,128]{1,0:T(8,128)(2,1)S(1)} collective-permute-done((bf16[384,128]{1,0:T(8,128)(2,1)S(1)}, bf16[384,128]{1,0:T(8,128)(2,1)S(1)}, u32[]{:S(2)}, u32[]{:S(2)}) %collective-permute-start.16) | collective-permute-done | bytes 98336 | tf_op jit(solution)/shard_map/ppermute | solution.py:64
  91.8 1.5 %collective-permute-start.21 = (bf16[384,128]{1,0:T(8,128)(2,1)S(1)}, bf16[384,128]{1,0:T(8,128)(2,1)S(1)}, u32[]{:S(2)}, u32[]{:S(2)}) collective-permute-start(bf16[384,128]{1,0:T(8,128)(2,1)S(1)} %get-tuple-element.39), channel_id=1, source_target_pairs={{0,2},{1,3},{2,0},{3,1},{4,6},{5,7},{6,4},{7,5},{8,10},{9,11},{10,... | collective-permute-start | bytes 294920 | tf_op jit(solution)/shard_map/ppermute | solution.py:64
  93.3 1.4 %collective-permute-done.17.refs_1_ = bf16[384,128]{1,0:T(8,128)(2,1)S(1)} collective-permute-done((bf16[384,128]{1,0:T(8,128)(2,1)S(1)}, bf16[384,128]{1,0:T(8,128)(2,1)S(1)}, u32[]{:S(2)}, u32[]{:S(2)}) %collective-permute-start.17) | collective-permute-done | bytes 98336 | tf_op jit(solution)/shard_map/ppermute | solution.py:64
  96.0 1.1 %collective-permute-done.18.refs_2_ = bf16[384,128]{1,0:T(8,128)(2,1)S(1)} collective-permute-done((bf16[384,128]{1,0:T(8,128)(2,1)S(1)}, bf16[384,128]{1,0:T(8,128)(2,1)S(1)}, u32[]{:S(2)}, u32[]{:S(2)}) %collective-permute-start.18) | collective-permute-done | bytes 98336 | tf_op jit(solution)/shard_map/ppermute | solution.py:64
  97.1 2.5 %collective-permute-done.19.refs_3_ = bf16[384,128]{1,0:T(8,128)(2,1)S(1)} collective-permute-done((bf16[384,128]{1,0:T(8,128)(2,1)S(1)}, bf16[384,128]{1,0:T(8,128)(2,1)S(1)}, u32[]{:S(2)}, u32[]{:S(2)}) %collective-permute-start.19) | collective-permute-done | bytes 98336 | tf_op jit(solution)/shard_map/ppermute | solution.py:64
  99.9 0.8 collective-permute-done.22.refs_6_
  100.7 1.5 %finish.1 = bf16[256,256]{1,0:T(8,128)(2,1)} custom-call(s32[3]{0:T(128)S(1)} %pad_add_fusion.ints_ref, s32[8]{0:T(128)S(1)} %copy-done.4, s32[4]{0:T(128)S(1)} %copy-done.5, s32[4]{0:T(128)S(1)} %copy-done.6, bf16[4,256,128]{2,1,0:T(8,128)(2,1)S(1)} %ups.1.up_ref, f32[384,128]{1,0:T(8,128)S(1)} %get-tuple-element.33.mine_ref, ...), custom_call_target="tpu_custom_call" | custom-call | tf_op jit(solution)/shard_map/finish/pallas_call | solution.py:19
  (36 shorter events, 7.9 us)
Async XLA Ops:
  0.0 13.8 %copy-start.5 = (s32[4]{0:T(128)S(1)}, s32[4]{0:T(128)}, u32[]{:S(2)}) copy-start(s32[4]{0:T(128)} %block_ref.3) | copy-start | bytes 52
  0.0 13.8 %copy-start.4 = (s32[8]{0:T(128)S(1)}, s32[8]{0:T(128)}, u32[]{:S(2)}) copy-start(s32[8]{0:T(128)} %table_ref.3) | copy-start | bytes 100
  0.1 1.2 %copy-start = (bf16[2048,256]{1,0:T(8,128)(2,1)S(1)}, bf16[2048,256]{1,0:T(8,128)(2,1)}, u32[]{:S(2)}) copy-start(bf16[2048,256]{1,0:T(8,128)(2,1)} %w_ref.1) | copy-start | bytes 3145732
  1.3 1.0 %copy-start.2 = (bf16[2,2048,64]{1,2,0:T(8,128)(2,1)S(1)}, bf16[2,2048,64]{1,2,0:T(8,128)(2,1)}, u32[]{:S(2)}) copy-start(bf16[2,2048,64]{1,2,0:T(8,128)(2,1)} %param.9) | copy-start | bytes 1572868
  2.3 0.8 copy-start.3
  3.2 10.6 %copy-start.1 = (bf16[256,2048]{1,0:T(8,128)(2,1)S(1)}, bf16[256,2048]{1,0:T(8,128)(2,1)}, u32[]{:S(2)}) copy-start(bf16[256,2048]{1,0:T(8,128)(2,1)} %tok_ref.1) | copy-start | bytes 3145732
  4.1 30.6 %collective-permute-start = (bf16[1792,128]{1,0:T(8,128)(2,1)S(1)}, bf16[1792,128]{1,0:T(8,128)(2,1)S(1)}, u32[]{:S(2)}, u32[]{:S(2)}) collective-permute-start(bf16[1792,128]{1,0:T(8,128)(2,1)S(1)} %get-tuple-element.23.own.own_l), channel_id=1, source_target_pairs={{0,4},{1,5},{2,6},{3,7},{12,8},{13,9},{14,10},{15,11},{16,20},{17,... | collective-permute-start | bytes 1376264 | tf_op jit(solution)/shard_map/ppermute | solution.py:64
  9.0 31.0 %collective-permute-start.13 = (bf16[1536,128]{1,0:T(8,128)(2,1)S(1)}, bf16[1536,128]{1,0:T(8,128)(2,1)S(1)}, u32[]{:S(2)}, u32[]{:S(2)}) collective-permute-start(bf16[1536,128]{1,0:T(8,128)(2,1)S(1)} %get-tuple-element.28.own_h), channel_id=1, source_target_pairs={{4,8},{5,9},{6,10},{7,11},{8,4},{9,5},{10,6},{11,7},{20,24},{21,25... | collective-permute-start | bytes 1179656 | tf_op jit(solution)/shard_map/ppermute | solution.py:64
  9.7 31.9 %collective-permute-start.12 = (bf16[1536,128]{1,0:T(8,128)(2,1)S(1)}, bf16[1536,128]{1,0:T(8,128)(2,1)S(1)}, u32[]{:S(2)}, u32[]{:S(2)}) collective-permute-start(bf16[1536,128]{1,0:T(8,128)(2,1)S(1)} %get-tuple-element.28.own_h), channel_id=1, source_target_pairs={{0,4},{1,5},{2,6},{3,7},{12,8},{13,9},{14,10},{15,11},{16,20},{17,... | collective-permute-start | bytes 1179656 | tf_op jit(solution)/shard_map/ppermute | solution.py:64
  14.6 19.4 %collective-permute-start.9 = (bf16[256,512]{1,0:T(8,128)(2,1)S(1)}, bf16[256,512]{1,0:T(8,128)(2,1)S(1)}, u32[]{:S(2)}, u32[]{:S(2)}) collective-permute-start(bf16[256,512]{1,0:T(8,128)(2,1)S(1)} %get-tuple-element.27), channel_id=1, source_target_pairs={{0,4},{1,5},{2,6},{3,7},{12,8},{13,9},{14,10},{15,11},{16,20},{17,... | collective-permute-start | bytes 786440 | tf_op jit(solution)/shard_map/ppermute | solution.py:64
  15.9 22.9 %collective-permute-start.8 = (bf16[272,512]{1,0:T(8,128)(2,1)S(1)}, bf16[272,512]{1,0:T(8,128)(2,1)S(1)}, u32[]{:S(2)}, u32[]{:S(2)}) collective-permute-start(bf16[272,512]{1,0:T(8,128)(2,1)S(1)} %get-tuple-element.26), channel_id=1, source_target_pairs={{0,4},{1,5},{2,6},{3,7},{12,8},{13,9},{14,10},{15,11},{16,20},{17,... | collective-permute-start | bytes 835592 | tf_op jit(solution)/shard_map/ppermute | solution.py:64
  34.0 8.4 %collective-permute-start.1 = (bf16[1792,128]{1,0:T(8,128)(2,1)S(1)}, bf16[1792,128]{1,0:T(8,128)(2,1)S(1)}, u32[]{:S(2)}, u32[]{:S(2)}) collective-permute-start(bf16[1792,128]{1,0:T(8,128)(2,1)S(1)} %get-tuple-element.23.own.own_l), channel_id=1, source_target_pairs={{4,8},{5,9},{6,10},{7,11},{8,4},{9,5},{10,6},{11,7},{20,24},{21,25... | collective-permute-start | bytes 1376264 | tf_op jit(solution)/shard_map/ppermute | solution.py:64
  34.6 9.0 %collective-permute-start.2 = (bf16[1792,128]{1,0:T(8,128)(2,1)S(1)}, bf16[1792,128]{1,0:T(8,128)(2,1)S(1)}, u32[]{:S(2)}, u32[]{:S(2)}) collective-permute-start(bf16[1792,128]{1,0:T(8,128)(2,1)S(1)} %collective-permute-done.in_l), channel_id=1, source_target_pairs={{4,8},{5,9},{6,10},{7,11},{8,4},{9,5},{10,6},{11,7},{20,24},{21,25... | collective-permute-start | bytes 1376264 | tf_op jit(solution)/shard_map/ppermute | solution.py:64
  38.8 16.2 %collective-permute-start.3 = (bf16[1792,128]{1,0:T(8,128)(2,1)S(1)}, bf16[1792,128]{1,0:T(8,128)(2,1)S(1)}, u32[]{:S(2)}, u32[]{:S(2)}) collective-permute-start(bf16[1792,128]{1,0:T(8,128)(2,1)S(1)} %get-tuple-element.23.own.own_l), channel_id=1, source_target_pairs={{4,0},{5,1},{6,2},{7,3},{8,12},{9,13},{10,14},{11,15},{20,16},{21,... | collective-permute-start | bytes 1376264 | tf_op jit(solution)/shard_map/ppermute | solution.py:64
  40.1 16.3 %collective-permute-start.6 = (bf16[272,1024]{1,0:T(8,128)(2,1)S(1)}, bf16[272,1024]{1,0:T(8,128)(2,1)S(1)}, u32[]{:S(2)}, u32[]{:S(2)}) collective-permute-start(bf16[272,1024]{1,0:T(8,128)(2,1)S(1)} %get-tuple-element.24.low_a), channel_id=1, source_target_pairs={{0,16},{1,17},{2,18},{3,19},{4,20},{5,21},{6,22},{7,23},{8,24},{9,... | collective-permute-start | bytes 1671176 | tf_op jit(solution)/shard_map/ppermute | solution.py:64
  41.7 14.0 %collective-permute-start.7 = (bf16[256,1024]{1,0:T(8,128)(2,1)S(1)}, bf16[256,1024]{1,0:T(8,128)(2,1)S(1)}, u32[]{:S(2)}, u32[]{:S(2)}) collective-permute-start(bf16[256,1024]{1,0:T(8,128)(2,1)S(1)} %get-tuple-element.25.high_a), channel_id=1, source_target_pairs={{4,20},{5,21},{6,22},{7,23},{8,24},{9,25},{10,26},{11,27},{20,4},{... | collective-permute-start | bytes 1572872 | tf_op jit(solution)/shard_map/ppermute | solution.py:64
  42.4 22.5 %collective-permute-start.4 = (bf16[1792,128]{1,0:T(8,128)(2,1)S(1)}, bf16[1792,128]{1,0:T(8,128)(2,1)S(1)}, u32[]{:S(2)}, u32[]{:S(2)}) collective-permute-start(bf16[1792,128]{1,0:T(8,128)(2,1)S(1)} %collective-permute-done.1.mid_l), channel_id=1, source_target_pairs={{4,0},{5,1},{6,2},{7,3},{8,12},{9,13},{10,14},{11,15},{20,16},{21,... | collective-permute-start | bytes 1376264 | tf_op jit(solution)/shard_map/ppermute | solution.py:64
  43.7 28.2 %collective-permute-start.5 = (bf16[1792,128]{1,0:T(8,128)(2,1)S(1)}, bf16[1792,128]{1,0:T(8,128)(2,1)S(1)}, u32[]{:S(2)}, u32[]{:S(2)}) collective-permute-start(bf16[1792,128]{1,0:T(8,128)(2,1)S(1)} %collective-permute-done.2.far_l), channel_id=1, source_target_pairs={{4,0},{5,1},{6,2},{7,3},{8,12},{9,13},{10,14},{11,15},{20,16},{21,... | collective-permute-start | bytes 1376264 | tf_op jit(solution)/shard_map/ppermute | solution.py:64
  55.0 11.5 %collective-permute-start.14 = (bf16[1536,128]{1,0:T(8,128)(2,1)S(1)}, bf16[1536,128]{1,0:T(8,128)(2,1)S(1)}, u32[]{:S(2)}, u32[]{:S(2)}) collective-permute-start(bf16[1536,128]{1,0:T(8,128)(2,1)S(1)} %collective-permute-done.12.in_h), channel_id=1, source_target_pairs={{4,8},{5,9},{6,10},{7,11},{8,4},{9,5},{10,6},{11,7},{20,24},{21,25... | collective-permute-start | bytes 1179656 | tf_op jit(solution)/shard_map/ppermute | solution.py:64
  55.7 10.8 %collective-permute-start.10 = (bf16[272,512]{1,0:T(8,128)(2,1)S(1)}, bf16[272,512]{1,0:T(8,128)(2,1)S(1)}, u32[]{:S(2)}, u32[]{:S(2)}) collective-permute-start(bf16[272,512]{1,0:T(8,128)(2,1)S(1)} %collective-permute-done.8.na), channel_id=1, source_target_pairs={{4,20},{5,21},{6,22},{7,23},{8,24},{9,25},{10,26},{11,27},{20,4},{... | collective-permute-start | bytes 835592 | tf_op jit(solution)/shard_map/ppermute | solution.py:64
  56.4 10.0 %collective-permute-start.11 = (bf16[256,512]{1,0:T(8,128)(2,1)S(1)}, bf16[256,512]{1,0:T(8,128)(2,1)S(1)}, u32[]{:S(2)}, u32[]{:S(2)}) collective-permute-start(bf16[256,512]{1,0:T(8,128)(2,1)S(1)} %collective-permute-done.9.nb), channel_id=1, source_target_pairs={{4,20},{5,21},{6,22},{7,23},{8,24},{9,25},{10,26},{11,27},{20,4},{... | collective-permute-start | bytes 786440 | tf_op jit(solution)/shard_map/ppermute | solution.py:64
  73.1 2.2 %collective-permute-start.15 = (bf16[2560,128]{1,0:T(8,128)(2,1)S(1)}, bf16[2560,128]{1,0:T(8,128)(2,1)S(1)}, u32[]{:S(2)}, u32[]{:S(2)}) collective-permute-start(bf16[2560,128]{1,0:T(8,128)(2,1)S(1)} %get-tuple-element.32), channel_id=1, source_target_pairs={{0,1},{1,0},{2,3},{3,2},{4,5},{5,4},{6,7},{7,6},{8,9},{9,8},{10,11... | collective-permute-start | bytes 1966088 | tf_op jit(solution)/shard_map/ppermute | solution.py:64
  75.9 15.9 %collective-permute-start.16 = (bf16[384,128]{1,0:T(8,128)(2,1)S(1)}, bf16[384,128]{1,0:T(8,128)(2,1)S(1)}, u32[]{:S(2)}, u32[]{:S(2)}) collective-permute-start(bf16[384,128]{1,0:T(8,128)(2,1)S(1)} %get-tuple-element.34), channel_id=1, source_target_pairs={{4,0},{5,1},{6,2},{7,3},{8,12},{9,13},{10,14},{11,15},{20,16},{21,... | collective-permute-start | bytes 294920 | tf_op jit(solution)/shard_map/ppermute | solution.py:64
  77.2 17.5 %collective-permute-start.17 = (bf16[384,128]{1,0:T(8,128)(2,1)S(1)}, bf16[384,128]{1,0:T(8,128)(2,1)S(1)}, u32[]{:S(2)}, u32[]{:S(2)}) collective-permute-start(bf16[384,128]{1,0:T(8,128)(2,1)S(1)} %get-tuple-element.35), channel_id=1, source_target_pairs={{4,16},{5,17},{6,18},{7,19},{8,28},{9,29},{10,30},{11,31},{20,0},{... | collective-permute-start | bytes 294920 | tf_op jit(solution)/shard_map/ppermute | solution.py:64
  78.5 18.5 %collective-permute-start.18 = (bf16[384,128]{1,0:T(8,128)(2,1)S(1)}, bf16[384,128]{1,0:T(8,128)(2,1)S(1)}, u32[]{:S(2)}, u32[]{:S(2)}) collective-permute-start(bf16[384,128]{1,0:T(8,128)(2,1)S(1)} %get-tuple-element.36), channel_id=1, source_target_pairs={{4,2},{5,3},{6,0},{7,1},{8,14},{9,15},{10,12},{11,13},{20,18},{21,... | collective-permute-start | bytes 294920 | tf_op jit(solution)/shard_map/ppermute | solution.py:64
  79.8 19.7 %collective-permute-start.19 = (bf16[384,128]{1,0:T(8,128)(2,1)S(1)}, bf16[384,128]{1,0:T(8,128)(2,1)S(1)}, u32[]{:S(2)}, u32[]{:S(2)}) collective-permute-start(bf16[384,128]{1,0:T(8,128)(2,1)S(1)} %get-tuple-element.37), channel_id=1, source_target_pairs={{4,18},{5,19},{6,16},{7,17},{8,30},{9,31},{10,28},{11,29},{20,2},{... | collective-permute-start | bytes 294920 | tf_op jit(solution)/shard_map/ppermute | solution.py:64
  81.1 18.4 %collective-permute-start.20 = (bf16[384,128]{1,0:T(8,128)(2,1)S(1)}, bf16[384,128]{1,0:T(8,128)(2,1)S(1)}, u32[]{:S(2)}, u32[]{:S(2)}) collective-permute-start(bf16[384,128]{1,0:T(8,128)(2,1)S(1)} %get-tuple-element.38), channel_id=1, source_target_pairs={{0,18},{1,19},{2,16},{3,17},{4,22},{5,23},{6,20},{7,21},{8,26},{9,... | collective-permute-start | bytes 294920 | tf_op jit(solution)/shard_map/ppermute | solution.py:64
  91.8 8.1 %collective-permute-start.21 = (bf16[384,128]{1,0:T(8,128)(2,1)S(1)}, bf16[384,128]{1,0:T(8,128)(2,1)S(1)}, u32[]{:S(2)}, u32[]{:S(2)}) collective-permute-start(bf16[384,128]{1,0:T(8,128)(2,1)S(1)} %get-tuple-element.39), channel_id=1, source_target_pairs={{0,2},{1,3},{2,0},{3,1},{4,6},{5,7},{6,4},{7,5},{8,10},{9,11},{10,... | collective-permute-start | bytes 294920 | tf_op jit(solution)/shard_map/ppermute | solution.py:64
  94.7 6.0 %copy-start.6 = (s32[4]{0:T(128)S(1)}, s32[4]{0:T(128)}, u32[]{:S(2)}) copy-start(s32[4]{0:T(128)} %live_ref.1) | copy-start | bytes 52
  94.7 6.0 %collective-permute-start.22 = (bf16[384,128]{1,0:T(8,128)(2,1)S(1)}, bf16[384,128]{1,0:T(8,128)(2,1)S(1)}, u32[]{:S(2)}, u32[]{:S(2)}) collective-permute-start(bf16[384,128]{1,0:T(8,128)(2,1)S(1)} %get-tuple-element.40), channel_id=1, source_target_pairs={{0,16},{1,17},{2,18},{3,19},{4,20},{5,21},{6,22},{7,23},{8,24},{9,... | collective-permute-start | bytes 294920 | tf_op jit(solution)/shard_map/ppermute | solution.py:64

commit v3 on v0

--- a/solution.py
+++ b/solution.py
@@ -1,7 +1,428 @@
 import jax
 import jax.numpy as jnp
 from jax import lax
+from jax.experimental import pallas as pl
+from jax.experimental.pallas import tpu as pltpu
 from jax.sharding import PartitionSpec as P
+
+AXES = ("groups", "dp", "tensor")
+LANES = 128
+CODE_ROWS = 16
+F32 = jnp.float32
+BF16 = jnp.bfloat16
+VMEM = pl.BlockSpec(memory_space=pltpu.VMEM)
+SMEM = pl.BlockSpec(memory_space=pltpu.SMEM)
+HBM = pl.BlockSpec(memory_space=pltpu.HBM)
+
+
+def call(body, name, outs, specs, ins, scratch=(), mib=16):
+    return pl.pallas_call(
+        body,
+        name=name,
+        out_shape=outs,
+        in_specs=specs,
+        out_specs=jax.tree.map(lambda _: VMEM, outs),
+        scratch_shapes=scratch,
+        compiler_params=pltpu.CompilerParams(vmem_limit_bytes=mib * 2**20),
+    )(*ins)
+
+
+def like(rows, cols, dtype=BF16):
+    return jax.ShapeDtypeStruct((rows, cols), dtype)
+
+
+def local_line(sizes, tokens, value_weight, down, up, slot_table, per_block, live_rows):
+    groups, dp, tensor = sizes
+    y, z, t = (lax.axis_index(a) for a in AXES)
+    place = jnp.stack([y, z, t]).astype(jnp.int32)
+    rows, feats = tokens.shape
+    blocks = per_block.shape[0]
+    block_len = rows // blocks
+    per_dev, _, rank = down.shape
+    out_cols = up.shape[2]
+    half_cols = value_weight.shape[1] // groups
+    half = feats // 2
+    up_rows = per_dev * rank * out_cols // LANES
+    col_tiles = out_cols // LANES
+    pairs = dp // 2
+    both = groups * rows
+    s_msg = rows // 2
+    total = pairs * both + 3 * s_msg
+
+    def device(a, b, c):
+        return (a * dp + b) * tensor + c
+
+    def swap(x, where):
+        perm = [
+            (device(a, b, c), device(*where(a, b, c)))
+            for a in range(groups)
+            for b in range(dp)
+            for c in range(tensor)
+        ]
+        return lax.ppermute(x, AXES, perm)
+
+    def to_neighbour(x):
+        return swap(x, lambda a, b, c: (a, b ^ 1, c))
+
+    def to_middle(x):
+        return swap(x, lambda a, b, c: (a, 3 - b, c) if b in (1, 2) else (a, b, c ^ 1))
+
+    def to_group(x):
+        return swap(x, lambda a, b, c: (1 - a, b, c))
+
+    def tie(x, *earlier):
+        return lax.optimization_barrier((x, *earlier))[0]
+
+    def outer_plane(here):
+        return (here == 0) | (here == 3)
+
+    def where_from(here, slot):
+        near = here ^ 1
+        if slot == 0:
+            return here
+        if slot == 1:
+            return near
+        if slot == 2:
+            return jnp.where(outer_plane(here), 3 - near, 3 - here)
+        return jnp.where(outer_plane(here), 3 - here, 3 - near)
+
+    def block_at(table_ref, block_ref, holder):
+        which, local_slot = jnp.int32(0), jnp.int32(0)
+        for k in range(blocks):
+            s = table_ref[block_ref[k]]
+            hit = s // per_dev == holder
+            which = jnp.where(hit, k, which)
+            local_slot = jnp.where(hit, s % per_dev, local_slot)
+        return which, local_slot
+
+    def pack(ints_ref, w_ref, d_ref, u_ref, wide_ref, own_ref, other_ref, d_held, sems):
+        me = ints_ref[0]
+        cols = pl.ds(pl.multiple_of(me * half_cols, LANES), half_cols)
+        copies = [
+            pltpu.make_async_copy(d_ref.at[me], d_held.at[0], sems.at[0]),
+            pltpu.make_async_copy(d_ref.at[1 - me], d_held.at[1], sems.at[1]),
+            pltpu.make_async_copy(w_ref.at[:, cols], wide_ref.at[pl.ds(0, feats)], sems.at[2]),
+        ]
+        for s in range(per_dev):
+            for v in range(col_tiles):
+                n = s * col_tiles + v
+                copies.append(
+                    pltpu.make_async_copy(
+                        u_ref.at[s, :, pl.ds(v * LANES, LANES)],
+                        wide_ref.at[pl.ds(feats + n * rank, rank)],
+                        sems.at[3 + n],
+                    )
+                )
+        for c in copies:
+            c.start()
+        for n, ref in ((0, own_ref), (1, other_ref)):
+            copies[n].wait()
+            ref[...] = jnp.concatenate([d_held[n, :, 0:half], d_held[n, :, half:feats]], axis=0).T
+        for c in copies[2:]:
+            c.wait()
+
+    own_w, own_d, own_e = call(
+        pack,
+        "pack_weights",
+        (like(feats + up_rows, LANES), like(half, LANES), like(half, LANES)),
+        [SMEM, HBM, HBM, HBM],
+        (place, value_weight, jnp.transpose(down, (0, 2, 1)), up),
+        [
+            pltpu.VMEM((per_dev, rank, feats), BF16),
+            pltpu.SemaphoreType.DMA((3 + per_dev * col_tiles,)),
+        ],
+        mib=56,
+    )
+
+    tiles = feats // LANES
+    tile_rows = tiles * block_len
+    wide_rows = feats + up_rows
+    code_at = half + tile_rows
+
+    def pack_tokens(
+        ints_ref, table_ref, block_ref, tok_ref, d_ref, sorted_ref, first_ref, second_ref, sems
+    ):
+        here = ints_ref[1]
+        copies = []
+        row = lax.broadcasted_iota(jnp.int32, (CODE_ROWS, LANES), 0)
+        code = jnp.zeros((CODE_ROWS, LANES), jnp.int32)
+        for slot in range(dp):
+            which, local_slot = block_at(table_ref, block_ref, where_from(here, slot))
+            src = tok_ref.at[pl.ds(pl.multiple_of(which * block_len, block_len), block_len)]
+            to = sorted_ref.at[pl.ds(slot * block_len, block_len)]
+            copies.append(pltpu.make_async_copy(src, to, sems.at[slot]))
+            copies[-1].start()
+            code = jnp.where(row == slot, local_slot, code)
+        code = code.astype(F32).astype(BF16)
+        sorted_ref[rows:, 0:LANES] = code
+        first_ref[code_at : code_at + CODE_ROWS, :] = code
+        first_ref[0:half, :] = d_ref[...]
+        for c in copies:
+            c.wait()
+        for n, (ref, at) in enumerate(((first_ref, half), (second_ref, 0), (second_ref, tile_rows))):
+            for i in range(tiles):
+                ref[at + i * block_len : at + (i + 1) * block_len, :] = sorted_ref[
+                    (n + 1) * block_len : (n + 2) * block_len, i * LANES : (i + 1) * LANES
+                ]
+
+    in_order, first, second = call(
+        pack_tokens,
+        "pack_blocks",
+        (
+            like(rows + CODE_ROWS, feats),
+            like(wide_rows, LANES),
+            like(wide_rows, LANES),
+        ),
+        [SMEM, SMEM, SMEM, HBM, VMEM],
+        (place, slot_table, per_block, tokens, own_d),
+        [pltpu.SemaphoreType.DMA((dp,))],
+        mib=56,
+    )
+
+    def choose(ints_ref, outer_ref, inner_ref, out_ref):
+        is_outer = outer_plane(ints_ref[1])
+
+        @pl.when(is_outer)
+        def _():
+            out_ref[...] = outer_ref[...]
+
+        @pl.when(jnp.logical_not(is_outer))
+        def _():
+            out_ref[...] = inner_ref[...]
+
+    def chosen(x, y):
+        return call(choose, "choose", like(wide_rows, LANES), [SMEM, VMEM, VMEM], (place, x, y))
+
+    near_w = to_neighbour(own_w)
+    mid_w = to_middle(own_w)
+    others = to_group(in_order)
+    two = to_neighbour(chosen(first, mid_w))
+    far_w = to_middle(near_w)
+    mid_d = to_middle(tie(own_d, near_w))
+    three = to_neighbour(chosen(second, far_w))
+    mid_e = to_group(tie(mid_d, others))
+    far_d = to_middle(tie(two[0:half], mid_d))
+    far_e = to_group(tie(far_d, mid_e))
+
+    def columns(a_ref, b_ref, w_ref, out_ref, at):
+        for g, x in enumerate((a_ref, b_ref)):
+            out_ref[at + g * rows : at + (g + 1) * rows, :] = jnp.dot(
+                x[0:rows, :], w_ref[0:feats, :], preferred_element_type=F32
+            )
+
+    def early(ints_ref, a_ref, b_ref, w0, w1, mid, out, part_ref):
+        columns(a_ref, b_ref, w0, part_ref, 0)
+        columns(a_ref, b_ref, w1, part_ref, both)
+        is_outer = outer_plane(ints_ref[1])
+        pl.when(is_outer)(lambda: columns(a_ref, b_ref, out, part_ref, 2 * both))
+        pl.when(jnp.logical_not(is_outer))(lambda: columns(a_ref, b_ref, mid, part_ref, 2 * both))
+
+    part = call(
+        early,
+        "early_columns",
+        like(3 * both, LANES, F32),
+        [SMEM] + [VMEM] * 6,
+        (place, in_order, others, own_w, near_w, mid_w, two),
+    )
+
+    def late(
+        ints_ref, a_ref, b_ref, two_ref, three_ref, d0, e0, d2, e2, d3, e3,
+        far, part_ref, keep, away, last_ref, s_ref,
+    ):
+        me, here, core = ints_ref[0], ints_ref[1], ints_ref[2] % 2
+        is_outer = outer_plane(here)
+
+        def put(ref, ref_at, holder):
+            at = pl.ds(pl.multiple_of((holder // 2) * both, both), both)
+
+            @pl.when(holder % 2 == core)
+            def _():
+                keep[at, :] = ref[ref_at : ref_at + both, :]
+
+            @pl.when(holder % 2 != core)
+            def _():
+                away[at, :] = ref[ref_at : ref_at + both, :].astype(BF16)
+
+        number = me.astype(F32)
+        codes = [ref[rows:, 0:LANES].astype(F32) for ref in (a_ref, b_ref)]
+        near_codes = two_ref[code_at : code_at + CODE_ROWS, :].astype(F32)
+        s_ref[...] = jnp.zeros_like(s_ref)
+
+        def shrink(slot, d_ref, e_ref=None, theirs=0):
+            at = slice(slot * block_len, (slot + 1) * block_len)
+            x = [a_ref[at, :], b_ref[at, :]]
+            rhs = d_ref[0:half, :]
+            if theirs:
+                ref, near_at = ((two_ref, half), (three_ref, 0), (three_ref, tile_rows))[theirs - 1]
+                x.append(
+                    jnp.concatenate(
+                        [
+                            ref[near_at + i * block_len : near_at + (i + 1) * block_len, :]
+                            for i in range(tiles)
+                        ],
+                        axis=1,
+                    )
+                )
+                rhs = jnp.concatenate([rhs, e_ref[...]], axis=1)
+            x = jnp.concatenate(x, axis=0)
+            low = jnp.dot(x[:, 0:half], rhs, preferred_element_type=F32)
+            high = jnp.dot(x[:, half:feats], rhs, preferred_element_type=F32)
+            mine = low[:, 0:rank] + high[:, rank : 2 * rank]
+            for g in range(groups):
+                hit = codes[g][slot : slot + 1, 0:rank] == number
+                s_ref[g, at, :] = jnp.where(hit, mine[g * block_len : (g + 1) * block_len, :], 0.0)
+            if theirs:
+                last = slice(groups * block_len, (groups + 1) * block_len)
+                other = (
+                    low[last, LANES : LANES + rank] + high[last, LANES + rank : LANES + 2 * rank]
+                )
+                hit = near_codes[theirs : theirs + 1, 0:rank] == number
+                s_ref[2, theirs * block_len : (theirs + 1) * block_len, :] = jnp.where(
+                    hit, mine[last, :], other
+                )
+
+        @pl.when(is_outer)
+        def _():
+            columns(a_ref, b_ref, three_ref, last_ref, 0)
+            shrink(0, d0)
+
+        @pl.when(jnp.logical_not(is_outer))
+        def _():
+            columns(a_ref, b_ref, far, last_ref, 0)
+            shrink(0, d0, e0, 1)
+            shrink(1, two_ref)
+            shrink(2, d2, e2, 2)
+            shrink(3, d3, e3, 3)
+
+        for slot in range(3):
+            put(part_ref, slot * both, where_from(here, slot))
+        put(last_ref, 0, where_from(here, 3))
+        for g in range(3):
+            s = jnp.concatenate([s_ref[g, 0:s_msg, :], s_ref[g, s_msg:rows, :]], axis=1)
+            at = pairs * both + g * s_msg
+            keep[at : at + s_msg, :] = s
+            away[at : at + s_msg, :] = s.astype(BF16)
+
+    keep, away = call(
+        late,
+        "late_columns",
+        (like(total, LANES, F32), like(total, LANES)),
+        [SMEM] + [VMEM] * 12,
+        (
+            place, in_order, others, two, three, own_d, own_e, mid_d, mid_e,
+            far_d, far_e, far_w, part,
+        ),
+        [pltpu.VMEM((both, LANES), F32), pltpu.VMEM((3, rows, rank), F32)],
+    )
+    came = swap(away, lambda a, b, c: (a, b, c ^ 1))
+
+    def add_cores(ints_ref, keep_ref, came_ref, mine_out, x_out, y_out, d_out, near_out):
+        side = ints_ref[2] // 2
+
+        def tile(out, side_at, g):
+            at = pl.ds(pl.multiple_of(side_at * both + g * rows, rows), rows)
+            out[0:rows, :] = (keep_ref[at, :] + came_ref[at, :].astype(F32)).astype(out.dtype)
+
+        def low_rank(out, at, g):
+            s = pl.ds(pairs * both + g * s_msg, s_msg)
+            out[at : at + s_msg, :] = (keep_ref[s, :] + came_ref[s, :].astype(F32)).astype(out.dtype)
+
+        tile(mine_out, side, 0)
+        tile(x_out, 1 - side, 0)
+        tile(y_out, side, 1)
+        tile(d_out, 1 - side, 1)
+        low_rank(mine_out, rows, 0)
+        low_rank(x_out, rows, 0)
+        low_rank(y_out, rows, 1)
+        low_rank(d_out, rows, 1)
+        low_rank(near_out, 0, 2)
+
+    mine, to_x, to_y, to_d, to_near = call(
+        add_cores,
+        "add_cores",
+        (
+            like(rows + s_msg, LANES, F32),
+            like(rows + s_msg, LANES),
+            like(rows + s_msg, LANES),
+            like(rows + s_msg, LANES),
+            like(s_msg, LANES),
+        ),
+        [SMEM, VMEM, VMEM],
+        (place, keep, came),
+    )
+    from_d = swap(to_d, lambda a, b, c: (1 - a, b, c ^ 2))
+    from_nearx = swap(to_near, lambda a, b, c: (a, b ^ 1, c ^ 2))
+    from_x = swap(to_x, lambda a, b, c: (a, b, c ^ 2))
+    from_y = to_group(to_y)
+    from_near = to_neighbour(to_near)
+
+    def ups(ints_ref, own, near, mid, far, out2, out3, out):
+        here = ints_ref[1]
+        is_outer = outer_plane(here)
+
+        def put(ref, slot):
+            out[where_from(here, slot)] = ref[feats : feats + up_rows, :]
+
+        put(own, 0)
+        put(near, 1)
+
+        @pl.when(is_outer)
+        def _():
+            put(out2, 2)
+            put(out3, 3)
+
+        @pl.when(jnp.logical_not(is_outer))
+        def _():
+            put(mid, 2)
+            put(far, 3)
+
+    up_all = call(
+        ups,
+        "ups",
+        jax.ShapeDtypeStruct((dp, up_rows, LANES), BF16),
+        [SMEM] + [VMEM] * 6,
+        (place, own_w, near_w, mid_w, far_w, two, three),
+    )
+
+    def finish(
+        ints_ref, table_ref, block_ref, live_ref, up_ref, mine_ref, x_ref, y_ref, d_ref, n_ref,
+        nx_ref, out_ref,
+    ):
+        me, here = ints_ref[0], ints_ref[1]
+        ours = mine_ref[0:rows, :] + x_ref[0:rows, :].astype(F32)
+        theirs = y_ref[0:rows, :].astype(F32) + d_ref[0:rows, :].astype(F32)
+        split = (jnp.where(me == 0, ours, theirs), jnp.where(me == 0, theirs, ours))
+        s = mine_ref[rows:, :] + n_ref[...].astype(F32) + nx_ref[...].astype(F32)
+        for ref in (x_ref, y_ref, d_ref):
+            s = s + ref[rows:, :].astype(F32)
+        s = s.astype(BF16)
+        per_lane = dp // 2
+        row = lax.broadcasted_iota(jnp.int32, (block_len, LANES), 0)
+        for slot in range(dp):
+            holder = where_from(here, slot)
+            which, local_slot = block_at(table_ref, block_ref, holder)
+            piece = s[
+                (slot % per_lane) * block_len : (slot % per_lane + 1) * block_len,
+                (slot // per_lane) * rank : (slot // per_lane + 1) * rank,
+            ]
+            to = pl.ds(pl.multiple_of(which * block_len, block_len), block_len)
+            for v in range(col_tiles):
+                at = pl.ds(pl.multiple_of((local_slot * col_tiles + v) * rank, rank), rank)
+                delta = jnp.dot(piece, up_ref[holder, at, :], preferred_element_type=F32)
+                base = split[v][slot * block_len : (slot + 1) * block_len, :]
+                mixed = jnp.where(row < live_ref[which], base + delta.astype(BF16).astype(F32), 0.0)
+                out_ref[to, v * LANES : (v + 1) * LANES] = mixed.astype(BF16)
+
+    return call(
+        finish,
+        "finish",
+        like(rows, out_cols),
+        [SMEM] * 4 + [VMEM] * 7,
+        (
+            place, slot_table, per_block, live_rows, up_all, mine, from_x, from_y, from_d,
+            from_near, from_nearx,
+        ),
+    )
 
 
 def local(
@@ -95,6 +516,11 @@
         P(("groups", "dp")),
         P(("groups", "dp")),
     )
+    sizes = tuple(mesh.shape[a] for a in AXES)
+    if sizes == (2, 4, 4):
+        body = lambda *args: local_line(sizes, *args)
+    else:
+        body = local
     return jax.shard_map(
-        local, mesh=mesh, in_specs=placed, out_specs=P(("groups", "dp"), "tensor"), check_vma=False
-    )
+        body, mesh=mesh, in_specs=placed, out_specs=P(("groups", "dp"), "tensor"), check_vma=False
+    )

time: 165 us -> 71.1 us (0.43)
  waiting for transfers between devices: 111 us -> 20.7 us
  starting transfers between devices: 13.6 us -> 33.4 us
  Pallas kernels: 0 us -> 14.8 us
  between operations: 13.5 us -> 0.19 us
  blocking collectives: 12.7 us -> 0 us
  matrix products: 6.94 us -> 0 us
  local copies, waits for them, and re-layouts: 4.95 us -> 1.11 us
  other arithmetic: 2.61 us -> 0.65 us
    all_to_all x3 -> x0, waiting for transfers between devices: 56.8 us -> none  [the longest x1 55.6 us: local(): lax.all_to_all(sent_x, 'dp', split_axis=0, concat_axis=0, tiled=True)]
    ppermute x0 -> x16, starting transfers between devices: none -> 33.4 us  [swap(): return lax.ppermute(x, AXES, perm)]
    psum x1 -> x0, waiting for transfers between devices: 32.7 us -> none  [local(): lax.psum(partial_value.astype(jnp.bfloat16), 'tensor').astype(jnp.float32)]
    ppermute x0 -> x16, waiting for transfers between devices: none -> 20.7 us  [swap(): return lax.ppermute(x, AXES, perm)]
    all_gather x1 -> x0, waiting for transfers between devices: 20.5 us -> none  [local(): lax.all_gather(value_weight, 'dp', axis=1, tiled=True)]
    pallas_call x0 -> x9, Pallas kernels: none -> 14.8 us  [call(): pl.pallas_call(body, name=name, out_shape=outs, in_specs=specs, out_specs...]
    all_to_all x3 -> x0, starting transfers between devices: 13.5 us -> none  [the longest x1 6.32 us: local(): lax.all_to_all(wanted_hot, 'dp', split_axis=0, concat_axis=0, tiled=True)]
    psum x1 -> x0, blocking collectives: 12.7 us -> none  [local(): reduced_input = lax.psum(picked.astype(jnp.bfloat16), 'tensor')]
  transfers between devices with their start and end apart: 5 -> 16, of which waited for: 4 -> 6; matrix products, arithmetic and copies ran while one was open for 8% -> 0% of each run, Pallas kernels for 0% -> 11%
where the time goes in v3:
time: 71.1 us; the launch traced here: 70.9 us
  starting transfers between devices  33.4 us (47%)
  waiting for transfers between devices  20.7 us (29%)
  Pallas kernels  14.8 us (21%)
  local copies, waits for them, and re-layouts  1.11 us (2%)
    ppermute x16, starting transfers between devices, swap(): return lax.ppermute(x, AXES, perm)  33.4 us
    ppermute x16, waiting for transfers between devices, swap(): return lax.ppermute(x, AXES, perm)  20.7 us
    pallas_call x9, Pallas kernels, call(): pl.pallas_call(body, name=name, out_shape=outs, in_specs=specs, out_specs...  14.8 us
  transfers between devices with their start and end apart: 16, of which 6 were waited for; matrix products, arithmetic and copies ran while one was open for 0% of the time, Pallas kernels for 11%

profile of v3, /device:TPU:0, one launch (start us, length us, event | category | flops | bytes accessed | tf_op | source)
XLA Modules:
  0.0 70.9 jit_solution(17184508157978195338)
XLA Ops:
  0.0 0.6 pad_add_fusion.ints_ref
  0.7 3.1 %pack_weights.1 = (bf16[2304,128]{1,0:T(8,128)(2,1)}, bf16[1024,128]{1,0:T(8,128)(2,1)}, bf16[1024,128]{1,0:T(8,128)(2,1)}) custom-call(s32[3]{0:T(128)} %pad_add_fusion.ints_ref, bf16[2048,256]{1,0:T(8,128)(2,1)} %w_ref.1, bf16[2,64,2048]{2,1,0:T(8,128)(2,1)} %bitcast.4, bf16[2,64,256]{2,1,0:T(8,128)(2,1)} %u_ref.1), custom_call_target="tpu_custom_call" | custom-call | tf_op jit(solution)/shard_map/pack_weights/pallas_call | solution.py:19
  3.7 3.1 %collective-permute-start = (bf16[2304,128]{1,0:T(8,128)(2,1)}, bf16[2304,128]{1,0:T(8,128)(2,1)S(1)}, u32[]{:S(2)}, u32[]{:S(2)}) collective-permute-start(bf16[2304,128]{1,0:T(8,128)(2,1)} %get-tuple-element.22.own.w0), channel_id=1, source_target_pairs={{0,4},{1,5},{2,6},{3,7},{4,0},{5,1},{6,2},{7,3},{8,12},{9,13},{10,... | collective-permute-start | bytes 1769480 | tf_op jit(solution)/shard_map/ppermute | solution.py:62
  6.8 3.8 %pack_blocks.1 = (bf16[272,2048]{1,0:T(8,128)(2,1)}, bf16[2304,128]{1,0:T(8,128)(2,1)}, bf16[2304,128]{1,0:T(8,128)(2,1)}) custom-call(s32[3]{0:T(128)} %pad_add_fusion.ints_ref, s32[8]{0:T(128)} %table_ref.3, s32[4]{0:T(128)} %block_ref.3, bf16[256,2048]{1,0:T(8,128)(2,1)} %tok_ref.1, bf16[1024,128]{1,0:T(8,128)(2,1)} %get-tuple-element.28.d_ref.d0), custom_call_target="tpu_custom_call" | custom-call | tf_op jit(solution)/shard_map/pack_blocks/pallas_call | solution.py:19
  10.6 1.6 %collective-permute-start.5 = (bf16[272,2048]{1,0:T(8,128)(2,1)}, bf16[272,2048]{1,0:T(8,128)(2,1)S(1)}, u32[]{:S(2)}, u32[]{:S(2)}) collective-permute-start(bf16[272,2048]{1,0:T(8,128)(2,1)} %get-tuple-element.26.a_ref), channel_id=1, source_target_pairs={{0,16},{1,17},{2,18},{3,19},{4,20},{5,21},{6,22},{7,23},{8,24},{9,... | collective-permute-start | bytes 3342344 | tf_op jit(solution)/shard_map/ppermute | solution.py:62
  12.2 8.1 %collective-permute-done.near.w1 = bf16[2304,128]{1,0:T(8,128)(2,1)S(1)} collective-permute-done((bf16[2304,128]{1,0:T(8,128)(2,1)}, bf16[2304,128]{1,0:T(8,128)(2,1)S(1)}, u32[]{:S(2)}, u32[]{:S(2)}) %collective-permute-start) | collective-permute-done | bytes 589856 | tf_op jit(solution)/shard_map/ppermute | solution.py:62
  20.3 0.0 collective-permute-done.1.inner_ref.mid
  20.4 1.1 %copy-done.4 = bf16[2304,128]{1,0:T(8,128)(2,1)S(1)} copy-done((bf16[2304,128]{1,0:T(8,128)(2,1)S(1)}, bf16[2304,128]{1,0:T(8,128)(2,1)}, u32[]{:S(2)}) %copy-start.4) | copy-done | bytes 589848
  21.4 0.6 choose.2
  22.0 3.4 %collective-permute-start.3 = (bf16[2304,128]{1,0:T(8,128)(2,1)S(1)}, bf16[2304,128]{1,0:T(8,128)(2,1)S(1)}, u32[]{:S(2)}, u32[]{:S(2)}) collective-permute-start(bf16[2304,128]{1,0:T(8,128)(2,1)S(1)} %choose.2), channel_id=1, source_target_pairs={{0,4},{1,5},{2,6},{3,7},{4,0},{5,1},{6,2},{7,3},{8,12},{9,13},{10,... | collective-permute-start | bytes 1769480 | tf_op jit(solution)/shard_map/ppermute | solution.py:62
  25.4 0.6 choose.3
  26.0 13.0 %collective-permute-start.4 = (bf16[2304,128]{1,0:T(8,128)(2,1)S(1)}, bf16[2304,128]{1,0:T(8,128)(2,1)S(1)}, u32[]{:S(2)}, u32[]{:S(2)}) collective-permute-start(bf16[2304,128]{1,0:T(8,128)(2,1)S(1)} %choose.3), channel_id=1, source_target_pairs={{0,4},{1,5},{2,6},{3,7},{4,0},{5,1},{6,2},{7,3},{8,12},{9,13},{10,... | collective-permute-start | bytes 1769480 | tf_op jit(solution)/shard_map/ppermute | solution.py:62
  39.0 1.5 %collective-permute-start.7 = (bf16[1024,128]{1,0:T(8,128)(2,1)S(1)}, bf16[1024,128]{1,0:T(8,128)(2,1)S(1)}, u32[]{:S(2)}, u32[]{:S(2)}) collective-permute-start(bf16[1024,128]{1,0:T(8,128)(2,1)S(1)} %collective-permute-done.6.d2), channel_id=1, source_target_pairs={{0,16},{1,17},{2,18},{3,19},{4,20},{5,21},{6,22},{7,23},{8,24},{9,... | collective-permute-start | bytes 786440 | tf_op jit(solution)/shard_map/ppermute | solution.py:62
  40.5 0.0 collective-permute-done.3.out2.out.two_ref
  40.6 0.1 collective-permute-start.8
  40.7 5.1 %collective-permute-done.7.e2 = bf16[1024,128]{1,0:T(8,128)(2,1)S(1)} collective-permute-done((bf16[1024,128]{1,0:T(8,128)(2,1)S(1)}, bf16[1024,128]{1,0:T(8,128)(2,1)S(1)}, u32[]{:S(2)}, u32[]{:S(2)}) %collective-permute-start.7) | collective-permute-done | bytes 262176 | tf_op jit(solution)/shard_map/ppermute | solution.py:62
  45.8 1.5 %collective-permute-start.9 = (bf16[1024,128]{1,0:T(8,128)(2,1)S(1)}, bf16[1024,128]{1,0:T(8,128)(2,1)S(1)}, u32[]{:S(2)}, u32[]{:S(2)}) collective-permute-start(bf16[1024,128]{1,0:T(8,128)(2,1)S(1)} %collective-permute-done.8.d3), channel_id=1, source_target_pairs={{0,16},{1,17},{2,18},{3,19},{4,20},{5,21},{6,22},{7,23},{8,24},{9,... | collective-permute-start | bytes 786440 | tf_op jit(solution)/shard_map/ppermute | solution.py:62
  47.3 2.5 %early_columns.1.part_ref = f32[1536,128]{1,0:T(8,128)S(1)} custom-call(s32[3]{0:T(128)S(1)} %copy-done.6, bf16[272,2048]{1,0:T(8,128)(2,1)S(1)} %copy-done, bf16[272,2048]{1,0:T(8,128)(2,1)S(1)} %collective-permute-done.5.b_ref, bf16[2304,128]{1,0:T(8,128)(2,1)S(1)} %copy-done.1, bf16[2304,128]{1,0:T(8,128)(2,1)S(1)} %collective-permute-done.near.w1, ...), custom_call_target="tpu_custom_call" | custom-call | tf_op jit(solution)/shard_map/early_columns/pallas_call | solution.py:19
  49.8 2.3 %collective-permute-done.9.e3 = bf16[1024,128]{1,0:T(8,128)(2,1)S(1)} collective-permute-done((bf16[1024,128]{1,0:T(8,128)(2,1)S(1)}, bf16[1024,128]{1,0:T(8,128)(2,1)S(1)}, u32[]{:S(2)}, u32[]{:S(2)}) %collective-permute-start.9) | collective-permute-done | bytes 262176 | tf_op jit(solution)/shard_map/ppermute | solution.py:62
  52.2 0.0 collective-permute-done.4.out3.three_ref
  52.2 1.7 %late_columns.1 = (f32[1408,128]{1,0:T(8,128)S(1)}, bf16[1408,128]{1,0:T(8,128)(2,1)S(1)}) custom-call(s32[3]{0:T(128)S(1)} %copy-done.6, bf16[272,2048]{1,0:T(8,128)(2,1)S(1)} %copy-done, bf16[272,2048]{1,0:T(8,128)(2,1)S(1)} %collective-permute-done.5.b_ref, bf16[2304,128]{1,0:T(8,128)(2,1)S(1)} %collective-permute-done.3.out2.out.two_ref, ...), custom_call_target="tpu_custom_call" | custom-call | tf_op jit(solution)/shard_map/late_columns/pallas_call | solution.py:19
  53.9 0.1 collective-permute-start.10
  53.9 1.7 %collective-permute-done.10.came_ref = bf16[1408,128]{1,0:T(8,128)(2,1)S(1)} collective-permute-done((bf16[1408,128]{1,0:T(8,128)(2,1)S(1)}, bf16[1408,128]{1,0:T(8,128)(2,1)S(1)}, u32[]{:S(2)}, u32[]{:S(2)}) %collective-permute-start.10) | collective-permute-done | bytes 360480 | tf_op jit(solution)/shard_map/ppermute | solution.py:62
  55.6 0.6 add_cores.1
  56.2 1.6 %collective-permute-start.11 = (bf16[384,128]{1,0:T(8,128)(2,1)S(1)}, bf16[384,128]{1,0:T(8,128)(2,1)S(1)}, u32[]{:S(2)}, u32[]{:S(2)}) collective-permute-start(bf16[384,128]{1,0:T(8,128)(2,1)S(1)} %get-tuple-element.35), channel_id=1, source_target_pairs={{0,2},{1,3},{2,0},{3,1},{4,6},{5,7},{6,4},{7,5},{8,10},{9,11},{10,... | collective-permute-start | bytes 294920 | tf_op jit(solution)/shard_map/ppermute | solution.py:62
  57.8 1.5 %collective-permute-start.12 = (bf16[384,128]{1,0:T(8,128)(2,1)S(1)}, bf16[384,128]{1,0:T(8,128)(2,1)S(1)}, u32[]{:S(2)}, u32[]{:S(2)}) collective-permute-start(bf16[384,128]{1,0:T(8,128)(2,1)S(1)} %get-tuple-element.36), channel_id=1, source_target_pairs={{0,16},{1,17},{2,18},{3,19},{4,20},{5,21},{6,22},{7,23},{8,24},{9,... | collective-permute-start | bytes 294920 | tf_op jit(solution)/shard_map/ppermute | solution.py:62
  59.3 0.5 collective-permute-start.13
  59.8 5.7 %collective-permute-start.15 = (bf16[128,128]{1,0:T(8,128)(2,1)S(1)}, bf16[128,128]{1,0:T(8,128)(2,1)S(1)}, u32[]{:S(2)}, u32[]{:S(2)}) collective-permute-start(bf16[128,128]{1,0:T(8,128)(2,1)S(1)} %get-tuple-element.38), channel_id=1, source_target_pairs={{0,6},{1,7},{2,4},{3,5},{4,2},{5,3},{6,0},{7,1},{8,14},{9,15},{10,... | collective-permute-start | bytes 98312 | tf_op jit(solution)/shard_map/ppermute | solution.py:62
  65.4 0.6 ups.1.up_ref
  66.0 1.6 %collective-permute-done.15.nx_ref = bf16[128,128]{1,0:T(8,128)(2,1)S(1)} collective-permute-done((bf16[128,128]{1,0:T(8,128)(2,1)S(1)}, bf16[128,128]{1,0:T(8,128)(2,1)S(1)}, u32[]{:S(2)}, u32[]{:S(2)}) %collective-permute-start.15) | collective-permute-done | bytes 32800 | tf_op jit(solution)/shard_map/ppermute | solution.py:62
  67.6 1.7 %collective-permute-done.14.n_ref = bf16[128,128]{1,0:T(8,128)(2,1)S(1)} collective-permute-done((bf16[128,128]{1,0:T(8,128)(2,1)S(1)}, bf16[128,128]{1,0:T(8,128)(2,1)S(1)}, u32[]{:S(2)}, u32[]{:S(2)}) %collective-permute-start.14) | collective-permute-done | bytes 32800 | tf_op jit(solution)/shard_map/ppermute | solution.py:62
  69.4 1.5 %finish.1 = bf16[256,256]{1,0:T(8,128)(2,1)} custom-call(s32[3]{0:T(128)S(1)} %copy-done.6, s32[8]{0:T(128)S(1)} %copy-done.7, s32[4]{0:T(128)S(1)} %copy-done.8, s32[4]{0:T(128)S(1)} %copy-done.9, bf16[4,256,128]{2,1,0:T(8,128)(2,1)S(1)} %ups.1.up_ref, f32[384,128]{1,0:T(8,128)S(1)} %get-tuple-element.34.mine_ref, ...), custom_call_target="tpu_custom_call" | custom-call | tf_op jit(solution)/shard_map/finish/pallas_call | solution.py:19
  (31 shorter events, 0.1 us)
Async XLA Ops:
  0.6 19.7 %copy-start.6 = (s32[3]{0:T(128)S(1)}, s32[3]{0:T(128)}, u32[]{:S(2)}) copy-start(s32[3]{0:T(128)} %pad_add_fusion.ints_ref) | copy-start | bytes 40
  3.7 16.6 %collective-permute-start = (bf16[2304,128]{1,0:T(8,128)(2,1)}, bf16[2304,128]{1,0:T(8,128)(2,1)S(1)}, u32[]{:S(2)}, u32[]{:S(2)}) collective-permute-start(bf16[2304,128]{1,0:T(8,128)(2,1)} %get-tuple-element.22.own.w0), channel_id=1, source_target_pairs={{0,4},{1,5},{2,6},{3,7},{4,0},{5,1},{6,2},{7,3},{8,12},{9,13},{10,... | collective-permute-start | bytes 1769480 | tf_op jit(solution)/shard_map/ppermute | solution.py:62
  6.8 13.5 %collective-permute-start.1 = (bf16[2304,128]{1,0:T(8,128)(2,1)}, bf16[2304,128]{1,0:T(8,128)(2,1)S(1)}, u32[]{:S(2)}, u32[]{:S(2)}) collective-permute-start(bf16[2304,128]{1,0:T(8,128)(2,1)} %get-tuple-element.22.own.w0), channel_id=1, source_target_pairs={{0,1},{1,0},{2,3},{3,2},{4,8},{5,9},{6,10},{7,11},{8,4},{9,5},{10,... | collective-permute-start | bytes 1769480 | tf_op jit(solution)/shard_map/ppermute | solution.py:62
  10.6 14.8 %copy-start.2 = (bf16[1024,128]{1,0:T(8,128)(2,1)S(1)}, bf16[1024,128]{1,0:T(8,128)(2,1)}, u32[]{:S(2)}) copy-start(bf16[1024,128]{1,0:T(8,128)(2,1)} %get-tuple-element.28.d_ref.d0) | copy-start | bytes 786436
  10.6 14.8 %copy-start.3 = (bf16[2304,128]{1,0:T(8,128)(2,1)S(1)}, bf16[2304,128]{1,0:T(8,128)(2,1)}, u32[]{:S(2)}) copy-start(bf16[2304,128]{1,0:T(8,128)(2,1)} %get-tuple-element.25.outer_ref) | copy-start | bytes 1769476
  10.6 28.4 %collective-permute-start.5 = (bf16[272,2048]{1,0:T(8,128)(2,1)}, bf16[272,2048]{1,0:T(8,128)(2,1)S(1)}, u32[]{:S(2)}, u32[]{:S(2)}) collective-permute-start(bf16[272,2048]{1,0:T(8,128)(2,1)} %get-tuple-element.26.a_ref), channel_id=1, source_target_pairs={{0,16},{1,17},{2,18},{3,19},{4,20},{5,21},{6,22},{7,23},{8,24},{9,... | collective-permute-start | bytes 3342344 | tf_op jit(solution)/shard_map/ppermute | solution.py:62
  20.3 5.1 %collective-permute-start.2 = (bf16[2304,128]{1,0:T(8,128)(2,1)S(1)}, bf16[2304,128]{1,0:T(8,128)(2,1)S(1)}, u32[]{:S(2)}, u32[]{:S(2)}) collective-permute-start(bf16[2304,128]{1,0:T(8,128)(2,1)S(1)} %collective-permute-done.near.w1), channel_id=1, source_target_pairs={{0,1},{1,0},{2,3},{3,2},{4,8},{5,9},{6,10},{7,11},{8,4},{9,5},{10,... | collective-permute-start | bytes 1769480 | tf_op jit(solution)/shard_map/ppermute | solution.py:62
  20.4 1.1 %copy-start.4 = (bf16[2304,128]{1,0:T(8,128)(2,1)S(1)}, bf16[2304,128]{1,0:T(8,128)(2,1)}, u32[]{:S(2)}) copy-start(bf16[2304,128]{1,0:T(8,128)(2,1)} %get-tuple-element.24.outer_ref) | copy-start | bytes 1769476
  22.0 18.5 %collective-permute-start.3 = (bf16[2304,128]{1,0:T(8,128)(2,1)S(1)}, bf16[2304,128]{1,0:T(8,128)(2,1)S(1)}, u32[]{:S(2)}, u32[]{:S(2)}) collective-permute-start(bf16[2304,128]{1,0:T(8,128)(2,1)S(1)} %choose.2), channel_id=1, source_target_pairs={{0,4},{1,5},{2,6},{3,7},{4,0},{5,1},{6,2},{7,3},{8,12},{9,13},{10,... | collective-permute-start | bytes 1769480 | tf_op jit(solution)/shard_map/ppermute | solution.py:62
  25.4 13.6 %collective-permute-start.6 = (bf16[1024,128]{1,0:T(8,128)(2,1)S(1)}, bf16[1024,128]{1,0:T(8,128)(2,1)S(1)}, u32[]{:S(2)}, u32[]{:S(2)}) collective-permute-start(bf16[1024,128]{1,0:T(8,128)(2,1)S(1)} %copy-done.2), channel_id=1, source_target_pairs={{0,1},{1,0},{2,3},{3,2},{4,8},{5,9},{6,10},{7,11},{8,4},{9,5},{10,... | collective-permute-start | bytes 786440 | tf_op jit(solution)/shard_map/ppermute | solution.py:62
  25.4 21.9 %copy-start = (bf16[272,2048]{1,0:T(8,128)(2,1)S(1)}, bf16[272,2048]{1,0:T(8,128)(2,1)}, u32[]{:S(2)}) copy-start(bf16[272,2048]{1,0:T(8,128)(2,1)} %get-tuple-element.26.a_ref) | copy-start | bytes 3342340
  25.4 21.9 %copy-start.1 = (bf16[2304,128]{1,0:T(8,128)(2,1)S(1)}, bf16[2304,128]{1,0:T(8,128)(2,1)}, u32[]{:S(2)}) copy-start(bf16[2304,128]{1,0:T(8,128)(2,1)} %get-tuple-element.22.own.w0) | copy-start | bytes 1769476
  26.0 26.2 %collective-permute-start.4 = (bf16[2304,128]{1,0:T(8,128)(2,1)S(1)}, bf16[2304,128]{1,0:T(8,128)(2,1)S(1)}, u32[]{:S(2)}, u32[]{:S(2)}) collective-permute-start(bf16[2304,128]{1,0:T(8,128)(2,1)S(1)} %choose.3), channel_id=1, source_target_pairs={{0,4},{1,5},{2,6},{3,7},{4,0},{5,1},{6,2},{7,3},{8,12},{9,13},{10,... | collective-permute-start | bytes 1769480 | tf_op jit(solution)/shard_map/ppermute | solution.py:62
  39.0 6.8 %collective-permute-start.7 = (bf16[1024,128]{1,0:T(8,128)(2,1)S(1)}, bf16[1024,128]{1,0:T(8,128)(2,1)S(1)}, u32[]{:S(2)}, u32[]{:S(2)}) collective-permute-start(bf16[1024,128]{1,0:T(8,128)(2,1)S(1)} %collective-permute-done.6.d2), channel_id=1, source_target_pairs={{0,16},{1,17},{2,18},{3,19},{4,20},{5,21},{6,22},{7,23},{8,24},{9,... | collective-permute-start | bytes 786440 | tf_op jit(solution)/shard_map/ppermute | solution.py:62
  40.6 11.6 %copy-start.5 = (bf16[1024,128]{1,0:T(8,128)(2,1)S(1)}, bf16[1024,128]{1,0:T(8,128)(2,1)}, u32[]{:S(2)}) copy-start(bf16[1024,128]{1,0:T(8,128)(2,1)} %get-tuple-element.27.e0) | copy-start | bytes 786436
  40.6 5.2 %collective-permute-start.8 = (bf16[1024,128]{1,0:T(8,128)(2,1)S(1)}, bf16[1024,128]{1,0:T(8,128)(2,1)S(1)}, u32[]{:S(2)}, u32[]{:S(2)}) collective-permute-start(bf16[1024,128]{1,0:T(8,128)(2,1)S(1)} %slice.4), channel_id=1, source_target_pairs={{0,1},{1,0},{2,3},{3,2},{4,8},{5,9},{6,10},{7,11},{8,4},{9,5},{10,... | collective-permute-start | bytes 786440 | tf_op jit(solution)/shard_map/ppermute | solution.py:62
  45.8 6.4 %collective-permute-start.9 = (bf16[1024,128]{1,0:T(8,128)(2,1)S(1)}, bf16[1024,128]{1,0:T(8,128)(2,1)S(1)}, u32[]{:S(2)}, u32[]{:S(2)}) collective-permute-start(bf16[1024,128]{1,0:T(8,128)(2,1)S(1)} %collective-permute-done.8.d3), channel_id=1, source_target_pairs={{0,16},{1,17},{2,18},{3,19},{4,20},{5,21},{6,22},{7,23},{8,24},{9,... | collective-permute-start | bytes 786440 | tf_op jit(solution)/shard_map/ppermute | solution.py:62
  53.9 1.7 %collective-permute-start.10 = (bf16[1408,128]{1,0:T(8,128)(2,1)S(1)}, bf16[1408,128]{1,0:T(8,128)(2,1)S(1)}, u32[]{:S(2)}, u32[]{:S(2)}) collective-permute-start(bf16[1408,128]{1,0:T(8,128)(2,1)S(1)} %get-tuple-element.33), channel_id=1, source_target_pairs={{0,1},{1,0},{2,3},{3,2},{4,5},{5,4},{6,7},{7,6},{8,9},{9,8},{10,11... | collective-permute-start | bytes 1081352 | tf_op jit(solution)/shard_map/ppermute | solution.py:62
  56.2 13.1 %collective-permute-start.11 = (bf16[384,128]{1,0:T(8,128)(2,1)S(1)}, bf16[384,128]{1,0:T(8,128)(2,1)S(1)}, u32[]{:S(2)}, u32[]{:S(2)}) collective-permute-start(bf16[384,128]{1,0:T(8,128)(2,1)S(1)} %get-tuple-element.35), channel_id=1, source_target_pairs={{0,2},{1,3},{2,0},{3,1},{4,6},{5,7},{6,4},{7,5},{8,10},{9,11},{10,... | collective-permute-start | bytes 294920 | tf_op jit(solution)/shard_map/ppermute | solution.py:62
  57.8 11.6 %collective-permute-start.12 = (bf16[384,128]{1,0:T(8,128)(2,1)S(1)}, bf16[384,128]{1,0:T(8,128)(2,1)S(1)}, u32[]{:S(2)}, u32[]{:S(2)}) collective-permute-start(bf16[384,128]{1,0:T(8,128)(2,1)S(1)} %get-tuple-element.36), channel_id=1, source_target_pairs={{0,16},{1,17},{2,18},{3,19},{4,20},{5,21},{6,22},{7,23},{8,24},{9,... | collective-permute-start | bytes 294920 | tf_op jit(solution)/shard_map/ppermute | solution.py:62
  59.3 10.1 %collective-permute-start.13 = (bf16[384,128]{1,0:T(8,128)(2,1)S(1)}, bf16[384,128]{1,0:T(8,128)(2,1)S(1)}, u32[]{:S(2)}, u32[]{:S(2)}) collective-permute-start(bf16[384,128]{1,0:T(8,128)(2,1)S(1)} %get-tuple-element.37), channel_id=1, source_target_pairs={{0,18},{1,19},{2,16},{3,17},{4,22},{5,23},{6,20},{7,21},{8,26},{9,... | collective-permute-start | bytes 294920 | tf_op jit(solution)/shard_map/ppermute | solution.py:62
  59.8 9.6 %copy-start.7 = (s32[8]{0:T(128)S(1)}, s32[8]{0:T(128)}, u32[]{:S(2)}) copy-start(s32[8]{0:T(128)} %table_ref.3) | copy-start | bytes 100
  59.8 9.6 %copy-start.8 = (s32[4]{0:T(128)S(1)}, s32[4]{0:T(128)}, u32[]{:S(2)}) copy-start(s32[4]{0:T(128)} %block_ref.3) | copy-start | bytes 52
  59.8 9.6 %copy-start.9 = (s32[4]{0:T(128)S(1)}, s32[4]{0:T(128)}, u32[]{:S(2)}) copy-start(s32[4]{0:T(128)} %live_ref.1) | copy-start | bytes 52
  59.8 7.9 %collective-permute-start.15 = (bf16[128,128]{1,0:T(8,128)(2,1)S(1)}, bf16[128,128]{1,0:T(8,128)(2,1)S(1)}, u32[]{:S(2)}, u32[]{:S(2)}) collective-permute-start(bf16[128,128]{1,0:T(8,128)(2,1)S(1)} %get-tuple-element.38), channel_id=1, source_target_pairs={{0,6},{1,7},{2,4},{3,5},{4,2},{5,3},{6,0},{7,1},{8,14},{9,15},{10,... | collective-permute-start | bytes 98312 | tf_op jit(solution)/shard_map/ppermute | solution.py:62
  65.4 3.9 %collective-permute-start.14 = (bf16[128,128]{1,0:T(8,128)(2,1)S(1)}, bf16[128,128]{1,0:T(8,128)(2,1)S(1)}, u32[]{:S(2)}, u32[]{:S(2)}) collective-permute-start(bf16[128,128]{1,0:T(8,128)(2,1)S(1)} %get-tuple-element.38), channel_id=1, source_target_pairs={{0,4},{1,5},{2,6},{3,7},{4,0},{5,1},{6,2},{7,3},{8,12},{9,13},{10,... | collective-permute-start | bytes 98312 | tf_op jit(solution)/shard_map/ppermute | solution.py:62

commit v4 on v3

--- a/solution.py
+++ b/solution.py
@@ -47,7 +47,6 @@
     pairs = dp // 2
     both = groups * rows
     s_msg = rows // 2
-    total = pairs * both + 3 * s_msg
 
     def device(a, b, c):
         return (a * dp + b) * tensor + c
@@ -95,13 +94,11 @@
             local_slot = jnp.where(hit, s % per_dev, local_slot)
         return which, local_slot
 
-    def pack(ints_ref, w_ref, d_ref, u_ref, wide_ref, own_ref, other_ref, d_held, sems):
+    def pack_columns(ints_ref, w_ref, u_ref, wide_ref, sems):
         me = ints_ref[0]
         cols = pl.ds(pl.multiple_of(me * half_cols, LANES), half_cols)
         copies = [
-            pltpu.make_async_copy(d_ref.at[me], d_held.at[0], sems.at[0]),
-            pltpu.make_async_copy(d_ref.at[1 - me], d_held.at[1], sems.at[1]),
-            pltpu.make_async_copy(w_ref.at[:, cols], wide_ref.at[pl.ds(0, feats)], sems.at[2]),
+            pltpu.make_async_copy(w_ref.at[:, cols], wide_ref.at[pl.ds(0, feats)], sems.at[0]),
         ]
         for s in range(per_dev):
             for v in range(col_tiles):
@@ -110,28 +107,22 @@
                     pltpu.make_async_copy(
                         u_ref.at[s, :, pl.ds(v * LANES, LANES)],
                         wide_ref.at[pl.ds(feats + n * rank, rank)],
-                        sems.at[3 + n],
+                        sems.at[1 + n],
                     )
                 )
         for c in copies:
             c.start()
-        for n, ref in ((0, own_ref), (1, other_ref)):
-            copies[n].wait()
-            ref[...] = jnp.concatenate([d_held[n, :, 0:half], d_held[n, :, half:feats]], axis=0).T
-        for c in copies[2:]:
+        for c in copies:
             c.wait()
 
-    own_w, own_d, own_e = call(
-        pack,
-        "pack_weights",
-        (like(feats + up_rows, LANES), like(half, LANES), like(half, LANES)),
-        [SMEM, HBM, HBM, HBM],
-        (place, value_weight, jnp.transpose(down, (0, 2, 1)), up),
-        [
-            pltpu.VMEM((per_dev, rank, feats), BF16),
-            pltpu.SemaphoreType.DMA((3 + per_dev * col_tiles,)),
-        ],
-        mib=56,
+    own_w = call(
+        pack_columns,
+        "pack_columns",
+        like(feats + up_rows, LANES),
+        [SMEM, HBM, HBM],
+        (place, value_weight, up),
+        [pltpu.SemaphoreType.DMA((1 + per_dev * col_tiles,))],
+        mib=16,
     )
 
     tiles = feats // LANES
@@ -139,9 +130,7 @@
     wide_rows = feats + up_rows
     code_at = half + tile_rows
 
-    def pack_tokens(
-        ints_ref, table_ref, block_ref, tok_ref, d_ref, sorted_ref, first_ref, second_ref, sems
-    ):
+    def sort_blocks(ints_ref, table_ref, block_ref, tok_ref, sorted_ref, sems):
         here = ints_ref[1]
         copies = []
         row = lax.broadcasted_iota(jnp.int32, (CODE_ROWS, LANES), 0)
@@ -153,30 +142,39 @@
             copies.append(pltpu.make_async_copy(src, to, sems.at[slot]))
             copies[-1].start()
             code = jnp.where(row == slot, local_slot, code)
-        code = code.astype(F32).astype(BF16)
-        sorted_ref[rows:, 0:LANES] = code
-        first_ref[code_at : code_at + CODE_ROWS, :] = code
-        first_ref[0:half, :] = d_ref[...]
+        sorted_ref[rows:, 0:LANES] = code.astype(F32).astype(BF16)
         for c in copies:
             c.wait()
+
+    in_order = call(
+        sort_blocks,
+        "sort_blocks",
+        like(rows + CODE_ROWS, feats),
+        [SMEM, SMEM, SMEM, HBM],
+        (place, slot_table, per_block, tokens),
+        [pltpu.SemaphoreType.DMA((dp,))],
+        mib=16,
+    )
+
+    def pack_shrinks(ints_ref, sorted_ref, d_ref, own_ref, other_ref, first_ref, second_ref):
+        me = ints_ref[0]
+        for which, ref in ((me, own_ref), (1 - me, other_ref)):
+            d = d_ref[which]
+            ref[...] = jnp.concatenate([d[:, 0:half], d[:, half:feats]], axis=0).T
+        first_ref[0:half, :] = own_ref[...]
+        first_ref[code_at : code_at + CODE_ROWS, :] = sorted_ref[rows:, 0:LANES]
         for n, (ref, at) in enumerate(((first_ref, half), (second_ref, 0), (second_ref, tile_rows))):
             for i in range(tiles):
                 ref[at + i * block_len : at + (i + 1) * block_len, :] = sorted_ref[
                     (n + 1) * block_len : (n + 2) * block_len, i * LANES : (i + 1) * LANES
                 ]
 
-    in_order, first, second = call(
-        pack_tokens,
-        "pack_blocks",
-        (
-            like(rows + CODE_ROWS, feats),
-            like(wide_rows, LANES),
-            like(wide_rows, LANES),
-        ),
-        [SMEM, SMEM, SMEM, HBM, VMEM],
-        (place, slot_table, per_block, tokens, own_d),
-        [pltpu.SemaphoreType.DMA((dp,))],
-        mib=56,
+    own_d, own_e, first, second = call(
+        pack_shrinks,
+        "pack_shrinks",
+        (like(half, LANES), like(half, LANES), like(wide_rows, LANES), like(wide_rows, LANES)),
+        [SMEM, VMEM, VMEM],
+        (place, in_order, jnp.transpose(down, (0, 2, 1))),
     )
 
     def choose(ints_ref, outer_ref, inner_ref, out_ref):
@@ -201,7 +199,7 @@
     mid_d = to_middle(tie(own_d, near_w))
     three = to_neighbour(chosen(second, far_w))
     mid_e = to_group(tie(mid_d, others))
-    far_d = to_middle(tie(two[0:half], mid_d))
+    far_d = to_middle(two[0:half])
     far_e = to_group(tie(far_d, mid_e))
 
     def columns(a_ref, b_ref, w_ref, out_ref, at):
@@ -210,50 +208,18 @@
                 x[0:rows, :], w_ref[0:feats, :], preferred_element_type=F32
             )
 
-    def early(ints_ref, a_ref, b_ref, w0, w1, mid, out, part_ref):
-        columns(a_ref, b_ref, w0, part_ref, 0)
-        columns(a_ref, b_ref, w1, part_ref, both)
-        is_outer = outer_plane(ints_ref[1])
-        pl.when(is_outer)(lambda: columns(a_ref, b_ref, out, part_ref, 2 * both))
-        pl.when(jnp.logical_not(is_outer))(lambda: columns(a_ref, b_ref, mid, part_ref, 2 * both))
-
-    part = call(
-        early,
-        "early_columns",
-        like(3 * both, LANES, F32),
-        [SMEM] + [VMEM] * 6,
-        (place, in_order, others, own_w, near_w, mid_w, two),
-    )
-
-    def late(
-        ints_ref, a_ref, b_ref, two_ref, three_ref, d0, e0, d2, e2, d3, e3,
-        far, part_ref, keep, away, last_ref, s_ref,
-    ):
-        me, here, core = ints_ref[0], ints_ref[1], ints_ref[2] % 2
-        is_outer = outer_plane(here)
-
-        def put(ref, ref_at, holder):
-            at = pl.ds(pl.multiple_of((holder // 2) * both, both), both)
-
-            @pl.when(holder % 2 == core)
-            def _():
-                keep[at, :] = ref[ref_at : ref_at + both, :]
-
-            @pl.when(holder % 2 != core)
-            def _():
-                away[at, :] = ref[ref_at : ref_at + both, :].astype(BF16)
-
+    def shrinker(me, a_ref, b_ref, two_ref, three_ref, s_ref):
         number = me.astype(F32)
         codes = [ref[rows:, 0:LANES].astype(F32) for ref in (a_ref, b_ref)]
         near_codes = two_ref[code_at : code_at + CODE_ROWS, :].astype(F32)
-        s_ref[...] = jnp.zeros_like(s_ref)
 
         def shrink(slot, d_ref, e_ref=None, theirs=0):
             at = slice(slot * block_len, (slot + 1) * block_len)
             x = [a_ref[at, :], b_ref[at, :]]
             rhs = d_ref[0:half, :]
             if theirs:
-                ref, near_at = ((two_ref, half), (three_ref, 0), (three_ref, tile_rows))[theirs - 1]
+                ref = two_ref if theirs == 1 else three_ref
+                near_at = (half, 0, tile_rows)[theirs - 1]
                 x.append(
                     jnp.concatenate(
                         [
@@ -281,42 +247,93 @@
                     hit, mine[last, :], other
                 )
 
+        return shrink
+
+    def early(ints_ref, a_ref, b_ref, w0, w1, mid, two_ref, d0, e0, part_ref, s_ref):
+        columns(a_ref, b_ref, w0, part_ref, 0)
+        columns(a_ref, b_ref, w1, part_ref, both)
+        is_outer = outer_plane(ints_ref[1])
+        shrink = shrinker(ints_ref[0], a_ref, b_ref, two_ref, None, s_ref)
+        s_ref[...] = jnp.zeros_like(s_ref)
+
         @pl.when(is_outer)
         def _():
-            columns(a_ref, b_ref, three_ref, last_ref, 0)
+            columns(a_ref, b_ref, two_ref, part_ref, 2 * both)
             shrink(0, d0)
 
         @pl.when(jnp.logical_not(is_outer))
         def _():
-            columns(a_ref, b_ref, far, last_ref, 0)
+            columns(a_ref, b_ref, mid, part_ref, 2 * both)
             shrink(0, d0, e0, 1)
             shrink(1, two_ref)
-            shrink(2, d2, e2, 2)
-            shrink(3, d3, e3, 3)
-
+
+    s_shape = jax.ShapeDtypeStruct((3, rows, rank), F32)
+    part, shrunk = call(
+        early,
+        "early_columns",
+        (like(3 * both, LANES, F32), s_shape),
+        [SMEM] + [VMEM] * 8,
+        (place, in_order, others, own_w, near_w, mid_w, two, own_d, own_e),
+    )
+
+    def last_columns(ints_ref, a_ref, b_ref, three_ref, far, part_ref, keep, away, last_ref):
+        here, core = ints_ref[1], ints_ref[2] % 2
+        is_outer = outer_plane(here)
+
+        def put(ref, ref_at, holder):
+            at = pl.ds(pl.multiple_of((holder // 2) * both, both), both)
+
+            @pl.when(holder % 2 == core)
+            def _():
+                keep[at, :] = ref[ref_at : ref_at + both, :]
+
+            @pl.when(holder % 2 != core)
+            def _():
+                away[at, :] = ref[ref_at : ref_at + both, :].astype(BF16)
+
+        pl.when(is_outer)(lambda: columns(a_ref, b_ref, three_ref, last_ref, 0))
+        pl.when(jnp.logical_not(is_outer))(lambda: columns(a_ref, b_ref, far, last_ref, 0))
         for slot in range(3):
             put(part_ref, slot * both, where_from(here, slot))
         put(last_ref, 0, where_from(here, 3))
+
+    keep, away = call(
+        last_columns,
+        "last_columns",
+        (like(pairs * both, LANES, F32), like(pairs * both, LANES)),
+        [SMEM] + [VMEM] * 5,
+        (place, in_order, others, three, far_w, part),
+        [pltpu.VMEM((both, LANES), F32)],
+    )
+    came = swap(away, lambda a, b, c: (a, b, c ^ 1))
+
+    def last_shrinks(ints_ref, a_ref, b_ref, two_ref, three_ref, d2, e2, d3, e3, s_in, keep, away, s_ref):
+        shrink = shrinker(ints_ref[0], a_ref, b_ref, two_ref, three_ref, s_ref)
+        s_ref[...] = s_in[...]
+
+        @pl.when(jnp.logical_not(outer_plane(ints_ref[1])))
+        def _():
+            shrink(2, d2, e2, 2)
+            shrink(3, d3, e3, 3)
+
         for g in range(3):
             s = jnp.concatenate([s_ref[g, 0:s_msg, :], s_ref[g, s_msg:rows, :]], axis=1)
-            at = pairs * both + g * s_msg
-            keep[at : at + s_msg, :] = s
-            away[at : at + s_msg, :] = s.astype(BF16)
-
-    keep, away = call(
-        late,
-        "late_columns",
-        (like(total, LANES, F32), like(total, LANES)),
-        [SMEM] + [VMEM] * 12,
-        (
-            place, in_order, others, two, three, own_d, own_e, mid_d, mid_e,
-            far_d, far_e, far_w, part,
-        ),
-        [pltpu.VMEM((both, LANES), F32), pltpu.VMEM((3, rows, rank), F32)],
-    )
-    came = swap(away, lambda a, b, c: (a, b, c ^ 1))
-
-    def add_cores(ints_ref, keep_ref, came_ref, mine_out, x_out, y_out, d_out, near_out):
+            keep[g * s_msg : (g + 1) * s_msg, :] = s
+            away[g * s_msg : (g + 1) * s_msg, :] = s.astype(BF16)
+
+    s_keep, s_away = call(
+        last_shrinks,
+        "last_shrinks",
+        (like(3 * s_msg, LANES, F32), like(3 * s_msg, LANES)),
+        [SMEM] + [VMEM] * 9,
+        (place, in_order, others, two, three, mid_d, mid_e, far_d, far_e, shrunk),
+        [pltpu.VMEM((3, rows, rank), F32)],
+    )
+    s_came = swap(s_away, lambda a, b, c: (a, b, c ^ 1))
+
+    def add_cores(
+        ints_ref, keep_ref, came_ref, s_keep, s_came, mine_out, x_out, y_out, d_out, near_out,
+    ):
         side = ints_ref[2] // 2
 
         def tile(out, side_at, g):
@@ -324,8 +341,8 @@
             out[0:rows, :] = (keep_ref[at, :] + came_ref[at, :].astype(F32)).astype(out.dtype)
 
         def low_rank(out, at, g):
-            s = pl.ds(pairs * both + g * s_msg, s_msg)
-            out[at : at + s_msg, :] = (keep_ref[s, :] + came_ref[s, :].astype(F32)).astype(out.dtype)
+            s = pl.ds(g * s_msg, s_msg)
+            out[at : at + s_msg, :] = (s_keep[s, :] + s_came[s, :].astype(F32)).astype(out.dtype)
 
         tile(mine_out, side, 0)
         tile(x_out, 1 - side, 0)
@@ -347,8 +364,8 @@
             like(rows + s_msg, LANES),
             like(s_msg, LANES),
         ),
-        [SMEM, VMEM, VMEM],
-        (place, keep, came),
+        [SMEM] + [VMEM] * 4,
+        (place, keep, came, s_keep, s_came),
     )
     from_d = swap(to_d, lambda a, b, c: (1 - a, b, c ^ 2))
     from_nearx = swap(to_near, lambda a, b, c: (a, b ^ 1, c ^ 2))

time: 71.1 us -> 68.6 us (0.965)
  Pallas kernels: 14.8 us -> 10.9 us
  starting transfers between devices: 33.4 us -> 34.4 us
  local copies, waits for them, and re-layouts: 1.11 us -> 2.1 us
    pallas_call x9 -> x11, Pallas kernels: 14.8 us -> 10.9 us  [call(): pl.pallas_call(body, name=name, out_shape=outs, in_specs=specs, out_specs...]
    ppermute x16 -> x17, starting transfers between devices: 33.4 us -> 34.4 us  [swap(): return lax.ppermute(x, AXES, perm)]
    unnamed x20 -> x14, local copies, waits for them, and re-layouts: 1.09 us -> 2.09 us
    ppermute x16 -> x17, waiting for transfers between devices: 20.7 us -> 20.7 us  [swap(): return lax.ppermute(x, AXES, perm)]
  transfers between devices with their start and end apart: 16 -> 17, of which waited for: 6 -> 6; matrix products, arithmetic and copies ran while one was open for 0% -> 0% of each run, Pallas kernels for 11% -> 12%
where the time goes in v4:
time: 68.6 us; the launch traced here: 68.4 us
  starting transfers between devices  34.4 us (50%)
  waiting for transfers between devices  20.7 us (30%)
  Pallas kernels  10.9 us (16%)
  local copies, waits for them, and re-layouts  2.1 us (3%)
    ppermute x17, starting transfers between devices, swap(): return lax.ppermute(x, AXES, perm)  34.4 us
    ppermute x17, waiting for transfers between devices, swap(): return lax.ppermute(x, AXES, perm)  20.7 us
    pallas_call x11, Pallas kernels, call(): pl.pallas_call(body, name=name, out_shape=outs, in_specs=specs, out_specs...  10.9 us
    unnamed x14, local copies, waits for them, and re-layouts  2.09 us
  transfers between devices with their start and end apart: 17, of which 6 were waited for; matrix products, arithmetic and copies ran while one was open for 0% of the time, Pallas kernels for 12%

profile of v4, /device:TPU:0, one launch (start us, length us, event | category | flops | bytes accessed | tf_op | source)
XLA Modules:
  0.0 68.4 jit_solution(16165226847197074399)
XLA Ops:
  0.0 0.1 pad_add_fusion.ints_ref
  0.1 1.2 %copy-done = bf16[2048,256]{1,0:T(8,128)(2,1)S(1)} copy-done((bf16[2048,256]{1,0:T(8,128)(2,1)S(1)}, bf16[2048,256]{1,0:T(8,128)(2,1)}, u32[]{:S(2)}) %copy-start) | copy-done | bytes 1048600
  1.3 0.8 %copy-done.3 = bf16[2,64,256]{2,1,0:T(8,128)(2,1)S(1)} copy-done((bf16[2,64,256]{2,1,0:T(8,128)(2,1)S(1)}, bf16[2,64,256]{2,1,0:T(8,128)(2,1)}, u32[]{:S(2)}) %copy-start.3) | copy-done | bytes 65560
  2.1 0.7 %pack_columns.1.own.w0 = bf16[2304,128]{1,0:T(8,128)(2,1)S(1)} custom-call(s32[3]{0:T(128)S(1)} %pad_add_fusion.ints_ref, bf16[2048,256]{1,0:T(8,128)(2,1)S(1)} %copy-done, bf16[2,64,256]{2,1,0:T(8,128)(2,1)S(1)} %copy-done.3), custom_call_target="tpu_custom_call" | custom-call | tf_op jit(solution)/shard_map/pack_columns/pallas_call | solution.py:19
  2.9 3.1 %collective-permute-start = (bf16[2304,128]{1,0:T(8,128)(2,1)S(1)}, bf16[2304,128]{1,0:T(8,128)(2,1)S(1)}, u32[]{:S(2)}, u32[]{:S(2)}) collective-permute-start(bf16[2304,128]{1,0:T(8,128)(2,1)S(1)} %pack_columns.1.own.w0), channel_id=1, source_target_pairs={{0,4},{1,5},{2,6},{3,7},{4,0},{5,1},{6,2},{7,3},{8,12},{9,13},{10,... | collective-permute-start | bytes 1769480 | tf_op jit(solution)/shard_map/ppermute | solution.py:61
  6.0 0.8 %sort_blocks.1.sorted_ref.a_ref = bf16[272,2048]{1,0:T(8,128)(2,1)S(1)} custom-call(s32[3]{0:T(128)S(1)} %pad_add_fusion.ints_ref, s32[8]{0:T(128)S(1)} %copy-done.4, s32[4]{0:T(128)S(1)} %copy-done.5, bf16[256,2048]{1,0:T(8,128)(2,1)S(1)} %copy-done.1), custom_call_target="tpu_custom_call" | custom-call | tf_op jit(solution)/shard_map/sort_blocks/pallas_call | solution.py:19
  6.8 1.6 %collective-permute-start.5 = (bf16[272,2048]{1,0:T(8,128)(2,1)S(1)}, bf16[272,2048]{1,0:T(8,128)(2,1)S(1)}, u32[]{:S(2)}, u32[]{:S(2)}) collective-permute-start(bf16[272,2048]{1,0:T(8,128)(2,1)S(1)} %sort_blocks.1.sorted_ref.a_ref), channel_id=1, source_target_pairs={{0,16},{1,17},{2,18},{3,19},{4,20},{5,21},{6,22},{7,23},{8,24},{9,... | collective-permute-start | bytes 3342344 | tf_op jit(solution)/shard_map/ppermute | solution.py:61
  8.4 10.9 %collective-permute-done.near.w1 = bf16[2304,128]{1,0:T(8,128)(2,1)S(1)} collective-permute-done((bf16[2304,128]{1,0:T(8,128)(2,1)S(1)}, bf16[2304,128]{1,0:T(8,128)(2,1)S(1)}, u32[]{:S(2)}, u32[]{:S(2)}) %collective-permute-start) | collective-permute-done | bytes 589856 | tf_op jit(solution)/shard_map/ppermute | solution.py:61
  19.3 0.8 %pack_shrinks.1 = (bf16[1024,128]{1,0:T(8,128)(2,1)S(1)}, bf16[1024,128]{1,0:T(8,128)(2,1)S(1)}, bf16[2304,128]{1,0:T(8,128)(2,1)S(1)}, bf16[2304,128]{1,0:T(8,128)(2,1)S(1)}) custom-call(s32[3]{0:T(128)S(1)} %pad_add_fusion.ints_ref, bf16[272,2048]{1,0:T(8,128)(2,1)S(1)} %sort_blocks.1.sorted_ref.a_ref, bf16[2,64,2048]{2,1,0:T(8,128)(2,1)S(1)} %bitcast.4), custom_call_target="tpu_custom_call" | custom-call | tf_op jit(solution)/shard_map/pack_shrinks/pallas_call | solution.py:19
  20.2 0.6 choose.2
  20.8 3.4 %collective-permute-start.3 = (bf16[2304,128]{1,0:T(8,128)(2,1)S(1)}, bf16[2304,128]{1,0:T(8,128)(2,1)S(1)}, u32[]{:S(2)}, u32[]{:S(2)}) collective-permute-start(bf16[2304,128]{1,0:T(8,128)(2,1)S(1)} %choose.2), channel_id=1, source_target_pairs={{0,4},{1,5},{2,6},{3,7},{4,0},{5,1},{6,2},{7,3},{8,12},{9,13},{10,... | collective-permute-start | bytes 1769480 | tf_op jit(solution)/shard_map/ppermute | solution.py:61
  24.1 0.6 choose.3
  24.7 13.2 %collective-permute-start.4 = (bf16[2304,128]{1,0:T(8,128)(2,1)S(1)}, bf16[2304,128]{1,0:T(8,128)(2,1)S(1)}, u32[]{:S(2)}, u32[]{:S(2)}) collective-permute-start(bf16[2304,128]{1,0:T(8,128)(2,1)S(1)} %choose.3), channel_id=1, source_target_pairs={{0,4},{1,5},{2,6},{3,7},{4,0},{5,1},{6,2},{7,3},{8,12},{9,13},{10,... | collective-permute-start | bytes 1769480 | tf_op jit(solution)/shard_map/ppermute | solution.py:61
  38.0 1.5 %collective-permute-start.8 = (bf16[1024,128]{1,0:T(8,128)(2,1)S(1)}, bf16[1024,128]{1,0:T(8,128)(2,1)S(1)}, u32[]{:S(2)}, u32[]{:S(2)}) collective-permute-start(bf16[1024,128]{1,0:T(8,128)(2,1)S(1)} %collective-permute-done.7.d2), channel_id=1, source_target_pairs={{0,16},{1,17},{2,18},{3,19},{4,20},{5,21},{6,22},{7,23},{8,24},{9,... | collective-permute-start | bytes 786440 | tf_op jit(solution)/shard_map/ppermute | solution.py:61
  39.5 0.1 collective-permute-start.9
  39.6 5.3 %collective-permute-done.8.e2 = bf16[1024,128]{1,0:T(8,128)(2,1)S(1)} collective-permute-done((bf16[1024,128]{1,0:T(8,128)(2,1)S(1)}, bf16[1024,128]{1,0:T(8,128)(2,1)S(1)}, u32[]{:S(2)}, u32[]{:S(2)}) %collective-permute-start.8) | collective-permute-done | bytes 262176 | tf_op jit(solution)/shard_map/ppermute | solution.py:61
  44.8 2.5 %collective-permute-start.10 = (bf16[1024,128]{1,0:T(8,128)(2,1)S(1)}, bf16[1024,128]{1,0:T(8,128)(2,1)S(1)}, u32[]{:S(2)}, u32[]{:S(2)}) collective-permute-start(bf16[1024,128]{1,0:T(8,128)(2,1)S(1)} %collective-permute-done.9.d3), channel_id=1, source_target_pairs={{0,16},{1,17},{2,18},{3,19},{4,20},{5,21},{6,22},{7,23},{8,24},{9,... | collective-permute-start | bytes 786440 | tf_op jit(solution)/shard_map/ppermute | solution.py:61
  47.3 2.7 %early_columns.1 = (f32[1536,128]{1,0:T(8,128)S(1)}, f32[3,256,64]{2,1,0:T(8,128)S(1)}) custom-call(s32[3]{0:T(128)S(1)} %pad_add_fusion.ints_ref, bf16[272,2048]{1,0:T(8,128)(2,1)S(1)} %sort_blocks.1.sorted_ref.a_ref, bf16[272,2048]{1,0:T(8,128)(2,1)S(1)} %collective-permute-done.5.b_ref, bf16[2304,128]{1,0:T(8,128)(2,1)S(1)} %pack_columns.1.own.w0, ...), custom_call_target="tpu_custom_call" | custom-call | tf_op jit(solution)/shard_map/early_columns/pallas_call | solution.py:19
  50.0 1.4 %last_columns.1 = (f32[1024,128]{1,0:T(8,128)S(1)}, bf16[1024,128]{1,0:T(8,128)(2,1)S(1)}) custom-call(s32[3]{0:T(128)S(1)} %pad_add_fusion.ints_ref, bf16[272,2048]{1,0:T(8,128)(2,1)S(1)} %sort_blocks.1.sorted_ref.a_ref, bf16[272,2048]{1,0:T(8,128)(2,1)S(1)} %collective-permute-done.5.b_ref, bf16[2304,128]{1,0:T(8,128)(2,1)S(1)} %collective-permute-done.4.out3.three_ref, ...), custom_call_target="tpu_custom_call" | custom-call | tf_op jit(solution)/shard_map/last_columns/pallas_call | solution.py:19
  51.5 0.2 collective-permute-done.10.e3
  51.7 0.7 last_shrinks.1
  52.4 0.4 collective-permute-start.11
  52.7 1.0 %collective-permute-done.11.s_came = bf16[384,128]{1,0:T(8,128)(2,1)S(1)} collective-permute-done((bf16[384,128]{1,0:T(8,128)(2,1)S(1)}, bf16[384,128]{1,0:T(8,128)(2,1)S(1)}, u32[]{:S(2)}, u32[]{:S(2)}) %collective-permute-start.11) | collective-permute-done | bytes 98336 | tf_op jit(solution)/shard_map/ppermute | solution.py:61
  53.7 0.6 add_cores.1
  54.3 1.6 %collective-permute-start.12 = (bf16[384,128]{1,0:T(8,128)(2,1)S(1)}, bf16[384,128]{1,0:T(8,128)(2,1)S(1)}, u32[]{:S(2)}, u32[]{:S(2)}) collective-permute-start(bf16[384,128]{1,0:T(8,128)(2,1)S(1)} %get-tuple-element.37), channel_id=1, source_target_pairs={{0,2},{1,3},{2,0},{3,1},{4,6},{5,7},{6,4},{7,5},{8,10},{9,11},{10,... | collective-permute-start | bytes 294920 | tf_op jit(solution)/shard_map/ppermute | solution.py:61
  55.9 2.0 %collective-permute-start.13 = (bf16[384,128]{1,0:T(8,128)(2,1)S(1)}, bf16[384,128]{1,0:T(8,128)(2,1)S(1)}, u32[]{:S(2)}, u32[]{:S(2)}) collective-permute-start(bf16[384,128]{1,0:T(8,128)(2,1)S(1)} %get-tuple-element.38), channel_id=1, source_target_pairs={{0,16},{1,17},{2,18},{3,19},{4,20},{5,21},{6,22},{7,23},{8,24},{9,... | collective-permute-start | bytes 294920 | tf_op jit(solution)/shard_map/ppermute | solution.py:61
  57.9 4.2 %collective-permute-start.15 = (bf16[128,128]{1,0:T(8,128)(2,1)S(1)}, bf16[128,128]{1,0:T(8,128)(2,1)S(1)}, u32[]{:S(2)}, u32[]{:S(2)}) collective-permute-start(bf16[128,128]{1,0:T(8,128)(2,1)S(1)} %get-tuple-element.40), channel_id=1, source_target_pairs={{0,4},{1,5},{2,6},{3,7},{4,0},{5,1},{6,2},{7,3},{8,12},{9,13},{10,... | collective-permute-start | bytes 98312 | tf_op jit(solution)/shard_map/ppermute | solution.py:61
  62.1 0.9 %collective-permute-start.16 = (bf16[128,128]{1,0:T(8,128)(2,1)S(1)}, bf16[128,128]{1,0:T(8,128)(2,1)S(1)}, u32[]{:S(2)}, u32[]{:S(2)}) collective-permute-start(bf16[128,128]{1,0:T(8,128)(2,1)S(1)} %get-tuple-element.40), channel_id=1, source_target_pairs={{0,6},{1,7},{2,4},{3,5},{4,2},{5,3},{6,0},{7,1},{8,14},{9,15},{10,... | collective-permute-start | bytes 98312 | tf_op jit(solution)/shard_map/ppermute | solution.py:61
  63.0 0.6 ups.1.up_ref
  63.6 0.4 collective-permute-done.15.n_ref
  64.0 2.9 %collective-permute-done.16.nx_ref = bf16[128,128]{1,0:T(8,128)(2,1)S(1)} collective-permute-done((bf16[128,128]{1,0:T(8,128)(2,1)S(1)}, bf16[128,128]{1,0:T(8,128)(2,1)S(1)}, u32[]{:S(2)}, u32[]{:S(2)}) %collective-permute-start.16) | collective-permute-done | bytes 32800 | tf_op jit(solution)/shard_map/ppermute | solution.py:61
  66.9 1.5 %finish.1 = bf16[256,256]{1,0:T(8,128)(2,1)} custom-call(s32[3]{0:T(128)S(1)} %pad_add_fusion.ints_ref, s32[8]{0:T(128)S(1)} %copy-done.4, s32[4]{0:T(128)S(1)} %copy-done.5, s32[4]{0:T(128)S(1)} %copy-done.6, bf16[4,256,128]{2,1,0:T(8,128)(2,1)S(1)} %ups.1.up_ref, f32[384,128]{1,0:T(8,128)S(1)} %get-tuple-element.36.mine_ref, ...), custom_call_target="tpu_custom_call" | custom-call | tf_op jit(solution)/shard_map/finish/pallas_call | solution.py:19
  (29 shorter events, 0.2 us)
Async XLA Ops:
  0.0 6.0 %copy-start.4 = (s32[8]{0:T(128)S(1)}, s32[8]{0:T(128)}, u32[]{:S(2)}) copy-start(s32[8]{0:T(128)} %table_ref.3) | copy-start | bytes 100
  0.0 6.0 %copy-start.5 = (s32[4]{0:T(128)S(1)}, s32[4]{0:T(128)}, u32[]{:S(2)}) copy-start(s32[4]{0:T(128)} %block_ref.3) | copy-start | bytes 52
  0.1 1.2 %copy-start = (bf16[2048,256]{1,0:T(8,128)(2,1)S(1)}, bf16[2048,256]{1,0:T(8,128)(2,1)}, u32[]{:S(2)}) copy-start(bf16[2048,256]{1,0:T(8,128)(2,1)} %w_ref.1) | copy-start | bytes 3145732
  1.3 0.8 %copy-start.3 = (bf16[2,64,256]{2,1,0:T(8,128)(2,1)S(1)}, bf16[2,64,256]{2,1,0:T(8,128)(2,1)}, u32[]{:S(2)}) copy-start(bf16[2,64,256]{2,1,0:T(8,128)(2,1)} %u_ref.1) | copy-start | bytes 196612
  2.1 3.8 %copy-start.1 = (bf16[256,2048]{1,0:T(8,128)(2,1)S(1)}, bf16[256,2048]{1,0:T(8,128)(2,1)}, u32[]{:S(2)}) copy-start(bf16[256,2048]{1,0:T(8,128)(2,1)} %tok_ref.1) | copy-start | bytes 3145732
  2.9 16.4 %copy-start.2 = (bf16[2,2048,64]{1,2,0:T(8,128)(2,1)S(1)}, bf16[2,2048,64]{1,2,0:T(8,128)(2,1)}, u32[]{:S(2)}) copy-start(bf16[2,2048,64]{1,2,0:T(8,128)(2,1)} %param.9) | copy-start | bytes 1572868
  2.9 16.4 %collective-permute-start = (bf16[2304,128]{1,0:T(8,128)(2,1)S(1)}, bf16[2304,128]{1,0:T(8,128)(2,1)S(1)}, u32[]{:S(2)}, u32[]{:S(2)}) collective-permute-start(bf16[2304,128]{1,0:T(8,128)(2,1)S(1)} %pack_columns.1.own.w0), channel_id=1, source_target_pairs={{0,4},{1,5},{2,6},{3,7},{4,0},{5,1},{6,2},{7,3},{8,12},{9,13},{10,... | collective-permute-start | bytes 1769480 | tf_op jit(solution)/shard_map/ppermute | solution.py:61
  6.0 14.2 %collective-permute-start.1 = (bf16[2304,128]{1,0:T(8,128)(2,1)S(1)}, bf16[2304,128]{1,0:T(8,128)(2,1)S(1)}, u32[]{:S(2)}, u32[]{:S(2)}) collective-permute-start(bf16[2304,128]{1,0:T(8,128)(2,1)S(1)} %pack_columns.1.own.w0), channel_id=1, source_target_pairs={{0,1},{1,0},{2,3},{3,2},{4,8},{5,9},{6,10},{7,11},{8,4},{9,5},{10,... | collective-permute-start | bytes 1769480 | tf_op jit(solution)/shard_map/ppermute | solution.py:61
  6.8 31.2 %collective-permute-start.5 = (bf16[272,2048]{1,0:T(8,128)(2,1)S(1)}, bf16[272,2048]{1,0:T(8,128)(2,1)S(1)}, u32[]{:S(2)}, u32[]{:S(2)}) collective-permute-start(bf16[272,2048]{1,0:T(8,128)(2,1)S(1)} %sort_blocks.1.sorted_ref.a_ref), channel_id=1, source_target_pairs={{0,16},{1,17},{2,18},{3,19},{4,20},{5,21},{6,22},{7,23},{8,24},{9,... | collective-permute-start | bytes 3342344 | tf_op jit(solution)/shard_map/ppermute | solution.py:61
  19.3 4.9 %collective-permute-start.2 = (bf16[2304,128]{1,0:T(8,128)(2,1)S(1)}, bf16[2304,128]{1,0:T(8,128)(2,1)S(1)}, u32[]{:S(2)}, u32[]{:S(2)}) collective-permute-start(bf16[2304,128]{1,0:T(8,128)(2,1)S(1)} %collective-permute-done.near.w1), channel_id=1, source_target_pairs={{0,1},{1,0},{2,3},{3,2},{4,8},{5,9},{6,10},{7,11},{8,4},{9,5},{10,... | collective-permute-start | bytes 1769480 | tf_op jit(solution)/shard_map/ppermute | solution.py:61
  20.8 18.7 %collective-permute-start.3 = (bf16[2304,128]{1,0:T(8,128)(2,1)S(1)}, bf16[2304,128]{1,0:T(8,128)(2,1)S(1)}, u32[]{:S(2)}, u32[]{:S(2)}) collective-permute-start(bf16[2304,128]{1,0:T(8,128)(2,1)S(1)} %choose.2), channel_id=1, source_target_pairs={{0,4},{1,5},{2,6},{3,7},{4,0},{5,1},{6,2},{7,3},{8,12},{9,13},{10,... | collective-permute-start | bytes 1769480 | tf_op jit(solution)/shard_map/ppermute | solution.py:61
  24.1 13.8 %collective-permute-start.7 = (bf16[1024,128]{1,0:T(8,128)(2,1)S(1)}, bf16[1024,128]{1,0:T(8,128)(2,1)S(1)}, u32[]{:S(2)}, u32[]{:S(2)}) collective-permute-start(bf16[1024,128]{1,0:T(8,128)(2,1)S(1)} %get-tuple-element.30.d0), channel_id=1, source_target_pairs={{0,1},{1,0},{2,3},{3,2},{4,8},{5,9},{6,10},{7,11},{8,4},{9,5},{10,... | collective-permute-start | bytes 786440 | tf_op jit(solution)/shard_map/ppermute | solution.py:61
  24.7 25.3 %collective-permute-start.4 = (bf16[2304,128]{1,0:T(8,128)(2,1)S(1)}, bf16[2304,128]{1,0:T(8,128)(2,1)S(1)}, u32[]{:S(2)}, u32[]{:S(2)}) collective-permute-start(bf16[2304,128]{1,0:T(8,128)(2,1)S(1)} %choose.3), channel_id=1, source_target_pairs={{0,4},{1,5},{2,6},{3,7},{4,0},{5,1},{6,2},{7,3},{8,12},{9,13},{10,... | collective-permute-start | bytes 1769480 | tf_op jit(solution)/shard_map/ppermute | solution.py:61
  38.0 6.9 %collective-permute-start.8 = (bf16[1024,128]{1,0:T(8,128)(2,1)S(1)}, bf16[1024,128]{1,0:T(8,128)(2,1)S(1)}, u32[]{:S(2)}, u32[]{:S(2)}) collective-permute-start(bf16[1024,128]{1,0:T(8,128)(2,1)S(1)} %collective-permute-done.7.d2), channel_id=1, source_target_pairs={{0,16},{1,17},{2,18},{3,19},{4,20},{5,21},{6,22},{7,23},{8,24},{9,... | collective-permute-start | bytes 786440 | tf_op jit(solution)/shard_map/ppermute | solution.py:61
  39.5 5.3 %collective-permute-start.9 = (bf16[1024,128]{1,0:T(8,128)(2,1)S(1)}, bf16[1024,128]{1,0:T(8,128)(2,1)S(1)}, u32[]{:S(2)}, u32[]{:S(2)}) collective-permute-start(bf16[1024,128]{1,0:T(8,128)(2,1)S(1)} %slice.4), channel_id=1, source_target_pairs={{0,1},{1,0},{2,3},{3,2},{4,8},{5,9},{6,10},{7,11},{8,4},{9,5},{10,... | collective-permute-start | bytes 786440 | tf_op jit(solution)/shard_map/ppermute | solution.py:61
  44.8 6.8 %collective-permute-start.10 = (bf16[1024,128]{1,0:T(8,128)(2,1)S(1)}, bf16[1024,128]{1,0:T(8,128)(2,1)S(1)}, u32[]{:S(2)}, u32[]{:S(2)}) collective-permute-start(bf16[1024,128]{1,0:T(8,128)(2,1)S(1)} %collective-permute-done.9.d3), channel_id=1, source_target_pairs={{0,16},{1,17},{2,18},{3,19},{4,20},{5,21},{6,22},{7,23},{8,24},{9,... | collective-permute-start | bytes 786440 | tf_op jit(solution)/shard_map/ppermute | solution.py:61
  51.4 2.3 %collective-permute-start.6 = (bf16[1024,128]{1,0:T(8,128)(2,1)S(1)}, bf16[1024,128]{1,0:T(8,128)(2,1)S(1)}, u32[]{:S(2)}, u32[]{:S(2)}) collective-permute-start(bf16[1024,128]{1,0:T(8,128)(2,1)S(1)} %get-tuple-element.29), channel_id=1, source_target_pairs={{0,1},{1,0},{2,3},{3,2},{4,5},{5,4},{6,7},{7,6},{8,9},{9,8},{10,11... | collective-permute-start | bytes 786440 | tf_op jit(solution)/shard_map/ppermute | solution.py:61
  52.4 1.4 %collective-permute-start.11 = (bf16[384,128]{1,0:T(8,128)(2,1)S(1)}, bf16[384,128]{1,0:T(8,128)(2,1)S(1)}, u32[]{:S(2)}, u32[]{:S(2)}) collective-permute-start(bf16[384,128]{1,0:T(8,128)(2,1)S(1)} %get-tuple-element.35), channel_id=1, source_target_pairs={{0,1},{1,0},{2,3},{3,2},{4,5},{5,4},{6,7},{7,6},{8,9},{9,8},{10,11... | collective-permute-start | bytes 294920 | tf_op jit(solution)/shard_map/ppermute | solution.py:61
  54.3 12.6 %collective-permute-start.12 = (bf16[384,128]{1,0:T(8,128)(2,1)S(1)}, bf16[384,128]{1,0:T(8,128)(2,1)S(1)}, u32[]{:S(2)}, u32[]{:S(2)}) collective-permute-start(bf16[384,128]{1,0:T(8,128)(2,1)S(1)} %get-tuple-element.37), channel_id=1, source_target_pairs={{0,2},{1,3},{2,0},{3,1},{4,6},{5,7},{6,4},{7,5},{8,10},{9,11},{10,... | collective-permute-start | bytes 294920 | tf_op jit(solution)/shard_map/ppermute | solution.py:61
  55.9 11.0 %collective-permute-start.13 = (bf16[384,128]{1,0:T(8,128)(2,1)S(1)}, bf16[384,128]{1,0:T(8,128)(2,1)S(1)}, u32[]{:S(2)}, u32[]{:S(2)}) collective-permute-start(bf16[384,128]{1,0:T(8,128)(2,1)S(1)} %get-tuple-element.38), channel_id=1, source_target_pairs={{0,16},{1,17},{2,18},{3,19},{4,20},{5,21},{6,22},{7,23},{8,24},{9,... | collective-permute-start | bytes 294920 | tf_op jit(solution)/shard_map/ppermute | solution.py:61
  57.9 9.0 %collective-permute-start.14 = (bf16[384,128]{1,0:T(8,128)(2,1)S(1)}, bf16[384,128]{1,0:T(8,128)(2,1)S(1)}, u32[]{:S(2)}, u32[]{:S(2)}) collective-permute-start(bf16[384,128]{1,0:T(8,128)(2,1)S(1)} %get-tuple-element.39), channel_id=1, source_target_pairs={{0,18},{1,19},{2,16},{3,17},{4,22},{5,23},{6,20},{7,21},{8,26},{9,... | collective-permute-start | bytes 294920 | tf_op jit(solution)/shard_map/ppermute | solution.py:61
  57.9 9.0 %copy-start.6 = (s32[4]{0:T(128)S(1)}, s32[4]{0:T(128)}, u32[]{:S(2)}) copy-start(s32[4]{0:T(128)} %live_ref.1) | copy-start | bytes 52
  57.9 6.0 %collective-permute-start.15 = (bf16[128,128]{1,0:T(8,128)(2,1)S(1)}, bf16[128,128]{1,0:T(8,128)(2,1)S(1)}, u32[]{:S(2)}, u32[]{:S(2)}) collective-permute-start(bf16[128,128]{1,0:T(8,128)(2,1)S(1)} %get-tuple-element.40), channel_id=1, source_target_pairs={{0,4},{1,5},{2,6},{3,7},{4,0},{5,1},{6,2},{7,3},{8,12},{9,13},{10,... | collective-permute-start | bytes 98312 | tf_op jit(solution)/shard_map/ppermute | solution.py:61
  62.1 4.8 %collective-permute-start.16 = (bf16[128,128]{1,0:T(8,128)(2,1)S(1)}, bf16[128,128]{1,0:T(8,128)(2,1)S(1)}, u32[]{:S(2)}, u32[]{:S(2)}) collective-permute-start(bf16[128,128]{1,0:T(8,128)(2,1)S(1)} %get-tuple-element.40), channel_id=1, source_target_pairs={{0,6},{1,7},{2,4},{3,5},{4,2},{5,3},{6,0},{7,1},{8,14},{9,15},{10,... | collective-permute-start | bytes 98312 | tf_op jit(solution)/shard_map/ppermute | solution.py:61

commit v5 on v4

--- a/solution.py
+++ b/solution.py
@@ -15,9 +15,14 @@
 HBM = pl.BlockSpec(memory_space=pltpu.HBM)
 
 
+class Place:
+    def __getitem__(self, n):
+        return lax.axis_index(AXES[n]).astype(jnp.int32)
+
+
 def call(body, name, outs, specs, ins, scratch=(), mib=16):
     return pl.pallas_call(
-        body,
+        lambda *refs: body(Place(), *refs),
         name=name,
         out_shape=outs,
         in_specs=specs,
@@ -33,8 +38,6 @@
 
 def local_line(sizes, tokens, value_weight, down, up, slot_table, per_block, live_rows):
     groups, dp, tensor = sizes
-    y, z, t = (lax.axis_index(a) for a in AXES)
-    place = jnp.stack([y, z, t]).astype(jnp.int32)
     rows, feats = tokens.shape
     blocks = per_block.shape[0]
     block_len = rows // blocks
@@ -85,10 +88,13 @@
             return jnp.where(outer_plane(here), 3 - near, 3 - here)
         return jnp.where(outer_plane(here), 3 - here, 3 - near)
 
-    def block_at(table_ref, block_ref, holder):
+    adapters = slot_table.shape[0]
+    info = jnp.concatenate([slot_table, per_block, live_rows])
+
+    def block_at(info_ref, holder):
         which, local_slot = jnp.int32(0), jnp.int32(0)
         for k in range(blocks):
-            s = table_ref[block_ref[k]]
+            s = info_ref[info_ref[adapters + k]]
             hit = s // per_dev == holder
             which = jnp.where(hit, k, which)
             local_slot = jnp.where(hit, s % per_dev, local_slot)
@@ -119,8 +125,8 @@
         pack_columns,
         "pack_columns",
         like(feats + up_rows, LANES),
-        [SMEM, HBM, HBM],
-        (place, value_weight, up),
+        [HBM, HBM],
+        (value_weight, up),
         [pltpu.SemaphoreType.DMA((1 + per_dev * col_tiles,))],
         mib=16,
     )
@@ -130,13 +136,13 @@
     wide_rows = feats + up_rows
     code_at = half + tile_rows
 
-    def sort_blocks(ints_ref, table_ref, block_ref, tok_ref, sorted_ref, sems):
+    def sort_blocks(ints_ref, info_ref, tok_ref, sorted_ref, sems):
         here = ints_ref[1]
         copies = []
         row = lax.broadcasted_iota(jnp.int32, (CODE_ROWS, LANES), 0)
         code = jnp.zeros((CODE_ROWS, LANES), jnp.int32)
         for slot in range(dp):
-            which, local_slot = block_at(table_ref, block_ref, where_from(here, slot))
+            which, local_slot = block_at(info_ref, where_from(here, slot))
             src = tok_ref.at[pl.ds(pl.multiple_of(which * block_len, block_len), block_len)]
             to = sorted_ref.at[pl.ds(slot * block_len, block_len)]
             copies.append(pltpu.make_async_copy(src, to, sems.at[slot]))
@@ -150,8 +156,8 @@
         sort_blocks,
         "sort_blocks",
         like(rows + CODE_ROWS, feats),
-        [SMEM, SMEM, SMEM, HBM],
-        (place, slot_table, per_block, tokens),
+        [SMEM, HBM],
+        (info, tokens),
         [pltpu.SemaphoreType.DMA((dp,))],
         mib=16,
     )
@@ -173,8 +179,8 @@
         pack_shrinks,
         "pack_shrinks",
         (like(half, LANES), like(half, LANES), like(wide_rows, LANES), like(wide_rows, LANES)),
-        [SMEM, VMEM, VMEM],
-        (place, in_order, jnp.transpose(down, (0, 2, 1))),
+        [VMEM, VMEM],
+        (in_order, jnp.transpose(down, (0, 2, 1))),
     )
 
     def choose(ints_ref, outer_ref, inner_ref, out_ref):
@@ -189,7 +195,7 @@
             out_ref[...] = inner_ref[...]
 
     def chosen(x, y):
-        return call(choose, "choose", like(wide_rows, LANES), [SMEM, VMEM, VMEM], (place, x, y))
+        return call(choose, "choose", like(wide_rows, LANES), [VMEM, VMEM], (x, y))
 
     near_w = to_neighbour(own_w)
     mid_w = to_middle(own_w)
@@ -272,11 +278,14 @@
         early,
         "early_columns",
         (like(3 * both, LANES, F32), s_shape),
-        [SMEM] + [VMEM] * 8,
-        (place, in_order, others, own_w, near_w, mid_w, two, own_d, own_e),
-    )
-
-    def last_columns(ints_ref, a_ref, b_ref, three_ref, far, part_ref, keep, away, last_ref):
+        [VMEM] * 8,
+        (in_order, others, own_w, near_w, mid_w, two, own_d, own_e),
+    )
+
+    def last_columns(
+        ints_ref, a_ref, b_ref, two_ref, three_ref, d2, e2, far, part_ref, s_in,
+        keep, away, s_ref, last_ref,
+    ):
         here, core = ints_ref[1], ints_ref[2] % 2
         is_outer = outer_plane(here)
 
@@ -292,28 +301,34 @@
                 away[at, :] = ref[ref_at : ref_at + both, :].astype(BF16)
 
         pl.when(is_outer)(lambda: columns(a_ref, b_ref, three_ref, last_ref, 0))
-        pl.when(jnp.logical_not(is_outer))(lambda: columns(a_ref, b_ref, far, last_ref, 0))
+        shrink = shrinker(ints_ref[0], a_ref, b_ref, two_ref, three_ref, s_ref)
+        s_ref[...] = s_in[...]
+
+        @pl.when(jnp.logical_not(is_outer))
+        def _():
+            columns(a_ref, b_ref, far, last_ref, 0)
+            shrink(2, d2, e2, 2)
+
         for slot in range(3):
             put(part_ref, slot * both, where_from(here, slot))
         put(last_ref, 0, where_from(here, 3))
 
-    keep, away = call(
+    keep, away, shrunk = call(
         last_columns,
         "last_columns",
-        (like(pairs * both, LANES, F32), like(pairs * both, LANES)),
-        [SMEM] + [VMEM] * 5,
-        (place, in_order, others, three, far_w, part),
+        (like(pairs * both, LANES, F32), like(pairs * both, LANES), s_shape),
+        [VMEM] * 9,
+        (in_order, others, two, three, mid_d, mid_e, far_w, part, shrunk),
         [pltpu.VMEM((both, LANES), F32)],
     )
     came = swap(away, lambda a, b, c: (a, b, c ^ 1))
 
-    def last_shrinks(ints_ref, a_ref, b_ref, two_ref, three_ref, d2, e2, d3, e3, s_in, keep, away, s_ref):
+    def last_shrinks(ints_ref, a_ref, b_ref, two_ref, three_ref, d3, e3, s_in, keep, away, s_ref):
         shrink = shrinker(ints_ref[0], a_ref, b_ref, two_ref, three_ref, s_ref)
         s_ref[...] = s_in[...]
 
         @pl.when(jnp.logical_not(outer_plane(ints_ref[1])))
         def _():
-            shrink(2, d2, e2, 2)
             shrink(3, d3, e3, 3)
 
         for g in range(3):
@@ -325,8 +340,8 @@
         last_shrinks,
         "last_shrinks",
         (like(3 * s_msg, LANES, F32), like(3 * s_msg, LANES)),
-        [SMEM] + [VMEM] * 9,
-        (place, in_order, others, two, three, mid_d, mid_e, far_d, far_e, shrunk),
+        [VMEM] * 7,
+        (in_order, others, two, three, far_d, far_e, shrunk),
         [pltpu.VMEM((3, rows, rank), F32)],
     )
     s_came = swap(s_away, lambda a, b, c: (a, b, c ^ 1))
@@ -364,8 +379,8 @@
             like(rows + s_msg, LANES),
             like(s_msg, LANES),
         ),
-        [SMEM] + [VMEM] * 4,
-        (place, keep, came, s_keep, s_came),
+        [VMEM] * 4,
+        (keep, came, s_keep, s_came),
     )
     from_d = swap(to_d, lambda a, b, c: (1 - a, b, c ^ 2))
     from_nearx = swap(to_near, lambda a, b, c: (a, b ^ 1, c ^ 2))
@@ -397,12 +412,12 @@
         ups,
         "ups",
         jax.ShapeDtypeStruct((dp, up_rows, LANES), BF16),
-        [SMEM] + [VMEM] * 6,
-        (place, own_w, near_w, mid_w, far_w, two, three),
+        [VMEM] * 6,
+        (own_w, near_w, mid_w, far_w, two, three),
     )
 
     def finish(
-        ints_ref, table_ref, block_ref, live_ref, up_ref, mine_ref, x_ref, y_ref, d_ref, n_ref,
+        ints_ref, info_ref, up_ref, mine_ref, x_ref, y_ref, d_ref, n_ref,
         nx_ref, out_ref,
     ):
         me, here = ints_ref[0], ints_ref[1]
@@ -417,7 +432,7 @@
         row = lax.broadcasted_iota(jnp.int32, (block_len, LANES), 0)
         for slot in range(dp):
             holder = where_from(here, slot)
-            which, local_slot = block_at(table_ref, block_ref, holder)
+            which, local_slot = block_at(info_ref, holder)
             piece = s[
                 (slot % per_lane) * block_len : (slot % per_lane + 1) * block_len,
                 (slot // per_lane) * rank : (slot // per_lane + 1) * rank,
@@ -427,16 +442,16 @@
                 at = pl.ds(pl.multiple_of((local_slot * col_tiles + v) * rank, rank), rank)
                 delta = jnp.dot(piece, up_ref[holder, at, :], preferred_element_type=F32)
                 base = split[v][slot * block_len : (slot + 1) * block_len, :]
-                mixed = jnp.where(row < live_ref[which], base + delta.astype(BF16).astype(F32), 0.0)
+                mixed = jnp.where(row < info_ref[adapters + blocks + which], base + delta.astype(BF16).astype(F32), 0.0)
                 out_ref[to, v * LANES : (v + 1) * LANES] = mixed.astype(BF16)
 
     return call(
         finish,
         "finish",
         like(rows, out_cols),
-        [SMEM] * 4 + [VMEM] * 7,
+        [SMEM] + [VMEM] * 7,
         (
-            place, slot_table, per_block, live_rows, up_all, mine, from_x, from_y, from_d,
+            info, up_all, mine, from_x, from_y, from_d,
             from_near, from_nearx,
         ),
     )

time: 68.6 us -> 66.7 us (0.972)
  Pallas kernels: 10.9 us -> 6.03 us
  waiting for transfers between devices: 20.7 us -> 22.5 us
  starting transfers between devices: 34.4 us -> 35.6 us
    pallas_call x11, Pallas kernels: 10.9 us -> 6.03 us  [call(): pl.pallas_call(lambda *refs: body(Place(), *refs), name=name, out_shape=o...]
    ppermute x17, waiting for transfers between devices: 20.7 us -> 22.5 us  [swap(): return lax.ppermute(x, AXES, perm)]
    ppermute x17, starting transfers between devices: 34.4 us -> 35.6 us  [swap(): return lax.ppermute(x, AXES, perm)]
  transfers between devices with their start and end apart: 17 -> 17, of which waited for: 6 -> 6; matrix products, arithmetic and copies ran while one was open for 0% -> 0% of each run, Pallas kernels for 12% -> 7%
where the time goes in v5:
time: 66.7 us; the launch traced here: 66.6 us
  starting transfers between devices  35.6 us (53%)
  waiting for transfers between devices  22.5 us (34%)
  Pallas kernels  6.03 us (9%)
  local copies, waits for them, and re-layouts  2.19 us (3%)
    ppermute x17, starting transfers between devices, swap(): return lax.ppermute(x, AXES, perm)  35.6 us
    ppermute x17, waiting for transfers between devices, swap(): return lax.ppermute(x, AXES, perm)  22.5 us
    pallas_call x11, Pallas kernels, call(): pl.pallas_call(lambda *refs: body(Place(), *refs), name=name, out_shape=o...  6.03 us
    unnamed x14, local copies, waits for them, and re-layouts  2.17 us
  transfers between devices with their start and end apart: 17, of which 6 were waited for; matrix products, arithmetic and copies ran while one was open for 0% of the time, Pallas kernels for 7%

profile of v5, /device:TPU:0, one launch (start us, length us, event | category | flops | bytes accessed | tf_op | source)
XLA Modules:
  0.0 66.6 jit_solution(5192110127311788868)
XLA Ops:
  0.0 1.3 %copy-done.1 = bf16[2048,256]{1,0:T(8,128)(2,1)S(1)} copy-done((bf16[2048,256]{1,0:T(8,128)(2,1)S(1)}, bf16[2048,256]{1,0:T(8,128)(2,1)}, u32[]{:S(2)}) %copy-start.1) | copy-done | bytes 1048600
  1.3 0.8 %copy-done.3 = bf16[2,64,256]{2,1,0:T(8,128)(2,1)S(1)} copy-done((bf16[2,64,256]{2,1,0:T(8,128)(2,1)S(1)}, bf16[2,64,256]{2,1,0:T(8,128)(2,1)}, u32[]{:S(2)}) %copy-start.3) | copy-done | bytes 65560
  2.2 0.2 pack_columns.1.refs_0_.refs_2_
  2.3 0.0 copy-start.2
  2.3 3.1 %collective-permute-start = (bf16[2304,128]{1,0:T(8,128)(2,1)S(1)}, bf16[2304,128]{1,0:T(8,128)(2,1)S(1)}, u32[]{:S(2)}, u32[]{:S(2)}) collective-permute-start(bf16[2304,128]{1,0:T(8,128)(2,1)S(1)} %pack_columns.1.refs_0_.refs_2_), channel_id=1, source_target_pairs={{0,4},{1,5},{2,6},{3,7},{4,0},{5,1},{6,2},{7,3},{8,12},{9,13},{10,... | collective-permute-start | bytes 1769480 | tf_op jit(solution)/shard_map/ppermute | solution.py:64
  5.4 0.1 pad_add_fusion.refs_0_
  5.5 0.8 %sort_blocks.1.refs_0_ = bf16[272,2048]{1,0:T(8,128)(2,1)S(1)} custom-call(s32[16]{0:T(128)S(1)} %pad_add_fusion.refs_0_, bf16[256,2048]{1,0:T(8,128)(2,1)S(1)} %copy-done), custom_call_target="tpu_custom_call" | custom-call | tf_op jit(solution)/shard_map/sort_blocks/pallas_call | solution.py:24
  6.3 1.6 %collective-permute-start.5 = (bf16[272,2048]{1,0:T(8,128)(2,1)S(1)}, bf16[272,2048]{1,0:T(8,128)(2,1)S(1)}, u32[]{:S(2)}, u32[]{:S(2)}) collective-permute-start(bf16[272,2048]{1,0:T(8,128)(2,1)S(1)} %sort_blocks.1.refs_0_), channel_id=1, source_target_pairs={{0,16},{1,17},{2,18},{3,19},{4,20},{5,21},{6,22},{7,23},{8,24},{9,... | collective-permute-start | bytes 3342344 | tf_op jit(solution)/shard_map/ppermute | solution.py:64
  7.9 10.8 %collective-permute-done.refs_1_.refs_3_ = bf16[2304,128]{1,0:T(8,128)(2,1)S(1)} collective-permute-done((bf16[2304,128]{1,0:T(8,128)(2,1)S(1)}, bf16[2304,128]{1,0:T(8,128)(2,1)S(1)}, u32[]{:S(2)}, u32[]{:S(2)}) %collective-permute-start) | collective-permute-done | bytes 589856 | tf_op jit(solution)/shard_map/ppermute | solution.py:64
  18.8 0.3 pack_shrinks.1
  19.1 0.1 choose.2
  19.1 3.4 %collective-permute-start.3 = (bf16[2304,128]{1,0:T(8,128)(2,1)S(1)}, bf16[2304,128]{1,0:T(8,128)(2,1)S(1)}, u32[]{:S(2)}, u32[]{:S(2)}) collective-permute-start(bf16[2304,128]{1,0:T(8,128)(2,1)S(1)} %choose.2), channel_id=1, source_target_pairs={{0,4},{1,5},{2,6},{3,7},{4,0},{5,1},{6,2},{7,3},{8,12},{9,13},{10,... | collective-permute-start | bytes 1769480 | tf_op jit(solution)/shard_map/ppermute | solution.py:64
  22.6 14.3 %collective-permute-start.4 = (bf16[2304,128]{1,0:T(8,128)(2,1)S(1)}, bf16[2304,128]{1,0:T(8,128)(2,1)S(1)}, u32[]{:S(2)}, u32[]{:S(2)}) collective-permute-start(bf16[2304,128]{1,0:T(8,128)(2,1)S(1)} %choose.3), channel_id=1, source_target_pairs={{0,4},{1,5},{2,6},{3,7},{4,0},{5,1},{6,2},{7,3},{8,12},{9,13},{10,... | collective-permute-start | bytes 1769480 | tf_op jit(solution)/shard_map/ppermute | solution.py:64
  36.9 1.5 %collective-permute-start.7 = (bf16[1024,128]{1,0:T(8,128)(2,1)S(1)}, bf16[1024,128]{1,0:T(8,128)(2,1)S(1)}, u32[]{:S(2)}, u32[]{:S(2)}) collective-permute-start(bf16[1024,128]{1,0:T(8,128)(2,1)S(1)} %collective-permute-done.6.refs_4_), channel_id=1, source_target_pairs={{0,16},{1,17},{2,18},{3,19},{4,20},{5,21},{6,22},{7,23},{8,24},{9,... | collective-permute-start | bytes 786440 | tf_op jit(solution)/shard_map/ppermute | solution.py:64
  38.4 0.1 collective-permute-start.9
  38.5 5.3 %collective-permute-done.7.refs_5_ = bf16[1024,128]{1,0:T(8,128)(2,1)S(1)} collective-permute-done((bf16[1024,128]{1,0:T(8,128)(2,1)S(1)}, bf16[1024,128]{1,0:T(8,128)(2,1)S(1)}, u32[]{:S(2)}, u32[]{:S(2)}) %collective-permute-start.7) | collective-permute-done | bytes 262176 | tf_op jit(solution)/shard_map/ppermute | solution.py:64
  43.8 2.5 %collective-permute-start.10 = (bf16[1024,128]{1,0:T(8,128)(2,1)S(1)}, bf16[1024,128]{1,0:T(8,128)(2,1)S(1)}, u32[]{:S(2)}, u32[]{:S(2)}) collective-permute-start(bf16[1024,128]{1,0:T(8,128)(2,1)S(1)} %collective-permute-done.9.refs_4_), channel_id=1, source_target_pairs={{0,16},{1,17},{2,18},{3,19},{4,20},{5,21},{6,22},{7,23},{8,24},{9,... | collective-permute-start | bytes 786440 | tf_op jit(solution)/shard_map/ppermute | solution.py:64
  46.2 2.1 %early_columns.1 = (f32[1536,128]{1,0:T(8,128)S(1)}, f32[3,256,64]{2,1,0:T(8,128)S(1)}) custom-call(bf16[272,2048]{1,0:T(8,128)(2,1)S(1)} %sort_blocks.1.refs_0_, bf16[272,2048]{1,0:T(8,128)(2,1)S(1)} %collective-permute-done.5.refs_1_, bf16[2304,128]{1,0:T(8,128)(2,1)S(1)} %pack_columns.1.refs_0_.refs_2_, ...), custom_call_target="tpu_custom_call" | custom-call | tf_op jit(solution)/shard_map/early_columns/pallas_call | solution.py:24
  48.4 0.8 %last_columns.1 = (f32[1024,128]{1,0:T(8,128)S(1)}, bf16[1024,128]{1,0:T(8,128)(2,1)S(1)}, f32[3,256,64]{2,1,0:T(8,128)S(1)}) custom-call(bf16[272,2048]{1,0:T(8,128)(2,1)S(1)} %sort_blocks.1.refs_0_, bf16[272,2048]{1,0:T(8,128)(2,1)S(1)} %collective-permute-done.5.refs_1_, bf16[2304,128]{1,0:T(8,128)(2,1)S(1)} %collective-permute-done.3.refs_4_.refs_5_.refs_2_, ...), custom_call_target="tpu_custom_call" | custom-call | tf_op jit(solution)/shard_map/last_columns/pallas_call | solution.py:24
  49.3 0.1 collective-permute-start.8
  49.3 1.3 %collective-permute-done.10.refs_5_ = bf16[1024,128]{1,0:T(8,128)(2,1)S(1)} collective-permute-done((bf16[1024,128]{1,0:T(8,128)(2,1)S(1)}, bf16[1024,128]{1,0:T(8,128)(2,1)S(1)}, u32[]{:S(2)}, u32[]{:S(2)}) %collective-permute-start.10) | collective-permute-done | bytes 262176 | tf_op jit(solution)/shard_map/ppermute | solution.py:64
  50.6 0.1 last_shrinks.1
  50.7 0.1 collective-permute-start.11
  50.8 1.3 %collective-permute-done.11.refs_3_ = bf16[384,128]{1,0:T(8,128)(2,1)S(1)} collective-permute-done((bf16[384,128]{1,0:T(8,128)(2,1)S(1)}, bf16[384,128]{1,0:T(8,128)(2,1)S(1)}, u32[]{:S(2)}, u32[]{:S(2)}) %collective-permute-start.11) | collective-permute-done | bytes 98336 | tf_op jit(solution)/shard_map/ppermute | solution.py:64
  52.1 0.1 add_cores.1
  52.2 1.6 %collective-permute-start.12 = (bf16[384,128]{1,0:T(8,128)(2,1)S(1)}, bf16[384,128]{1,0:T(8,128)(2,1)S(1)}, u32[]{:S(2)}, u32[]{:S(2)}) collective-permute-start(bf16[384,128]{1,0:T(8,128)(2,1)S(1)} %get-tuple-element.39), channel_id=1, source_target_pairs={{0,2},{1,3},{2,0},{3,1},{4,6},{5,7},{6,4},{7,5},{8,10},{9,11},{10,... | collective-permute-start | bytes 294920 | tf_op jit(solution)/shard_map/ppermute | solution.py:64
  53.7 2.0 %collective-permute-start.13 = (bf16[384,128]{1,0:T(8,128)(2,1)S(1)}, bf16[384,128]{1,0:T(8,128)(2,1)S(1)}, u32[]{:S(2)}, u32[]{:S(2)}) collective-permute-start(bf16[384,128]{1,0:T(8,128)(2,1)S(1)} %get-tuple-element.40), channel_id=1, source_target_pairs={{0,16},{1,17},{2,18},{3,19},{4,20},{5,21},{6,22},{7,23},{8,24},{9,... | collective-permute-start | bytes 294920 | tf_op jit(solution)/shard_map/ppermute | solution.py:64
  55.8 4.5 %collective-permute-start.15 = (bf16[128,128]{1,0:T(8,128)(2,1)S(1)}, bf16[128,128]{1,0:T(8,128)(2,1)S(1)}, u32[]{:S(2)}, u32[]{:S(2)}) collective-permute-start(bf16[128,128]{1,0:T(8,128)(2,1)S(1)} %get-tuple-element.42), channel_id=1, source_target_pairs={{0,4},{1,5},{2,6},{3,7},{4,0},{5,1},{6,2},{7,3},{8,12},{9,13},{10,... | collective-permute-start | bytes 98312 | tf_op jit(solution)/shard_map/ppermute | solution.py:64
  60.3 0.9 %collective-permute-start.16 = (bf16[128,128]{1,0:T(8,128)(2,1)S(1)}, bf16[128,128]{1,0:T(8,128)(2,1)S(1)}, u32[]{:S(2)}, u32[]{:S(2)}) collective-permute-start(bf16[128,128]{1,0:T(8,128)(2,1)S(1)} %get-tuple-element.42), channel_id=1, source_target_pairs={{0,6},{1,7},{2,4},{3,5},{4,2},{5,3},{6,0},{7,1},{8,14},{9,15},{10,... | collective-permute-start | bytes 98312 | tf_op jit(solution)/shard_map/ppermute | solution.py:64
  61.2 0.9 %collective-permute-done.15.refs_6_ = bf16[128,128]{1,0:T(8,128)(2,1)S(1)} collective-permute-done((bf16[128,128]{1,0:T(8,128)(2,1)S(1)}, bf16[128,128]{1,0:T(8,128)(2,1)S(1)}, u32[]{:S(2)}, u32[]{:S(2)}) %collective-permute-start.15) | collective-permute-done | bytes 32800 | tf_op jit(solution)/shard_map/ppermute | solution.py:64
  62.2 2.9 %collective-permute-done.16.refs_7_ = bf16[128,128]{1,0:T(8,128)(2,1)S(1)} collective-permute-done((bf16[128,128]{1,0:T(8,128)(2,1)S(1)}, bf16[128,128]{1,0:T(8,128)(2,1)S(1)}, u32[]{:S(2)}, u32[]{:S(2)}) %collective-permute-start.16) | collective-permute-done | bytes 32800 | tf_op jit(solution)/shard_map/ppermute | solution.py:64
  65.1 1.5 %finish.1 = bf16[256,256]{1,0:T(8,128)(2,1)} custom-call(s32[16]{0:T(128)S(1)} %pad_add_fusion.refs_0_, bf16[4,256,128]{2,1,0:T(8,128)(2,1)S(1)} %ups.1.refs_1_, f32[384,128]{1,0:T(8,128)S(1)} %get-tuple-element.38.refs_2_, bf16[384,128]{1,0:T(8,128)(2,1)S(1)} %collective-permute-done.12.refs_3_, bf16[384,128]{1,0:T(8,128)(2,1)S(1)} %collective-permute-done.13.refs_4_, ...), custom_call_target="tpu_custom_call" | custom-call | tf_op jit(solution)/shard_map/finish/pallas_call | solution.py:24
  (29 shorter events, 0.1 us)
Async XLA Ops:
  0.0 5.5 %copy-start = (bf16[256,2048]{1,0:T(8,128)(2,1)S(1)}, bf16[256,2048]{1,0:T(8,128)(2,1)}, u32[]{:S(2)}) copy-start(bf16[256,2048]{1,0:T(8,128)(2,1)} %refs_1_.3) | copy-start | bytes 3145732
  0.0 1.3 %copy-start.1 = (bf16[2048,256]{1,0:T(8,128)(2,1)S(1)}, bf16[2048,256]{1,0:T(8,128)(2,1)}, u32[]{:S(2)}) copy-start(bf16[2048,256]{1,0:T(8,128)(2,1)} %refs_0_.1) | copy-start | bytes 3145732
  1.3 0.8 %copy-start.3 = (bf16[2,64,256]{2,1,0:T(8,128)(2,1)S(1)}, bf16[2,64,256]{2,1,0:T(8,128)(2,1)}, u32[]{:S(2)}) copy-start(bf16[2,64,256]{2,1,0:T(8,128)(2,1)} %refs_1_.2) | copy-start | bytes 196612
  2.2 3.3 %copy-start.4 = (s32[4]{0:T(128)S(1)}, s32[4]{0:T(128)}, u32[]{:S(2)}) copy-start(s32[4]{0:T(128)} %param.13) | copy-start | bytes 52
  2.2 3.3 %copy-start.5 = (s32[4]{0:T(128)S(1)}, s32[4]{0:T(128)}, u32[]{:S(2)}) copy-start(s32[4]{0:T(128)} %param.12) | copy-start | bytes 52
  2.2 3.3 %copy-start.6 = (s32[8]{0:T(128)S(1)}, s32[8]{0:T(128)}, u32[]{:S(2)}) copy-start(s32[8]{0:T(128)} %param.11) | copy-start | bytes 100
  2.3 16.4 %copy-start.2 = (bf16[2,2048,64]{1,2,0:T(8,128)(2,1)S(1)}, bf16[2,2048,64]{1,2,0:T(8,128)(2,1)}, u32[]{:S(2)}) copy-start(bf16[2,2048,64]{1,2,0:T(8,128)(2,1)} %param.9) | copy-start | bytes 1572868
  2.3 16.4 %collective-permute-start = (bf16[2304,128]{1,0:T(8,128)(2,1)S(1)}, bf16[2304,128]{1,0:T(8,128)(2,1)S(1)}, u32[]{:S(2)}, u32[]{:S(2)}) collective-permute-start(bf16[2304,128]{1,0:T(8,128)(2,1)S(1)} %pack_columns.1.refs_0_.refs_2_), channel_id=1, source_target_pairs={{0,4},{1,5},{2,6},{3,7},{4,0},{5,1},{6,2},{7,3},{8,12},{9,13},{10,... | collective-permute-start | bytes 1769480 | tf_op jit(solution)/shard_map/ppermute | solution.py:64
  5.4 13.6 %collective-permute-start.1 = (bf16[2304,128]{1,0:T(8,128)(2,1)S(1)}, bf16[2304,128]{1,0:T(8,128)(2,1)S(1)}, u32[]{:S(2)}, u32[]{:S(2)}) collective-permute-start(bf16[2304,128]{1,0:T(8,128)(2,1)S(1)} %pack_columns.1.refs_0_.refs_2_), channel_id=1, source_target_pairs={{0,1},{1,0},{2,3},{3,2},{4,8},{5,9},{6,10},{7,11},{8,4},{9,5},{10,... | collective-permute-start | bytes 1769480 | tf_op jit(solution)/shard_map/ppermute | solution.py:64
  6.3 30.5 %collective-permute-start.5 = (bf16[272,2048]{1,0:T(8,128)(2,1)S(1)}, bf16[272,2048]{1,0:T(8,128)(2,1)S(1)}, u32[]{:S(2)}, u32[]{:S(2)}) collective-permute-start(bf16[272,2048]{1,0:T(8,128)(2,1)S(1)} %sort_blocks.1.refs_0_), channel_id=1, source_target_pairs={{0,16},{1,17},{2,18},{3,19},{4,20},{5,21},{6,22},{7,23},{8,24},{9,... | collective-permute-start | bytes 3342344 | tf_op jit(solution)/shard_map/ppermute | solution.py:64
  18.8 3.8 %collective-permute-start.2 = (bf16[2304,128]{1,0:T(8,128)(2,1)S(1)}, bf16[2304,128]{1,0:T(8,128)(2,1)S(1)}, u32[]{:S(2)}, u32[]{:S(2)}) collective-permute-start(bf16[2304,128]{1,0:T(8,128)(2,1)S(1)} %collective-permute-done.refs_1_.refs_3_), channel_id=1, source_target_pairs={{0,1},{1,0},{2,3},{3,2},{4,8},{5,9},{6,10},{7,11},{8,4},{9,5},{10,... | collective-permute-start | bytes 1769480 | tf_op jit(solution)/shard_map/ppermute | solution.py:64
  19.1 19.3 %collective-permute-start.3 = (bf16[2304,128]{1,0:T(8,128)(2,1)S(1)}, bf16[2304,128]{1,0:T(8,128)(2,1)S(1)}, u32[]{:S(2)}, u32[]{:S(2)}) collective-permute-start(bf16[2304,128]{1,0:T(8,128)(2,1)S(1)} %choose.2), channel_id=1, source_target_pairs={{0,4},{1,5},{2,6},{3,7},{4,0},{5,1},{6,2},{7,3},{8,12},{9,13},{10,... | collective-permute-start | bytes 1769480 | tf_op jit(solution)/shard_map/ppermute | solution.py:64
  22.5 14.3 %collective-permute-start.6 = (bf16[1024,128]{1,0:T(8,128)(2,1)S(1)}, bf16[1024,128]{1,0:T(8,128)(2,1)S(1)}, u32[]{:S(2)}, u32[]{:S(2)}) collective-permute-start(bf16[1024,128]{1,0:T(8,128)(2,1)S(1)} %get-tuple-element.27.refs_6_), channel_id=1, source_target_pairs={{0,1},{1,0},{2,3},{3,2},{4,8},{5,9},{6,10},{7,11},{8,4},{9,5},{10,... | collective-permute-start | bytes 786440 | tf_op jit(solution)/shard_map/ppermute | solution.py:64
  22.6 25.8 %collective-permute-start.4 = (bf16[2304,128]{1,0:T(8,128)(2,1)S(1)}, bf16[2304,128]{1,0:T(8,128)(2,1)S(1)}, u32[]{:S(2)}, u32[]{:S(2)}) collective-permute-start(bf16[2304,128]{1,0:T(8,128)(2,1)S(1)} %choose.3), channel_id=1, source_target_pairs={{0,4},{1,5},{2,6},{3,7},{4,0},{5,1},{6,2},{7,3},{8,12},{9,13},{10,... | collective-permute-start | bytes 1769480 | tf_op jit(solution)/shard_map/ppermute | solution.py:64
  36.9 6.9 %collective-permute-start.7 = (bf16[1024,128]{1,0:T(8,128)(2,1)S(1)}, bf16[1024,128]{1,0:T(8,128)(2,1)S(1)}, u32[]{:S(2)}, u32[]{:S(2)}) collective-permute-start(bf16[1024,128]{1,0:T(8,128)(2,1)S(1)} %collective-permute-done.6.refs_4_), channel_id=1, source_target_pairs={{0,16},{1,17},{2,18},{3,19},{4,20},{5,21},{6,22},{7,23},{8,24},{9,... | collective-permute-start | bytes 786440 | tf_op jit(solution)/shard_map/ppermute | solution.py:64
  38.4 5.3 %collective-permute-start.9 = (bf16[1024,128]{1,0:T(8,128)(2,1)S(1)}, bf16[1024,128]{1,0:T(8,128)(2,1)S(1)}, u32[]{:S(2)}, u32[]{:S(2)}) collective-permute-start(bf16[1024,128]{1,0:T(8,128)(2,1)S(1)} %slice.4), channel_id=1, source_target_pairs={{0,1},{1,0},{2,3},{3,2},{4,8},{5,9},{6,10},{7,11},{8,4},{9,5},{10,... | collective-permute-start | bytes 786440 | tf_op jit(solution)/shard_map/ppermute | solution.py:64
  43.8 6.8 %collective-permute-start.10 = (bf16[1024,128]{1,0:T(8,128)(2,1)S(1)}, bf16[1024,128]{1,0:T(8,128)(2,1)S(1)}, u32[]{:S(2)}, u32[]{:S(2)}) collective-permute-start(bf16[1024,128]{1,0:T(8,128)(2,1)S(1)} %collective-permute-done.9.refs_4_), channel_id=1, source_target_pairs={{0,16},{1,17},{2,18},{3,19},{4,20},{5,21},{6,22},{7,23},{8,24},{9,... | collective-permute-start | bytes 786440 | tf_op jit(solution)/shard_map/ppermute | solution.py:64
  49.3 2.9 %collective-permute-start.8 = (bf16[1024,128]{1,0:T(8,128)(2,1)S(1)}, bf16[1024,128]{1,0:T(8,128)(2,1)S(1)}, u32[]{:S(2)}, u32[]{:S(2)}) collective-permute-start(bf16[1024,128]{1,0:T(8,128)(2,1)S(1)} %get-tuple-element.33), channel_id=1, source_target_pairs={{0,1},{1,0},{2,3},{3,2},{4,5},{5,4},{6,7},{7,6},{8,9},{9,8},{10,11... | collective-permute-start | bytes 786440 | tf_op jit(solution)/shard_map/ppermute | solution.py:64
  50.7 1.4 %collective-permute-start.11 = (bf16[384,128]{1,0:T(8,128)(2,1)S(1)}, bf16[384,128]{1,0:T(8,128)(2,1)S(1)}, u32[]{:S(2)}, u32[]{:S(2)}) collective-permute-start(bf16[384,128]{1,0:T(8,128)(2,1)S(1)} %get-tuple-element.37), channel_id=1, source_target_pairs={{0,1},{1,0},{2,3},{3,2},{4,5},{5,4},{6,7},{7,6},{8,9},{9,8},{10,11... | collective-permute-start | bytes 294920 | tf_op jit(solution)/shard_map/ppermute | solution.py:64
  52.2 12.9 %collective-permute-start.12 = (bf16[384,128]{1,0:T(8,128)(2,1)S(1)}, bf16[384,128]{1,0:T(8,128)(2,1)S(1)}, u32[]{:S(2)}, u32[]{:S(2)}) collective-permute-start(bf16[384,128]{1,0:T(8,128)(2,1)S(1)} %get-tuple-element.39), channel_id=1, source_target_pairs={{0,2},{1,3},{2,0},{3,1},{4,6},{5,7},{6,4},{7,5},{8,10},{9,11},{10,... | collective-permute-start | bytes 294920 | tf_op jit(solution)/shard_map/ppermute | solution.py:64
  53.7 11.4 %collective-permute-start.13 = (bf16[384,128]{1,0:T(8,128)(2,1)S(1)}, bf16[384,128]{1,0:T(8,128)(2,1)S(1)}, u32[]{:S(2)}, u32[]{:S(2)}) collective-permute-start(bf16[384,128]{1,0:T(8,128)(2,1)S(1)} %get-tuple-element.40), channel_id=1, source_target_pairs={{0,16},{1,17},{2,18},{3,19},{4,20},{5,21},{6,22},{7,23},{8,24},{9,... | collective-permute-start | bytes 294920 | tf_op jit(solution)/shard_map/ppermute | solution.py:64
  55.8 9.3 %collective-permute-start.14 = (bf16[384,128]{1,0:T(8,128)(2,1)S(1)}, bf16[384,128]{1,0:T(8,128)(2,1)S(1)}, u32[]{:S(2)}, u32[]{:S(2)}) collective-permute-start(bf16[384,128]{1,0:T(8,128)(2,1)S(1)} %get-tuple-element.41), channel_id=1, source_target_pairs={{0,18},{1,19},{2,16},{3,17},{4,22},{5,23},{6,20},{7,21},{8,26},{9,... | collective-permute-start | bytes 294920 | tf_op jit(solution)/shard_map/ppermute | solution.py:64
  55.8 6.4 %collective-permute-start.15 = (bf16[128,128]{1,0:T(8,128)(2,1)S(1)}, bf16[128,128]{1,0:T(8,128)(2,1)S(1)}, u32[]{:S(2)}, u32[]{:S(2)}) collective-permute-start(bf16[128,128]{1,0:T(8,128)(2,1)S(1)} %get-tuple-element.42), channel_id=1, source_target_pairs={{0,4},{1,5},{2,6},{3,7},{4,0},{5,1},{6,2},{7,3},{8,12},{9,13},{10,... | collective-permute-start | bytes 98312 | tf_op jit(solution)/shard_map/ppermute | solution.py:64
  60.3 4.8 %collective-permute-start.16 = (bf16[128,128]{1,0:T(8,128)(2,1)S(1)}, bf16[128,128]{1,0:T(8,128)(2,1)S(1)}, u32[]{:S(2)}, u32[]{:S(2)}) collective-permute-start(bf16[128,128]{1,0:T(8,128)(2,1)S(1)} %get-tuple-element.42), channel_id=1, source_target_pairs={{0,6},{1,7},{2,4},{3,5},{4,2},{5,3},{6,0},{7,1},{8,14},{9,15},{10,... | collective-permute-start | bytes 98312 | tf_op jit(solution)/shard_map/ppermute | solution.py:64

commit v6 on v5

--- a/solution.py
+++ b/solution.py
@@ -100,35 +100,13 @@
             local_slot = jnp.where(hit, s % per_dev, local_slot)
         return which, local_slot
 
-    def pack_columns(ints_ref, w_ref, u_ref, wide_ref, sems):
-        me = ints_ref[0]
-        cols = pl.ds(pl.multiple_of(me * half_cols, LANES), half_cols)
-        copies = [
-            pltpu.make_async_copy(w_ref.at[:, cols], wide_ref.at[pl.ds(0, feats)], sems.at[0]),
+    mine_at = lax.axis_index("groups") * half_cols
+    up_tiles = up.reshape(per_dev, rank, col_tiles, LANES).transpose(0, 2, 1, 3)
+    own_w = jnp.concatenate(
+        [
+            lax.dynamic_slice_in_dim(value_weight, mine_at, half_cols, 1),
+            up_tiles.reshape(up_rows, LANES),
         ]
-        for s in range(per_dev):
-            for v in range(col_tiles):
-                n = s * col_tiles + v
-                copies.append(
-                    pltpu.make_async_copy(
-                        u_ref.at[s, :, pl.ds(v * LANES, LANES)],
-                        wide_ref.at[pl.ds(feats + n * rank, rank)],
-                        sems.at[1 + n],
-                    )
-                )
-        for c in copies:
-            c.start()
-        for c in copies:
-            c.wait()
-
-    own_w = call(
-        pack_columns,
-        "pack_columns",
-        like(feats + up_rows, LANES),
-        [HBM, HBM],
-        (value_weight, up),
-        [pltpu.SemaphoreType.DMA((1 + per_dev * col_tiles,))],
-        mib=16,
     )
 
     tiles = feats // LANES
@@ -388,12 +366,24 @@
     from_y = to_group(to_y)
     from_near = to_neighbour(to_near)
 
-    def ups(ints_ref, own, near, mid, far, out2, out3, out):
+    def ups(ints_ref, info_ref, own, near, mid, far, out2, out3, up_ref, mark_ref):
         here = ints_ref[1]
         is_outer = outer_plane(here)
 
+        live_at = dp * blocks
+        found = []
+        for slot in range(dp):
+            which, local_slot = block_at(info_ref, where_from(here, slot))
+            found.append(local_slot)
+            for k in range(blocks):
+                at = slot * blocks + k
+                mark_ref[at : at + 1, :] = jnp.full((1, LANES), (which == k).astype(F32), F32)
+            live = info_ref[adapters + blocks + which].astype(F32)
+            mark_ref[live_at + slot : live_at + slot + 1, :] = jnp.full((1, LANES), live, F32)
+
         def put(ref, slot):
-            out[where_from(here, slot)] = ref[feats : feats + up_rows, :]
+            at = feats + found[slot] * col_tiles * rank
+            up_ref[slot] = ref[pl.ds(pl.multiple_of(at, col_tiles * rank), col_tiles * rank), :]
 
         put(own, 0)
         put(near, 1)
@@ -408,19 +398,22 @@
             put(mid, 2)
             put(far, 3)
 
-    up_all = call(
+    up_used, marks = call(
         ups,
         "ups",
-        jax.ShapeDtypeStruct((dp, up_rows, LANES), BF16),
-        [VMEM] * 6,
-        (own_w, near_w, mid_w, far_w, two, three),
+        (
+            jax.ShapeDtypeStruct((dp, col_tiles * rank, LANES), BF16),
+            like(dp * blocks + 2 * dp, LANES, F32),
+        ),
+        [SMEM] + [VMEM] * 6,
+        (info, own_w, near_w, mid_w, far_w, two, three),
     )
 
     def finish(
-        ints_ref, info_ref, up_ref, mine_ref, x_ref, y_ref, d_ref, n_ref,
+        ints_ref, mark_ref, up_ref, mine_ref, x_ref, y_ref, d_ref, n_ref,
         nx_ref, out_ref,
     ):
-        me, here = ints_ref[0], ints_ref[1]
+        me = ints_ref[0]
         ours = mine_ref[0:rows, :] + x_ref[0:rows, :].astype(F32)
         theirs = y_ref[0:rows, :].astype(F32) + d_ref[0:rows, :].astype(F32)
         split = (jnp.where(me == 0, ours, theirs), jnp.where(me == 0, theirs, ours))
@@ -429,29 +422,38 @@
             s = s + ref[rows:, :].astype(F32)
         s = s.astype(BF16)
         per_lane = dp // 2
-        row = lax.broadcasted_iota(jnp.int32, (block_len, LANES), 0)
+        row = lax.broadcasted_iota(jnp.int32, (block_len, LANES), 0).astype(F32)
+        results = [[None] * col_tiles for _ in range(blocks)]
         for slot in range(dp):
-            holder = where_from(here, slot)
-            which, local_slot = block_at(info_ref, holder)
             piece = s[
                 (slot % per_lane) * block_len : (slot % per_lane + 1) * block_len,
                 (slot // per_lane) * rank : (slot // per_lane + 1) * rank,
             ]
-            to = pl.ds(pl.multiple_of(which * block_len, block_len), block_len)
+            live_at = dp * blocks + slot
+            live = row < mark_ref[live_at : live_at + 1, :]
             for v in range(col_tiles):
-                at = pl.ds(pl.multiple_of((local_slot * col_tiles + v) * rank, rank), rank)
-                delta = jnp.dot(piece, up_ref[holder, at, :], preferred_element_type=F32)
+                weight = up_ref[slot, v * rank : (v + 1) * rank, :]
+                delta = jnp.dot(piece, weight, preferred_element_type=F32)
                 base = split[v][slot * block_len : (slot + 1) * block_len, :]
-                mixed = jnp.where(row < info_ref[adapters + blocks + which], base + delta.astype(BF16).astype(F32), 0.0)
-                out_ref[to, v * LANES : (v + 1) * LANES] = mixed.astype(BF16)
+                mixed = jnp.where(live, base + delta.astype(BF16).astype(F32), 0.0)
+                for k in range(blocks):
+                    at = slot * blocks + k
+                    hit = mark_ref[at : at + 1, :] > 0.5
+                    before = results[k][v]
+                    results[k][v] = mixed if before is None else jnp.where(hit, mixed, before)
+        for k in range(blocks):
+            for v in range(col_tiles):
+                out_ref[
+                    k * block_len : (k + 1) * block_len, v * LANES : (v + 1) * LANES
+                ] = results[k][v].astype(BF16)
 
     return call(
         finish,
         "finish",
         like(rows, out_cols),
-        [SMEM] + [VMEM] * 7,
+        [VMEM] * 8,
         (
-            info, up_all, mine, from_x, from_y, from_d,
+            marks, up_used, mine, from_x, from_y, from_d,
             from_near, from_nearx,
         ),
     )

time: 66.7 us -> 65.2 us (0.978)
  local copies, waits for them, and re-layouts: 2.19 us -> 1.33 us
    unnamed x14 -> x12, local copies, waits for them, and re-layouts: 2.17 us -> 0.33 us
    reshape x0 -> x1, local copies, waits for them, and re-layouts: none -> 0.94 us  [local_line(): up_tiles = up.reshape(per_dev, rank, col_tiles, LANES).transpose(0, 2, 1, 3)]
    pallas_call x11 -> x10, Pallas kernels: 6.03 us -> 5.98 us  [call(): pl.pallas_call(lambda *refs: body(Place(), *refs), name=name, out_shape=o...]
  transfers between devices with their start and end apart: 17 -> 17, of which waited for: 6 -> 6; matrix products, arithmetic and copies ran while one was open for 0% -> 0% of each run, Pallas kernels for 7% -> 8%
where the time goes in v6:
time: 65.2 us; the launch traced here: 65 us
  starting transfers between devices  35.6 us (55%)
  waiting for transfers between devices  21.9 us (34%)
  Pallas kernels  5.98 us (9%)
  local copies, waits for them, and re-layouts  1.33 us (2%)
    ppermute x17, starting transfers between devices, swap(): return lax.ppermute(x, AXES, perm)  35.6 us
    ppermute x17, waiting for transfers between devices, swap(): return lax.ppermute(x, AXES, perm)  21.9 us
    pallas_call x10, Pallas kernels, call(): pl.pallas_call(lambda *refs: body(Place(), *refs), name=name, out_shape=o...  5.98 us
  transfers between devices with their start and end apart: 17, of which 6 were waited for; matrix products, arithmetic and copies ran while one was open for 0% of the time, Pallas kernels for 8%

profile of v6, /device:TPU:0, one launch (start us, length us, event | category | flops | bytes accessed | tf_op | source)
XLA Modules:
  0.0 65.0 jit_solution(2328444631203195899)
XLA Ops:
  0.0 0.9 %copy_bitcast_fusion = bf16[2,64,2,128]{3,1,2,0:T(8,128)(2,1)S(1)} fusion(bf16[2,64,256]{2,1,0:T(8,128)(2,1)} %param.10), kind=kLoop, calls=%fused_computation.1 | loop fusion | bytes 131072 | tf_op jit(solution)/shard_map/reshape | solution.py:104
  0.9 0.3 copy-done
  1.4 0.0 copy-start.2
  1.4 3.1 %collective-permute-start = (bf16[2304,128]{1,0:T(8,128)(2,1)S(1)}, bf16[2304,128]{1,0:T(8,128)(2,1)S(1)}, u32[]{:S(2)}, u32[]{:S(2)}) collective-permute-start(bf16[2304,128]{1,0:T(8,128)(2,1)S(1)} %pad_maximum_fusion.refs_1_.refs_2_), channel_id=1, source_target_pairs={{0,4},{1,5},{2,6},{3,7},{4,0},{5,1},{6,2},{7,3},{8,12},{9,13},{10,... | collective-permute-start | bytes 1769480 | tf_op jit(solution)/shard_map/ppermute | solution.py:64
  4.5 0.1 pad_add_fusion.refs_0_
  4.6 0.8 %sort_blocks.1.refs_0_ = bf16[272,2048]{1,0:T(8,128)(2,1)S(1)} custom-call(s32[16]{0:T(128)S(1)} %pad_add_fusion.refs_0_, bf16[256,2048]{1,0:T(8,128)(2,1)S(1)} %copy-done.1), custom_call_target="tpu_custom_call" | custom-call | tf_op jit(solution)/shard_map/sort_blocks/pallas_call | solution.py:24
  5.4 1.6 %collective-permute-start.5 = (bf16[272,2048]{1,0:T(8,128)(2,1)S(1)}, bf16[272,2048]{1,0:T(8,128)(2,1)S(1)}, u32[]{:S(2)}, u32[]{:S(2)}) collective-permute-start(bf16[272,2048]{1,0:T(8,128)(2,1)S(1)} %sort_blocks.1.refs_0_), channel_id=1, source_target_pairs={{0,16},{1,17},{2,18},{3,19},{4,20},{5,21},{6,22},{7,23},{8,24},{9,... | collective-permute-start | bytes 3342344 | tf_op jit(solution)/shard_map/ppermute | solution.py:64
  7.0 10.8 %collective-permute-done.refs_2_.refs_3_ = bf16[2304,128]{1,0:T(8,128)(2,1)S(1)} collective-permute-done((bf16[2304,128]{1,0:T(8,128)(2,1)S(1)}, bf16[2304,128]{1,0:T(8,128)(2,1)S(1)}, u32[]{:S(2)}, u32[]{:S(2)}) %collective-permute-start) | collective-permute-done | bytes 589856 | tf_op jit(solution)/shard_map/ppermute | solution.py:64
  17.8 0.3 pack_shrinks.1
  18.1 0.1 choose.2
  18.2 3.4 %collective-permute-start.3 = (bf16[2304,128]{1,0:T(8,128)(2,1)S(1)}, bf16[2304,128]{1,0:T(8,128)(2,1)S(1)}, u32[]{:S(2)}, u32[]{:S(2)}) collective-permute-start(bf16[2304,128]{1,0:T(8,128)(2,1)S(1)} %choose.2), channel_id=1, source_target_pairs={{0,4},{1,5},{2,6},{3,7},{4,0},{5,1},{6,2},{7,3},{8,12},{9,13},{10,... | collective-permute-start | bytes 1769480 | tf_op jit(solution)/shard_map/ppermute | solution.py:64
  21.6 14.3 %collective-permute-start.4 = (bf16[2304,128]{1,0:T(8,128)(2,1)S(1)}, bf16[2304,128]{1,0:T(8,128)(2,1)S(1)}, u32[]{:S(2)}, u32[]{:S(2)}) collective-permute-start(bf16[2304,128]{1,0:T(8,128)(2,1)S(1)} %choose.3), channel_id=1, source_target_pairs={{0,4},{1,5},{2,6},{3,7},{4,0},{5,1},{6,2},{7,3},{8,12},{9,13},{10,... | collective-permute-start | bytes 1769480 | tf_op jit(solution)/shard_map/ppermute | solution.py:64
  35.9 1.5 %collective-permute-start.7 = (bf16[1024,128]{1,0:T(8,128)(2,1)S(1)}, bf16[1024,128]{1,0:T(8,128)(2,1)S(1)}, u32[]{:S(2)}, u32[]{:S(2)}) collective-permute-start(bf16[1024,128]{1,0:T(8,128)(2,1)S(1)} %collective-permute-done.6.refs_4_), channel_id=1, source_target_pairs={{0,16},{1,17},{2,18},{3,19},{4,20},{5,21},{6,22},{7,23},{8,24},{9,... | collective-permute-start | bytes 786440 | tf_op jit(solution)/shard_map/ppermute | solution.py:64
  37.5 0.1 collective-permute-start.9
  37.5 5.3 %collective-permute-done.7.refs_5_ = bf16[1024,128]{1,0:T(8,128)(2,1)S(1)} collective-permute-done((bf16[1024,128]{1,0:T(8,128)(2,1)S(1)}, bf16[1024,128]{1,0:T(8,128)(2,1)S(1)}, u32[]{:S(2)}, u32[]{:S(2)}) %collective-permute-start.7) | collective-permute-done | bytes 262176 | tf_op jit(solution)/shard_map/ppermute | solution.py:64
  42.8 2.5 %collective-permute-start.10 = (bf16[1024,128]{1,0:T(8,128)(2,1)S(1)}, bf16[1024,128]{1,0:T(8,128)(2,1)S(1)}, u32[]{:S(2)}, u32[]{:S(2)}) collective-permute-start(bf16[1024,128]{1,0:T(8,128)(2,1)S(1)} %collective-permute-done.9.refs_4_), channel_id=1, source_target_pairs={{0,16},{1,17},{2,18},{3,19},{4,20},{5,21},{6,22},{7,23},{8,24},{9,... | collective-permute-start | bytes 786440 | tf_op jit(solution)/shard_map/ppermute | solution.py:64
  45.3 2.1 %early_columns.1 = (f32[1536,128]{1,0:T(8,128)S(1)}, f32[3,256,64]{2,1,0:T(8,128)S(1)}) custom-call(bf16[272,2048]{1,0:T(8,128)(2,1)S(1)} %sort_blocks.1.refs_0_, bf16[272,2048]{1,0:T(8,128)(2,1)S(1)} %collective-permute-done.5.refs_1_, bf16[2304,128]{1,0:T(8,128)(2,1)S(1)} %pad_maximum_fusion.refs_1_.refs_2_, ...), custom_call_target="tpu_custom_call" | custom-call | tf_op jit(solution)/shard_map/early_columns/pallas_call | solution.py:24
  47.4 0.8 %last_columns.1 = (f32[1024,128]{1,0:T(8,128)S(1)}, bf16[1024,128]{1,0:T(8,128)(2,1)S(1)}, f32[3,256,64]{2,1,0:T(8,128)S(1)}) custom-call(bf16[272,2048]{1,0:T(8,128)(2,1)S(1)} %sort_blocks.1.refs_0_, bf16[272,2048]{1,0:T(8,128)(2,1)S(1)} %collective-permute-done.5.refs_1_, bf16[2304,128]{1,0:T(8,128)(2,1)S(1)} %collective-permute-done.3.refs_5_.refs_2_, ...), custom_call_target="tpu_custom_call" | custom-call | tf_op jit(solution)/shard_map/last_columns/pallas_call | solution.py:24
  48.3 0.1 collective-permute-start.8
  48.4 1.3 %collective-permute-done.10.refs_5_ = bf16[1024,128]{1,0:T(8,128)(2,1)S(1)} collective-permute-done((bf16[1024,128]{1,0:T(8,128)(2,1)S(1)}, bf16[1024,128]{1,0:T(8,128)(2,1)S(1)}, u32[]{:S(2)}, u32[]{:S(2)}) %collective-permute-start.10) | collective-permute-done | bytes 262176 | tf_op jit(solution)/shard_map/ppermute | solution.py:64
  49.6 0.1 last_shrinks.1
  49.8 0.1 collective-permute-start.11
  49.9 1.3 %collective-permute-done.11.refs_3_ = bf16[384,128]{1,0:T(8,128)(2,1)S(1)} collective-permute-done((bf16[384,128]{1,0:T(8,128)(2,1)S(1)}, bf16[384,128]{1,0:T(8,128)(2,1)S(1)}, u32[]{:S(2)}, u32[]{:S(2)}) %collective-permute-start.11) | collective-permute-done | bytes 98336 | tf_op jit(solution)/shard_map/ppermute | solution.py:64
  51.1 0.1 add_cores.1
  51.2 1.6 %collective-permute-start.12 = (bf16[384,128]{1,0:T(8,128)(2,1)S(1)}, bf16[384,128]{1,0:T(8,128)(2,1)S(1)}, u32[]{:S(2)}, u32[]{:S(2)}) collective-permute-start(bf16[384,128]{1,0:T(8,128)(2,1)S(1)} %get-tuple-element.43), channel_id=1, source_target_pairs={{0,2},{1,3},{2,0},{3,1},{4,6},{5,7},{6,4},{7,5},{8,10},{9,11},{10,... | collective-permute-start | bytes 294920 | tf_op jit(solution)/shard_map/ppermute | solution.py:64
  52.8 2.0 %collective-permute-start.13 = (bf16[384,128]{1,0:T(8,128)(2,1)S(1)}, bf16[384,128]{1,0:T(8,128)(2,1)S(1)}, u32[]{:S(2)}, u32[]{:S(2)}) collective-permute-start(bf16[384,128]{1,0:T(8,128)(2,1)S(1)} %get-tuple-element.44), channel_id=1, source_target_pairs={{0,16},{1,17},{2,18},{3,19},{4,20},{5,21},{6,22},{7,23},{8,24},{9,... | collective-permute-start | bytes 294920 | tf_op jit(solution)/shard_map/ppermute | solution.py:64
  54.8 4.5 %collective-permute-start.15 = (bf16[128,128]{1,0:T(8,128)(2,1)S(1)}, bf16[128,128]{1,0:T(8,128)(2,1)S(1)}, u32[]{:S(2)}, u32[]{:S(2)}) collective-permute-start(bf16[128,128]{1,0:T(8,128)(2,1)S(1)} %get-tuple-element.46), channel_id=1, source_target_pairs={{0,4},{1,5},{2,6},{3,7},{4,0},{5,1},{6,2},{7,3},{8,12},{9,13},{10,... | collective-permute-start | bytes 98312 | tf_op jit(solution)/shard_map/ppermute | solution.py:64
  59.3 0.9 %collective-permute-start.16 = (bf16[128,128]{1,0:T(8,128)(2,1)S(1)}, bf16[128,128]{1,0:T(8,128)(2,1)S(1)}, u32[]{:S(2)}, u32[]{:S(2)}) collective-permute-start(bf16[128,128]{1,0:T(8,128)(2,1)S(1)} %get-tuple-element.46), channel_id=1, source_target_pairs={{0,6},{1,7},{2,4},{3,5},{4,2},{5,3},{6,0},{7,1},{8,14},{9,15},{10,... | collective-permute-start | bytes 98312 | tf_op jit(solution)/shard_map/ppermute | solution.py:64
  60.2 0.7 %ups.1 = (bf16[4,128,128]{2,1,0:T(8,128)(2,1)S(1)}, f32[24,128]{1,0:T(8,128)S(1)}) custom-call(s32[16]{0:T(128)S(1)} %pad_add_fusion.refs_0_, bf16[2304,128]{1,0:T(8,128)(2,1)S(1)} %pad_maximum_fusion.refs_1_.refs_2_, bf16[2304,128]{1,0:T(8,128)(2,1)S(1)} %collective-permute-done.refs_2_.refs_3_, ...), custom_call_target="tpu_custom_call" | custom-call | tf_op jit(solution)/shard_map/ups/pallas_call | solution.py:24
  60.9 0.3 collective-permute-done.15.refs_6_
  61.2 2.9 %collective-permute-done.16.refs_7_ = bf16[128,128]{1,0:T(8,128)(2,1)S(1)} collective-permute-done((bf16[128,128]{1,0:T(8,128)(2,1)S(1)}, bf16[128,128]{1,0:T(8,128)(2,1)S(1)}, u32[]{:S(2)}, u32[]{:S(2)}) %collective-permute-start.16) | collective-permute-done | bytes 32800 | tf_op jit(solution)/shard_map/ppermute | solution.py:64
  64.1 0.9 %finish.1 = bf16[256,256]{1,0:T(8,128)(2,1)} custom-call(f32[24,128]{1,0:T(8,128)S(1)} %get-tuple-element.28.refs_0_, bf16[4,128,128]{2,1,0:T(8,128)(2,1)S(1)} %get-tuple-element.29.refs_1_, f32[384,128]{1,0:T(8,128)S(1)} %get-tuple-element.42.refs_2_, bf16[384,128]{1,0:T(8,128)(2,1)S(1)} %collective-permute-done.12.refs_3_, ...), custom_call_target="tpu_custom_call" | custom-call | tf_op jit(solution)/shard_map/finish/pallas_call | solution.py:24
  (29 shorter events, 0.2 us)
Async XLA Ops:
  0.0 1.3 %copy-start = (bf16[2048,256]{1,0:T(8,128)(2,1)S(1)}, bf16[2048,256]{1,0:T(8,128)(2,1)}, u32[]{:S(2)}) copy-start(bf16[2048,256]{1,0:T(8,128)(2,1)} %param.8) | copy-start | bytes 3145732
  1.3 3.2 %copy-start.3 = (s32[4]{0:T(128)S(1)}, s32[4]{0:T(128)}, u32[]{:S(2)}) copy-start(s32[4]{0:T(128)} %param.13) | copy-start | bytes 52
  1.3 3.2 %copy-start.4 = (s32[4]{0:T(128)S(1)}, s32[4]{0:T(128)}, u32[]{:S(2)}) copy-start(s32[4]{0:T(128)} %param.12) | copy-start | bytes 52
  1.3 3.2 %copy-start.5 = (s32[8]{0:T(128)S(1)}, s32[8]{0:T(128)}, u32[]{:S(2)}) copy-start(s32[8]{0:T(128)} %param.11) | copy-start | bytes 100
  1.3 3.3 %copy-start.1 = (bf16[256,2048]{1,0:T(8,128)(2,1)S(1)}, bf16[256,2048]{1,0:T(8,128)(2,1)}, u32[]{:S(2)}) copy-start(bf16[256,2048]{1,0:T(8,128)(2,1)} %refs_1_.1) | copy-start | bytes 3145732
  1.4 16.4 %copy-start.2 = (bf16[2,2048,64]{1,2,0:T(8,128)(2,1)S(1)}, bf16[2,2048,64]{1,2,0:T(8,128)(2,1)}, u32[]{:S(2)}) copy-start(bf16[2,2048,64]{1,2,0:T(8,128)(2,1)} %param.9) | copy-start | bytes 1572868
  1.4 16.4 %collective-permute-start = (bf16[2304,128]{1,0:T(8,128)(2,1)S(1)}, bf16[2304,128]{1,0:T(8,128)(2,1)S(1)}, u32[]{:S(2)}, u32[]{:S(2)}) collective-permute-start(bf16[2304,128]{1,0:T(8,128)(2,1)S(1)} %pad_maximum_fusion.refs_1_.refs_2_), channel_id=1, source_target_pairs={{0,4},{1,5},{2,6},{3,7},{4,0},{5,1},{6,2},{7,3},{8,12},{9,13},{10,... | collective-permute-start | bytes 1769480 | tf_op jit(solution)/shard_map/ppermute | solution.py:64
  4.5 13.6 %collective-permute-start.1 = (bf16[2304,128]{1,0:T(8,128)(2,1)S(1)}, bf16[2304,128]{1,0:T(8,128)(2,1)S(1)}, u32[]{:S(2)}, u32[]{:S(2)}) collective-permute-start(bf16[2304,128]{1,0:T(8,128)(2,1)S(1)} %pad_maximum_fusion.refs_1_.refs_2_), channel_id=1, source_target_pairs={{0,1},{1,0},{2,3},{3,2},{4,8},{5,9},{6,10},{7,11},{8,4},{9,5},{10,... | collective-permute-start | bytes 1769480 | tf_op jit(solution)/shard_map/ppermute | solution.py:64
  5.4 30.5 %collective-permute-start.5 = (bf16[272,2048]{1,0:T(8,128)(2,1)S(1)}, bf16[272,2048]{1,0:T(8,128)(2,1)S(1)}, u32[]{:S(2)}, u32[]{:S(2)}) collective-permute-start(bf16[272,2048]{1,0:T(8,128)(2,1)S(1)} %sort_blocks.1.refs_0_), channel_id=1, source_target_pairs={{0,16},{1,17},{2,18},{3,19},{4,20},{5,21},{6,22},{7,23},{8,24},{9,... | collective-permute-start | bytes 3342344 | tf_op jit(solution)/shard_map/ppermute | solution.py:64
  17.8 3.8 %collective-permute-start.2 = (bf16[2304,128]{1,0:T(8,128)(2,1)S(1)}, bf16[2304,128]{1,0:T(8,128)(2,1)S(1)}, u32[]{:S(2)}, u32[]{:S(2)}) collective-permute-start(bf16[2304,128]{1,0:T(8,128)(2,1)S(1)} %collective-permute-done.refs_2_.refs_3_), channel_id=1, source_target_pairs={{0,1},{1,0},{2,3},{3,2},{4,8},{5,9},{6,10},{7,11},{8,4},{9,5},{10,... | collective-permute-start | bytes 1769480 | tf_op jit(solution)/shard_map/ppermute | solution.py:64
  18.2 19.3 %collective-permute-start.3 = (bf16[2304,128]{1,0:T(8,128)(2,1)S(1)}, bf16[2304,128]{1,0:T(8,128)(2,1)S(1)}, u32[]{:S(2)}, u32[]{:S(2)}) collective-permute-start(bf16[2304,128]{1,0:T(8,128)(2,1)S(1)} %choose.2), channel_id=1, source_target_pairs={{0,4},{1,5},{2,6},{3,7},{4,0},{5,1},{6,2},{7,3},{8,12},{9,13},{10,... | collective-permute-start | bytes 1769480 | tf_op jit(solution)/shard_map/ppermute | solution.py:64
  21.6 14.3 %collective-permute-start.6 = (bf16[1024,128]{1,0:T(8,128)(2,1)S(1)}, bf16[1024,128]{1,0:T(8,128)(2,1)S(1)}, u32[]{:S(2)}, u32[]{:S(2)}) collective-permute-start(bf16[1024,128]{1,0:T(8,128)(2,1)S(1)} %get-tuple-element.31.refs_6_), channel_id=1, source_target_pairs={{0,1},{1,0},{2,3},{3,2},{4,8},{5,9},{6,10},{7,11},{8,4},{9,5},{10,... | collective-permute-start | bytes 786440 | tf_op jit(solution)/shard_map/ppermute | solution.py:64
  21.6 25.8 %collective-permute-start.4 = (bf16[2304,128]{1,0:T(8,128)(2,1)S(1)}, bf16[2304,128]{1,0:T(8,128)(2,1)S(1)}, u32[]{:S(2)}, u32[]{:S(2)}) collective-permute-start(bf16[2304,128]{1,0:T(8,128)(2,1)S(1)} %choose.3), channel_id=1, source_target_pairs={{0,4},{1,5},{2,6},{3,7},{4,0},{5,1},{6,2},{7,3},{8,12},{9,13},{10,... | collective-permute-start | bytes 1769480 | tf_op jit(solution)/shard_map/ppermute | solution.py:64
  35.9 6.9 %collective-permute-start.7 = (bf16[1024,128]{1,0:T(8,128)(2,1)S(1)}, bf16[1024,128]{1,0:T(8,128)(2,1)S(1)}, u32[]{:S(2)}, u32[]{:S(2)}) collective-permute-start(bf16[1024,128]{1,0:T(8,128)(2,1)S(1)} %collective-permute-done.6.refs_4_), channel_id=1, source_target_pairs={{0,16},{1,17},{2,18},{3,19},{4,20},{5,21},{6,22},{7,23},{8,24},{9,... | collective-permute-start | bytes 786440 | tf_op jit(solution)/shard_map/ppermute | solution.py:64
  37.5 5.3 %collective-permute-start.9 = (bf16[1024,128]{1,0:T(8,128)(2,1)S(1)}, bf16[1024,128]{1,0:T(8,128)(2,1)S(1)}, u32[]{:S(2)}, u32[]{:S(2)}) collective-permute-start(bf16[1024,128]{1,0:T(8,128)(2,1)S(1)} %slice.4), channel_id=1, source_target_pairs={{0,1},{1,0},{2,3},{3,2},{4,8},{5,9},{6,10},{7,11},{8,4},{9,5},{10,... | collective-permute-start | bytes 786440 | tf_op jit(solution)/shard_map/ppermute | solution.py:64
  42.8 6.8 %collective-permute-start.10 = (bf16[1024,128]{1,0:T(8,128)(2,1)S(1)}, bf16[1024,128]{1,0:T(8,128)(2,1)S(1)}, u32[]{:S(2)}, u32[]{:S(2)}) collective-permute-start(bf16[1024,128]{1,0:T(8,128)(2,1)S(1)} %collective-permute-done.9.refs_4_), channel_id=1, source_target_pairs={{0,16},{1,17},{2,18},{3,19},{4,20},{5,21},{6,22},{7,23},{8,24},{9,... | collective-permute-start | bytes 786440 | tf_op jit(solution)/shard_map/ppermute | solution.py:64
  48.3 2.9 %collective-permute-start.8 = (bf16[1024,128]{1,0:T(8,128)(2,1)S(1)}, bf16[1024,128]{1,0:T(8,128)(2,1)S(1)}, u32[]{:S(2)}, u32[]{:S(2)}) collective-permute-start(bf16[1024,128]{1,0:T(8,128)(2,1)S(1)} %get-tuple-element.37), channel_id=1, source_target_pairs={{0,1},{1,0},{2,3},{3,2},{4,5},{5,4},{6,7},{7,6},{8,9},{9,8},{10,11... | collective-permute-start | bytes 786440 | tf_op jit(solution)/shard_map/ppermute | solution.py:64
  49.8 1.4 %collective-permute-start.11 = (bf16[384,128]{1,0:T(8,128)(2,1)S(1)}, bf16[384,128]{1,0:T(8,128)(2,1)S(1)}, u32[]{:S(2)}, u32[]{:S(2)}) collective-permute-start(bf16[384,128]{1,0:T(8,128)(2,1)S(1)} %get-tuple-element.41), channel_id=1, source_target_pairs={{0,1},{1,0},{2,3},{3,2},{4,5},{5,4},{6,7},{7,6},{8,9},{9,8},{10,11... | collective-permute-start | bytes 294920 | tf_op jit(solution)/shard_map/ppermute | solution.py:64
  51.2 12.9 %collective-permute-start.12 = (bf16[384,128]{1,0:T(8,128)(2,1)S(1)}, bf16[384,128]{1,0:T(8,128)(2,1)S(1)}, u32[]{:S(2)}, u32[]{:S(2)}) collective-permute-start(bf16[384,128]{1,0:T(8,128)(2,1)S(1)} %get-tuple-element.43), channel_id=1, source_target_pairs={{0,2},{1,3},{2,0},{3,1},{4,6},{5,7},{6,4},{7,5},{8,10},{9,11},{10,... | collective-permute-start | bytes 294920 | tf_op jit(solution)/shard_map/ppermute | solution.py:64
  52.8 11.4 %collective-permute-start.13 = (bf16[384,128]{1,0:T(8,128)(2,1)S(1)}, bf16[384,128]{1,0:T(8,128)(2,1)S(1)}, u32[]{:S(2)}, u32[]{:S(2)}) collective-permute-start(bf16[384,128]{1,0:T(8,128)(2,1)S(1)} %get-tuple-element.44), channel_id=1, source_target_pairs={{0,16},{1,17},{2,18},{3,19},{4,20},{5,21},{6,22},{7,23},{8,24},{9,... | collective-permute-start | bytes 294920 | tf_op jit(solution)/shard_map/ppermute | solution.py:64
  54.8 9.3 %collective-permute-start.14 = (bf16[384,128]{1,0:T(8,128)(2,1)S(1)}, bf16[384,128]{1,0:T(8,128)(2,1)S(1)}, u32[]{:S(2)}, u32[]{:S(2)}) collective-permute-start(bf16[384,128]{1,0:T(8,128)(2,1)S(1)} %get-tuple-element.45), channel_id=1, source_target_pairs={{0,18},{1,19},{2,16},{3,17},{4,22},{5,23},{6,20},{7,21},{8,26},{9,... | collective-permute-start | bytes 294920 | tf_op jit(solution)/shard_map/ppermute | solution.py:64
  54.8 6.4 %collective-permute-start.15 = (bf16[128,128]{1,0:T(8,128)(2,1)S(1)}, bf16[128,128]{1,0:T(8,128)(2,1)S(1)}, u32[]{:S(2)}, u32[]{:S(2)}) collective-permute-start(bf16[128,128]{1,0:T(8,128)(2,1)S(1)} %get-tuple-element.46), channel_id=1, source_target_pairs={{0,4},{1,5},{2,6},{3,7},{4,0},{5,1},{6,2},{7,3},{8,12},{9,13},{10,... | collective-permute-start | bytes 98312 | tf_op jit(solution)/shard_map/ppermute | solution.py:64
  59.3 4.8 %collective-permute-start.16 = (bf16[128,128]{1,0:T(8,128)(2,1)S(1)}, bf16[128,128]{1,0:T(8,128)(2,1)S(1)}, u32[]{:S(2)}, u32[]{:S(2)}) collective-permute-start(bf16[128,128]{1,0:T(8,128)(2,1)S(1)} %get-tuple-element.46), channel_id=1, source_target_pairs={{0,6},{1,7},{2,4},{3,5},{4,2},{5,3},{6,0},{7,1},{8,14},{9,15},{10,... | collective-permute-start | bytes 98312 | tf_op jit(solution)/shard_map/ppermute | solution.py:64

commit v7 on v6

--- a/solution.py
+++ b/solution.py
@@ -45,7 +45,7 @@
     out_cols = up.shape[2]
     half_cols = value_weight.shape[1] // groups
     half = feats // 2
-    up_rows = per_dev * rank * out_cols // LANES
+    up_rows = rank * out_cols // LANES
     col_tiles = out_cols // LANES
     pairs = dp // 2
     both = groups * rows
@@ -100,13 +100,11 @@
             local_slot = jnp.where(hit, s % per_dev, local_slot)
         return which, local_slot
 
-    mine_at = lax.axis_index("groups") * half_cols
-    up_tiles = up.reshape(per_dev, rank, col_tiles, LANES).transpose(0, 2, 1, 3)
+    group = lax.axis_index("groups")
+    up_mine = lax.dynamic_index_in_dim(up, group, 0, keepdims=False)
     own_w = jnp.concatenate(
-        [
-            lax.dynamic_slice_in_dim(value_weight, mine_at, half_cols, 1),
-            up_tiles.reshape(up_rows, LANES),
-        ]
+        [lax.dynamic_slice_in_dim(value_weight, group * half_cols, half_cols, 1)]
+        + [up_mine[:, v * LANES : (v + 1) * LANES] for v in range(col_tiles)]
     )
 
     tiles = feats // LANES
@@ -182,8 +180,9 @@
     far_w = to_middle(near_w)
     mid_d = to_middle(tie(own_d, near_w))
     three = to_neighbour(chosen(second, far_w))
-    mid_e = to_group(tie(mid_d, others))
-    far_d = to_middle(two[0:half])
+    near_d = two[0:half]
+    mid_e = to_group(tie(mid_d, others, near_d))
+    far_d = to_middle(near_d)
     far_e = to_group(tie(far_d, mid_e))
 
     def columns(a_ref, b_ref, w_ref, out_ref, at):
@@ -366,47 +365,63 @@
     from_y = to_group(to_y)
     from_near = to_neighbour(to_near)
 
-    def ups(ints_ref, info_ref, own, near, mid, far, out2, out3, up_ref, mark_ref):
-        here = ints_ref[1]
-        is_outer = outer_plane(here)
-
+    def gather_ups(ints_ref, own, near, mid, far, two, three, out_ref):
+        is_outer = outer_plane(ints_ref[1])
+
+        def put(ref, slot):
+            out_ref[slot * up_rows : (slot + 1) * up_rows, :] = ref[feats : feats + up_rows, :]
+
+        put(own, 0)
+        put(near, 1)
+
+        @pl.when(is_outer)
+        def _():
+            put(two, 2)
+            put(three, 3)
+
+        @pl.when(jnp.logical_not(is_outer))
+        def _():
+            put(mid, 2)
+            put(far, 3)
+
+    ups_mine = call(
+        gather_ups,
+        "gather_ups",
+        like(dp * up_rows, LANES),
+        [VMEM] * 6,
+        (own_w, near_w, mid_w, far_w, two, three),
+    )
+    ups_theirs = to_group(ups_mine)
+
+    def ups(ints_ref, info_ref, mine_ref, theirs_ref, up_ref, mark_ref):
+        me, here = ints_ref[0], ints_ref[1]
         live_at = dp * blocks
-        found = []
         for slot in range(dp):
             which, local_slot = block_at(info_ref, where_from(here, slot))
-            found.append(local_slot)
             for k in range(blocks):
                 at = slot * blocks + k
                 mark_ref[at : at + 1, :] = jnp.full((1, LANES), (which == k).astype(F32), F32)
             live = info_ref[adapters + blocks + which].astype(F32)
             mark_ref[live_at + slot : live_at + slot + 1, :] = jnp.full((1, LANES), live, F32)
-
-        def put(ref, slot):
-            at = feats + found[slot] * col_tiles * rank
-            up_ref[slot] = ref[pl.ds(pl.multiple_of(at, col_tiles * rank), col_tiles * rank), :]
-
-        put(own, 0)
-        put(near, 1)
-
-        @pl.when(is_outer)
-        def _():
-            put(out2, 2)
-            put(out3, 3)
-
-        @pl.when(jnp.logical_not(is_outer))
-        def _():
-            put(mid, 2)
-            put(far, 3)
+            rows_at = slice(slot * up_rows, (slot + 1) * up_rows)
+
+            @pl.when(local_slot == me)
+            def _():
+                up_ref[slot] = mine_ref[rows_at, :]
+
+            @pl.when(local_slot != me)
+            def _():
+                up_ref[slot] = theirs_ref[rows_at, :]
 
     up_used, marks = call(
         ups,
         "ups",
         (
-            jax.ShapeDtypeStruct((dp, col_tiles * rank, LANES), BF16),
+            jax.ShapeDtypeStruct((dp, up_rows, LANES), BF16),
             like(dp * blocks + 2 * dp, LANES, F32),
         ),
-        [SMEM] + [VMEM] * 6,
-        (info, own_w, near_w, mid_w, far_w, two, three),
+        [SMEM] + [VMEM] * 2,
+        (info, ups_mine, ups_theirs),
     )
 
     def finish(

time: 65.2 us -> 63.7 us (0.977)
  waiting for transfers between devices: 21.9 us -> 19.8 us
    ppermute x17 -> x18, waiting for transfers between devices: 21.9 us -> 19.8 us  [swap(): return lax.ppermute(x, AXES, perm)]
    reshape x1 -> x0, local copies, waits for them, and re-layouts: 0.94 us -> none  [local_line(): up_tiles = up.reshape(per_dev, rank, col_tiles, LANES).transpose(0, 2, 1, 3)]
    squeeze x0 -> x1, local copies, waits for them, and re-layouts: none -> 0.85 us  [local_line(): up_mine = lax.dynamic_index_in_dim(up, group, 0, keepdims=False)]
    ppermute x17 -> x18, starting transfers between devices: 35.6 us -> 36.1 us  [swap(): return lax.ppermute(x, AXES, perm)]
    pallas_call x10 -> x11, Pallas kernels: 5.98 us -> 6.03 us  [call(): pl.pallas_call(lambda *refs: body(Place(), *refs), name=name, out_shape=o...]
  transfers between devices with their start and end apart: 17 -> 18, of which waited for: 6 -> 5; matrix products, arithmetic and copies ran while one was open for 0% -> 0% of each run, Pallas kernels for 8% -> 8%
where the time goes in v7:
time: 63.7 us; the launch traced here: 63.5 us
  starting transfers between devices  36.1 us (57%)
  waiting for transfers between devices  19.8 us (31%)
  Pallas kernels  6.03 us (9%)
  local copies, waits for them, and re-layouts  1.29 us (2%)
    ppermute x18, starting transfers between devices, swap(): return lax.ppermute(x, AXES, perm)  36.1 us
    ppermute x18, waiting for transfers between devices, swap(): return lax.ppermute(x, AXES, perm)  19.8 us
    pallas_call x11, Pallas kernels, call(): pl.pallas_call(lambda *refs: body(Place(), *refs), name=name, out_shape=o...  6.03 us
  transfers between devices with their start and end apart: 18, of which 5 were waited for; matrix products, arithmetic and copies ran while one was open for 0% of the time, Pallas kernels for 8%

profile of v7, /device:TPU:0, one launch (start us, length us, event | category | flops | bytes accessed | tf_op | source)
XLA Modules:
  0.0 63.5 jit_solution(3221643879772187207)
XLA Ops:
  0.0 0.8 %dynamic-slice_bitcast_fusion = bf16[64,256]{1,0:T(8,128)(2,1)S(1)} fusion(bf16[2,64,256]{2,1,0:T(8,128)(2,1)} %param.10, s32[]{:T(128)S(6)} %select_n.8), kind=kLoop, calls=%fused_computation.1 | loop fusion | bytes 65540 | tf_op jit(solution)/shard_map/jit(dynamic_index_in_dim)/squeeze | solution.py:104
  0.9 0.0 copy-start.1
  0.9 0.4 copy-done
  1.3 3.1 %collective-permute-start = (bf16[2176,128]{1,0:T(8,128)(2,1)S(1)}, bf16[2176,128]{1,0:T(8,128)(2,1)S(1)}, u32[]{:S(2)}, u32[]{:S(2)}) collective-permute-start(bf16[2176,128]{1,0:T(8,128)(2,1)S(1)} %pad_maximum_fusion.refs_0_.refs_2_), channel_id=1, source_target_pairs={{0,4},{1,5},{2,6},{3,7},{4,0},{5,1},{6,2},{7,3},{8,12},{9,13},{10,... | collective-permute-start | bytes 1671176 | tf_op jit(solution)/shard_map/ppermute | solution.py:64
  4.4 0.1 pad_add_fusion.refs_0_
  4.5 0.8 %sort_blocks.1.refs_0_ = bf16[272,2048]{1,0:T(8,128)(2,1)S(1)} custom-call(s32[16]{0:T(128)S(1)} %pad_add_fusion.refs_0_, bf16[256,2048]{1,0:T(8,128)(2,1)S(1)} %copy-done.1), custom_call_target="tpu_custom_call" | custom-call | tf_op jit(solution)/shard_map/sort_blocks/pallas_call | solution.py:24
  5.3 1.6 %collective-permute-start.6 = (bf16[272,2048]{1,0:T(8,128)(2,1)S(1)}, bf16[272,2048]{1,0:T(8,128)(2,1)S(1)}, u32[]{:S(2)}, u32[]{:S(2)}) collective-permute-start(bf16[272,2048]{1,0:T(8,128)(2,1)S(1)} %sort_blocks.1.refs_0_), channel_id=1, source_target_pairs={{0,16},{1,17},{2,18},{3,19},{4,20},{5,21},{6,22},{7,23},{8,24},{9,... | collective-permute-start | bytes 3342344 | tf_op jit(solution)/shard_map/ppermute | solution.py:64
  6.9 10.1 %collective-permute-done.refs_1_.refs_3_ = bf16[2176,128]{1,0:T(8,128)(2,1)S(1)} collective-permute-done((bf16[2176,128]{1,0:T(8,128)(2,1)S(1)}, bf16[2176,128]{1,0:T(8,128)(2,1)S(1)}, u32[]{:S(2)}, u32[]{:S(2)}) %collective-permute-start) | collective-permute-done | bytes 557088 | tf_op jit(solution)/shard_map/ppermute | solution.py:64
  17.1 0.3 pack_shrinks.1
  17.4 0.1 choose.2
  17.4 3.4 %collective-permute-start.3 = (bf16[2176,128]{1,0:T(8,128)(2,1)S(1)}, bf16[2176,128]{1,0:T(8,128)(2,1)S(1)}, u32[]{:S(2)}, u32[]{:S(2)}) collective-permute-start(bf16[2176,128]{1,0:T(8,128)(2,1)S(1)} %choose.2), channel_id=1, source_target_pairs={{0,4},{1,5},{2,6},{3,7},{4,0},{5,1},{6,2},{7,3},{8,12},{9,13},{10,... | collective-permute-start | bytes 1671176 | tf_op jit(solution)/shard_map/ppermute | solution.py:64
  20.9 13.6 %collective-permute-start.4 = (bf16[2176,128]{1,0:T(8,128)(2,1)S(1)}, bf16[2176,128]{1,0:T(8,128)(2,1)S(1)}, u32[]{:S(2)}, u32[]{:S(2)}) collective-permute-start(bf16[2176,128]{1,0:T(8,128)(2,1)S(1)} %choose.3), channel_id=1, source_target_pairs={{0,4},{1,5},{2,6},{3,7},{4,0},{5,1},{6,2},{7,3},{8,12},{9,13},{10,... | collective-permute-start | bytes 1671176 | tf_op jit(solution)/shard_map/ppermute | solution.py:64
  34.5 1.6 %collective-permute-start.8 = (bf16[1024,128]{1,0:T(8,128)(2,1)S(1)}, bf16[1024,128]{1,0:T(8,128)(2,1)S(1)}, u32[]{:S(2)}, u32[]{:S(2)}) collective-permute-start(bf16[1024,128]{1,0:T(8,128)(2,1)S(1)} %collective-permute-done.7.refs_4_), channel_id=1, source_target_pairs={{0,16},{1,17},{2,18},{3,19},{4,20},{5,21},{6,22},{7,23},{8,24},{9,... | collective-permute-start | bytes 786440 | tf_op jit(solution)/shard_map/ppermute | solution.py:64
  36.1 5.4 %collective-permute-done.8.refs_5_ = bf16[1024,128]{1,0:T(8,128)(2,1)S(1)} collective-permute-done((bf16[1024,128]{1,0:T(8,128)(2,1)S(1)}, bf16[1024,128]{1,0:T(8,128)(2,1)S(1)}, u32[]{:S(2)}, u32[]{:S(2)}) %collective-permute-start.8) | collective-permute-done | bytes 262176 | tf_op jit(solution)/shard_map/ppermute | solution.py:64
  41.5 1.7 %collective-permute-start.11 = (bf16[1024,128]{1,0:T(8,128)(2,1)S(1)}, bf16[1024,128]{1,0:T(8,128)(2,1)S(1)}, u32[]{:S(2)}, u32[]{:S(2)}) collective-permute-start(bf16[1024,128]{1,0:T(8,128)(2,1)S(1)} %collective-permute-done.10.refs_4_), channel_id=1, source_target_pairs={{0,16},{1,17},{2,18},{3,19},{4,20},{5,21},{6,22},{7,23},{8,24},{9,... | collective-permute-start | bytes 786440 | tf_op jit(solution)/shard_map/ppermute | solution.py:64
  43.2 2.1 %early_columns.1 = (f32[1536,128]{1,0:T(8,128)S(1)}, f32[3,256,64]{2,1,0:T(8,128)S(1)}) custom-call(bf16[272,2048]{1,0:T(8,128)(2,1)S(1)} %sort_blocks.1.refs_0_, bf16[272,2048]{1,0:T(8,128)(2,1)S(1)} %collective-permute-done.6.refs_1_, bf16[2176,128]{1,0:T(8,128)(2,1)S(1)} %pad_maximum_fusion.refs_0_.refs_2_, ...), custom_call_target="tpu_custom_call" | custom-call | tf_op jit(solution)/shard_map/early_columns/pallas_call | solution.py:24
  45.3 0.8 %last_columns.1 = (f32[1024,128]{1,0:T(8,128)S(1)}, bf16[1024,128]{1,0:T(8,128)(2,1)S(1)}, f32[3,256,64]{2,1,0:T(8,128)S(1)}) custom-call(bf16[272,2048]{1,0:T(8,128)(2,1)S(1)} %sort_blocks.1.refs_0_, bf16[272,2048]{1,0:T(8,128)(2,1)S(1)} %collective-permute-done.6.refs_1_, bf16[2176,128]{1,0:T(8,128)(2,1)S(1)} %collective-permute-done.3.refs_4_.refs_5_.refs_2_, ...), custom_call_target="tpu_custom_call" | custom-call | tf_op jit(solution)/shard_map/last_columns/pallas_call | solution.py:24
  46.2 0.1 collective-permute-start.9
  46.2 1.6 %collective-permute-done.11.refs_5_ = bf16[1024,128]{1,0:T(8,128)(2,1)S(1)} collective-permute-done((bf16[1024,128]{1,0:T(8,128)(2,1)S(1)}, bf16[1024,128]{1,0:T(8,128)(2,1)S(1)}, u32[]{:S(2)}, u32[]{:S(2)}) %collective-permute-start.11) | collective-permute-done | bytes 262176 | tf_op jit(solution)/shard_map/ppermute | solution.py:64
  47.8 0.1 last_shrinks.1
  48.0 0.1 collective-permute-start.12
  48.1 1.8 %collective-permute-start.5 = (bf16[512,128]{1,0:T(8,128)(2,1)S(1)}, bf16[512,128]{1,0:T(8,128)(2,1)S(1)}, u32[]{:S(2)}, u32[]{:S(2)}) collective-permute-start(bf16[512,128]{1,0:T(8,128)(2,1)S(1)} %gather_ups.1.refs_1_), channel_id=1, source_target_pairs={{0,16},{1,17},{2,18},{3,19},{4,20},{5,21},{6,22},{7,23},{8,24},{9,... | collective-permute-start | bytes 393224 | tf_op jit(solution)/shard_map/ppermute | solution.py:64
  49.9 0.1 add_cores.1
  49.9 1.6 %collective-permute-start.13 = (bf16[384,128]{1,0:T(8,128)(2,1)S(1)}, bf16[384,128]{1,0:T(8,128)(2,1)S(1)}, u32[]{:S(2)}, u32[]{:S(2)}) collective-permute-start(bf16[384,128]{1,0:T(8,128)(2,1)S(1)} %get-tuple-element.43), channel_id=1, source_target_pairs={{0,2},{1,3},{2,0},{3,1},{4,6},{5,7},{6,4},{7,5},{8,10},{9,11},{10,... | collective-permute-start | bytes 294920 | tf_op jit(solution)/shard_map/ppermute | solution.py:64
  51.5 1.2 %collective-permute-start.14 = (bf16[384,128]{1,0:T(8,128)(2,1)S(1)}, bf16[384,128]{1,0:T(8,128)(2,1)S(1)}, u32[]{:S(2)}, u32[]{:S(2)}) collective-permute-start(bf16[384,128]{1,0:T(8,128)(2,1)S(1)} %get-tuple-element.44), channel_id=1, source_target_pairs={{0,16},{1,17},{2,18},{3,19},{4,20},{5,21},{6,22},{7,23},{8,24},{9,... | collective-permute-start | bytes 294920 | tf_op jit(solution)/shard_map/ppermute | solution.py:64
  52.7 0.8 %collective-permute-start.15 = (bf16[384,128]{1,0:T(8,128)(2,1)S(1)}, bf16[384,128]{1,0:T(8,128)(2,1)S(1)}, u32[]{:S(2)}, u32[]{:S(2)}) collective-permute-start(bf16[384,128]{1,0:T(8,128)(2,1)S(1)} %get-tuple-element.45), channel_id=1, source_target_pairs={{0,18},{1,19},{2,16},{3,17},{4,22},{5,23},{6,20},{7,21},{8,26},{9,... | collective-permute-start | bytes 294920 | tf_op jit(solution)/shard_map/ppermute | solution.py:64
  53.5 5.2 %collective-permute-start.17 = (bf16[128,128]{1,0:T(8,128)(2,1)S(1)}, bf16[128,128]{1,0:T(8,128)(2,1)S(1)}, u32[]{:S(2)}, u32[]{:S(2)}) collective-permute-start(bf16[128,128]{1,0:T(8,128)(2,1)S(1)} %get-tuple-element.46), channel_id=1, source_target_pairs={{0,6},{1,7},{2,4},{3,5},{4,2},{5,3},{6,0},{7,1},{8,14},{9,15},{10,... | collective-permute-start | bytes 98312 | tf_op jit(solution)/shard_map/ppermute | solution.py:64
  58.7 0.5 collective-permute-start.16
  59.2 0.7 %ups.1 = (bf16[4,128,128]{2,1,0:T(8,128)(2,1)S(1)}, f32[24,128]{1,0:T(8,128)S(1)}) custom-call(s32[16]{0:T(128)S(1)} %pad_add_fusion.refs_0_, bf16[512,128]{1,0:T(8,128)(2,1)S(1)} %gather_ups.1.refs_1_, bf16[512,128]{1,0:T(8,128)(2,1)S(1)} %collective-permute-done.5.refs_2_), custom_call_target="tpu_custom_call" | custom-call | tf_op jit(solution)/shard_map/ups/pallas_call | solution.py:24
  60.0 0.9 %collective-permute-done.17.refs_7_ = bf16[128,128]{1,0:T(8,128)(2,1)S(1)} collective-permute-done((bf16[128,128]{1,0:T(8,128)(2,1)S(1)}, bf16[128,128]{1,0:T(8,128)(2,1)S(1)}, u32[]{:S(2)}, u32[]{:S(2)}) %collective-permute-start.17) | collective-permute-done | bytes 32800 | tf_op jit(solution)/shard_map/ppermute | solution.py:64
  60.9 1.7 %collective-permute-done.16.refs_6_ = bf16[128,128]{1,0:T(8,128)(2,1)S(1)} collective-permute-done((bf16[128,128]{1,0:T(8,128)(2,1)S(1)}, bf16[128,128]{1,0:T(8,128)(2,1)S(1)}, u32[]{:S(2)}, u32[]{:S(2)}) %collective-permute-start.16) | collective-permute-done | bytes 32800 | tf_op jit(solution)/shard_map/ppermute | solution.py:64
  62.6 0.9 %finish.1 = bf16[256,256]{1,0:T(8,128)(2,1)} custom-call(f32[24,128]{1,0:T(8,128)S(1)} %get-tuple-element.28.refs_0_, bf16[4,128,128]{2,1,0:T(8,128)(2,1)S(1)} %get-tuple-element.29.refs_1_, f32[384,128]{1,0:T(8,128)S(1)} %get-tuple-element.42.refs_2_, bf16[384,128]{1,0:T(8,128)(2,1)S(1)} %collective-permute-done.13.refs_3_, ...), custom_call_target="tpu_custom_call" | custom-call | tf_op jit(solution)/shard_map/finish/pallas_call | solution.py:24
  (33 shorter events, 0.2 us)
Async XLA Ops:
  0.0 1.2 %copy-start = (bf16[2048,256]{1,0:T(8,128)(2,1)S(1)}, bf16[2048,256]{1,0:T(8,128)(2,1)}, u32[]{:S(2)}) copy-start(bf16[2048,256]{1,0:T(8,128)(2,1)} %param.8) | copy-start | bytes 3145732
  0.9 3.6 %copy-start.3 = (s32[4]{0:T(128)S(1)}, s32[4]{0:T(128)}, u32[]{:S(2)}) copy-start(s32[4]{0:T(128)} %param.13) | copy-start | bytes 52
  0.9 3.6 %copy-start.4 = (s32[4]{0:T(128)S(1)}, s32[4]{0:T(128)}, u32[]{:S(2)}) copy-start(s32[4]{0:T(128)} %param.12) | copy-start | bytes 52
  0.9 3.6 %copy-start.5 = (s32[8]{0:T(128)S(1)}, s32[8]{0:T(128)}, u32[]{:S(2)}) copy-start(s32[8]{0:T(128)} %param.11) | copy-start | bytes 100
  0.9 3.7 %copy-start.1 = (bf16[256,2048]{1,0:T(8,128)(2,1)S(1)}, bf16[256,2048]{1,0:T(8,128)(2,1)}, u32[]{:S(2)}) copy-start(bf16[256,2048]{1,0:T(8,128)(2,1)} %refs_1_.1) | copy-start | bytes 3145732
  1.3 15.7 %copy-start.2 = (bf16[2,2048,64]{1,2,0:T(8,128)(2,1)S(1)}, bf16[2,2048,64]{1,2,0:T(8,128)(2,1)}, u32[]{:S(2)}) copy-start(bf16[2,2048,64]{1,2,0:T(8,128)(2,1)} %param.9) | copy-start | bytes 1572868
  1.3 15.7 %collective-permute-start = (bf16[2176,128]{1,0:T(8,128)(2,1)S(1)}, bf16[2176,128]{1,0:T(8,128)(2,1)S(1)}, u32[]{:S(2)}, u32[]{:S(2)}) collective-permute-start(bf16[2176,128]{1,0:T(8,128)(2,1)S(1)} %pad_maximum_fusion.refs_0_.refs_2_), channel_id=1, source_target_pairs={{0,4},{1,5},{2,6},{3,7},{4,0},{5,1},{6,2},{7,3},{8,12},{9,13},{10,... | collective-permute-start | bytes 1671176 | tf_op jit(solution)/shard_map/ppermute | solution.py:64
  4.4 12.9 %collective-permute-start.1 = (bf16[2176,128]{1,0:T(8,128)(2,1)S(1)}, bf16[2176,128]{1,0:T(8,128)(2,1)S(1)}, u32[]{:S(2)}, u32[]{:S(2)}) collective-permute-start(bf16[2176,128]{1,0:T(8,128)(2,1)S(1)} %pad_maximum_fusion.refs_0_.refs_2_), channel_id=1, source_target_pairs={{0,1},{1,0},{2,3},{3,2},{4,8},{5,9},{6,10},{7,11},{8,4},{9,5},{10,... | collective-permute-start | bytes 1671176 | tf_op jit(solution)/shard_map/ppermute | solution.py:64
  5.3 29.2 %collective-permute-start.6 = (bf16[272,2048]{1,0:T(8,128)(2,1)S(1)}, bf16[272,2048]{1,0:T(8,128)(2,1)S(1)}, u32[]{:S(2)}, u32[]{:S(2)}) collective-permute-start(bf16[272,2048]{1,0:T(8,128)(2,1)S(1)} %sort_blocks.1.refs_0_), channel_id=1, source_target_pairs={{0,16},{1,17},{2,18},{3,19},{4,20},{5,21},{6,22},{7,23},{8,24},{9,... | collective-permute-start | bytes 3342344 | tf_op jit(solution)/shard_map/ppermute | solution.py:64
  17.1 3.8 %collective-permute-start.2 = (bf16[2176,128]{1,0:T(8,128)(2,1)S(1)}, bf16[2176,128]{1,0:T(8,128)(2,1)S(1)}, u32[]{:S(2)}, u32[]{:S(2)}) collective-permute-start(bf16[2176,128]{1,0:T(8,128)(2,1)S(1)} %collective-permute-done.refs_1_.refs_3_), channel_id=1, source_target_pairs={{0,1},{1,0},{2,3},{3,2},{4,8},{5,9},{6,10},{7,11},{8,4},{9,5},{10,... | collective-permute-start | bytes 1671176 | tf_op jit(solution)/shard_map/ppermute | solution.py:64
  17.4 17.0 %collective-permute-start.3 = (bf16[2176,128]{1,0:T(8,128)(2,1)S(1)}, bf16[2176,128]{1,0:T(8,128)(2,1)S(1)}, u32[]{:S(2)}, u32[]{:S(2)}) collective-permute-start(bf16[2176,128]{1,0:T(8,128)(2,1)S(1)} %choose.2), channel_id=1, source_target_pairs={{0,4},{1,5},{2,6},{3,7},{4,0},{5,1},{6,2},{7,3},{8,12},{9,13},{10,... | collective-permute-start | bytes 1671176 | tf_op jit(solution)/shard_map/ppermute | solution.py:64
  20.8 13.7 %collective-permute-start.7 = (bf16[1024,128]{1,0:T(8,128)(2,1)S(1)}, bf16[1024,128]{1,0:T(8,128)(2,1)S(1)}, u32[]{:S(2)}, u32[]{:S(2)}) collective-permute-start(bf16[1024,128]{1,0:T(8,128)(2,1)S(1)} %get-tuple-element.31.refs_6_), channel_id=1, source_target_pairs={{0,1},{1,0},{2,3},{3,2},{4,8},{5,9},{6,10},{7,11},{8,4},{9,5},{10,... | collective-permute-start | bytes 786440 | tf_op jit(solution)/shard_map/ppermute | solution.py:64
  20.9 24.4 %collective-permute-start.4 = (bf16[2176,128]{1,0:T(8,128)(2,1)S(1)}, bf16[2176,128]{1,0:T(8,128)(2,1)S(1)}, u32[]{:S(2)}, u32[]{:S(2)}) collective-permute-start(bf16[2176,128]{1,0:T(8,128)(2,1)S(1)} %choose.3), channel_id=1, source_target_pairs={{0,4},{1,5},{2,6},{3,7},{4,0},{5,1},{6,2},{7,3},{8,12},{9,13},{10,... | collective-permute-start | bytes 1671176 | tf_op jit(solution)/shard_map/ppermute | solution.py:64
  34.5 7.0 %collective-permute-start.8 = (bf16[1024,128]{1,0:T(8,128)(2,1)S(1)}, bf16[1024,128]{1,0:T(8,128)(2,1)S(1)}, u32[]{:S(2)}, u32[]{:S(2)}) collective-permute-start(bf16[1024,128]{1,0:T(8,128)(2,1)S(1)} %collective-permute-done.7.refs_4_), channel_id=1, source_target_pairs={{0,16},{1,17},{2,18},{3,19},{4,20},{5,21},{6,22},{7,23},{8,24},{9,... | collective-permute-start | bytes 786440 | tf_op jit(solution)/shard_map/ppermute | solution.py:64
  36.1 5.4 %collective-permute-start.10 = (bf16[1024,128]{1,0:T(8,128)(2,1)S(1)}, bf16[1024,128]{1,0:T(8,128)(2,1)S(1)}, u32[]{:S(2)}, u32[]{:S(2)}) collective-permute-start(bf16[1024,128]{1,0:T(8,128)(2,1)S(1)} %slice.14), channel_id=1, source_target_pairs={{0,1},{1,0},{2,3},{3,2},{4,8},{5,9},{6,10},{7,11},{8,4},{9,5},{10,... | collective-permute-start | bytes 786440 | tf_op jit(solution)/shard_map/ppermute | solution.py:64
  41.5 6.4 %collective-permute-start.11 = (bf16[1024,128]{1,0:T(8,128)(2,1)S(1)}, bf16[1024,128]{1,0:T(8,128)(2,1)S(1)}, u32[]{:S(2)}, u32[]{:S(2)}) collective-permute-start(bf16[1024,128]{1,0:T(8,128)(2,1)S(1)} %collective-permute-done.10.refs_4_), channel_id=1, source_target_pairs={{0,16},{1,17},{2,18},{3,19},{4,20},{5,21},{6,22},{7,23},{8,24},{9,... | collective-permute-start | bytes 786440 | tf_op jit(solution)/shard_map/ppermute | solution.py:64
  46.2 3.7 %collective-permute-start.9 = (bf16[1024,128]{1,0:T(8,128)(2,1)S(1)}, bf16[1024,128]{1,0:T(8,128)(2,1)S(1)}, u32[]{:S(2)}, u32[]{:S(2)}) collective-permute-start(bf16[1024,128]{1,0:T(8,128)(2,1)S(1)} %get-tuple-element.37), channel_id=1, source_target_pairs={{0,1},{1,0},{2,3},{3,2},{4,5},{5,4},{6,7},{7,6},{8,9},{9,8},{10,11... | collective-permute-start | bytes 786440 | tf_op jit(solution)/shard_map/ppermute | solution.py:64
  48.0 1.9 %collective-permute-start.12 = (bf16[384,128]{1,0:T(8,128)(2,1)S(1)}, bf16[384,128]{1,0:T(8,128)(2,1)S(1)}, u32[]{:S(2)}, u32[]{:S(2)}) collective-permute-start(bf16[384,128]{1,0:T(8,128)(2,1)S(1)} %get-tuple-element.41), channel_id=1, source_target_pairs={{0,1},{1,0},{2,3},{3,2},{4,5},{5,4},{6,7},{7,6},{8,9},{9,8},{10,11... | collective-permute-start | bytes 294920 | tf_op jit(solution)/shard_map/ppermute | solution.py:64
  48.1 10.6 %collective-permute-start.5 = (bf16[512,128]{1,0:T(8,128)(2,1)S(1)}, bf16[512,128]{1,0:T(8,128)(2,1)S(1)}, u32[]{:S(2)}, u32[]{:S(2)}) collective-permute-start(bf16[512,128]{1,0:T(8,128)(2,1)S(1)} %gather_ups.1.refs_1_), channel_id=1, source_target_pairs={{0,16},{1,17},{2,18},{3,19},{4,20},{5,21},{6,22},{7,23},{8,24},{9,... | collective-permute-start | bytes 393224 | tf_op jit(solution)/shard_map/ppermute | solution.py:64
  49.9 12.7 %collective-permute-start.13 = (bf16[384,128]{1,0:T(8,128)(2,1)S(1)}, bf16[384,128]{1,0:T(8,128)(2,1)S(1)}, u32[]{:S(2)}, u32[]{:S(2)}) collective-permute-start(bf16[384,128]{1,0:T(8,128)(2,1)S(1)} %get-tuple-element.43), channel_id=1, source_target_pairs={{0,2},{1,3},{2,0},{3,1},{4,6},{5,7},{6,4},{7,5},{8,10},{9,11},{10,... | collective-permute-start | bytes 294920 | tf_op jit(solution)/shard_map/ppermute | solution.py:64
  51.5 11.1 %collective-permute-start.14 = (bf16[384,128]{1,0:T(8,128)(2,1)S(1)}, bf16[384,128]{1,0:T(8,128)(2,1)S(1)}, u32[]{:S(2)}, u32[]{:S(2)}) collective-permute-start(bf16[384,128]{1,0:T(8,128)(2,1)S(1)} %get-tuple-element.44), channel_id=1, source_target_pairs={{0,16},{1,17},{2,18},{3,19},{4,20},{5,21},{6,22},{7,23},{8,24},{9,... | collective-permute-start | bytes 294920 | tf_op jit(solution)/shard_map/ppermute | solution.py:64
  52.7 10.0 %collective-permute-start.15 = (bf16[384,128]{1,0:T(8,128)(2,1)S(1)}, bf16[384,128]{1,0:T(8,128)(2,1)S(1)}, u32[]{:S(2)}, u32[]{:S(2)}) collective-permute-start(bf16[384,128]{1,0:T(8,128)(2,1)S(1)} %get-tuple-element.45), channel_id=1, source_target_pairs={{0,18},{1,19},{2,16},{3,17},{4,22},{5,23},{6,20},{7,21},{8,26},{9,... | collective-permute-start | bytes 294920 | tf_op jit(solution)/shard_map/ppermute | solution.py:64
  53.5 7.4 %collective-permute-start.17 = (bf16[128,128]{1,0:T(8,128)(2,1)S(1)}, bf16[128,128]{1,0:T(8,128)(2,1)S(1)}, u32[]{:S(2)}, u32[]{:S(2)}) collective-permute-start(bf16[128,128]{1,0:T(8,128)(2,1)S(1)} %get-tuple-element.46), channel_id=1, source_target_pairs={{0,6},{1,7},{2,4},{3,5},{4,2},{5,3},{6,0},{7,1},{8,14},{9,15},{10,... | collective-permute-start | bytes 98312 | tf_op jit(solution)/shard_map/ppermute | solution.py:64
  58.7 3.9 %collective-permute-start.16 = (bf16[128,128]{1,0:T(8,128)(2,1)S(1)}, bf16[128,128]{1,0:T(8,128)(2,1)S(1)}, u32[]{:S(2)}, u32[]{:S(2)}) collective-permute-start(bf16[128,128]{1,0:T(8,128)(2,1)S(1)} %get-tuple-element.46), channel_id=1, source_target_pairs={{0,4},{1,5},{2,6},{3,7},{4,0},{5,1},{6,2},{7,3},{8,12},{9,13},{10,... | collective-permute-start | bytes 98312 | tf_op jit(solution)/shard_map/ppermute | solution.py:64

commit v8 on v7

--- a/solution.py
+++ b/solution.py
@@ -179,7 +179,7 @@
     two = to_neighbour(chosen(first, mid_w))
     far_w = to_middle(near_w)
     mid_d = to_middle(tie(own_d, near_w))
-    three = to_neighbour(chosen(second, far_w))
+    three = to_neighbour(chosen(second, tie(far_w, two)))
     near_d = two[0:half]
     mid_e = to_group(tie(mid_d, others, near_d))
     far_d = to_middle(near_d)

time: 63.7 us -> 63.7 us (level)
  starting transfers between devices: 36.1 us -> 26.2 us
  waiting for transfers between devices: 19.8 us -> 29.7 us
    ppermute x18, starting transfers between devices: 36.1 us -> 26.2 us  [swap(): return lax.ppermute(x, AXES, perm)]
    ppermute x18, waiting for transfers between devices: 19.8 us -> 29.7 us  [swap(): return lax.ppermute(x, AXES, perm)]
where the time goes in v8:
time: 63.7 us; the launch traced here: 63.5 us
  waiting for transfers between devices  29.7 us (47%)
  starting transfers between devices  26.2 us (41%)
  Pallas kernels  6.02 us (9%)
  local copies, waits for them, and re-layouts  1.28 us (2%)
    ppermute x18, waiting for transfers between devices, swap(): return lax.ppermute(x, AXES, perm)  29.7 us
    ppermute x18, starting transfers between devices, swap(): return lax.ppermute(x, AXES, perm)  26.2 us
    pallas_call x11, Pallas kernels, call(): pl.pallas_call(lambda *refs: body(Place(), *refs), name=name, out_shape=o...  6.02 us
  transfers between devices with their start and end apart: 18, of which 5 were waited for; matrix products, arithmetic and copies ran while one was open for 0% of the time, Pallas kernels for 8%

profile of v8, /device:TPU:0, one launch (start us, length us, event | category | flops | bytes accessed | tf_op | source)
XLA Modules:
  0.0 63.5 jit_solution(7212828143231242012)
XLA Ops:
  0.0 0.8 %dynamic-slice_bitcast_fusion = bf16[64,256]{1,0:T(8,128)(2,1)S(1)} fusion(bf16[2,64,256]{2,1,0:T(8,128)(2,1)} %param.10, s32[]{:T(128)S(6)} %select_n.8), kind=kLoop, calls=%fused_computation.1 | loop fusion | bytes 65540 | tf_op jit(solution)/shard_map/jit(dynamic_index_in_dim)/squeeze | solution.py:104
  0.9 0.0 copy-start.1
  0.9 0.4 copy-done
  1.3 0.0 copy-start.2
  1.3 3.1 %collective-permute-start = (bf16[2176,128]{1,0:T(8,128)(2,1)S(1)}, bf16[2176,128]{1,0:T(8,128)(2,1)S(1)}, u32[]{:S(2)}, u32[]{:S(2)}) collective-permute-start(bf16[2176,128]{1,0:T(8,128)(2,1)S(1)} %pad_maximum_fusion.refs_0_.refs_2_), channel_id=1, source_target_pairs={{0,4},{1,5},{2,6},{3,7},{4,0},{5,1},{6,2},{7,3},{8,12},{9,13},{10,... | collective-permute-start | bytes 1671176 | tf_op jit(solution)/shard_map/ppermute | solution.py:64
  4.4 0.1 pad_add_fusion.refs_0_
  4.5 0.8 %sort_blocks.1.refs_0_ = bf16[272,2048]{1,0:T(8,128)(2,1)S(1)} custom-call(s32[16]{0:T(128)S(1)} %pad_add_fusion.refs_0_, bf16[256,2048]{1,0:T(8,128)(2,1)S(1)} %copy-done.1), custom_call_target="tpu_custom_call" | custom-call | tf_op jit(solution)/shard_map/sort_blocks/pallas_call | solution.py:24
  5.3 1.6 %collective-permute-start.6 = (bf16[272,2048]{1,0:T(8,128)(2,1)S(1)}, bf16[272,2048]{1,0:T(8,128)(2,1)S(1)}, u32[]{:S(2)}, u32[]{:S(2)}) collective-permute-start(bf16[272,2048]{1,0:T(8,128)(2,1)S(1)} %sort_blocks.1.refs_0_), channel_id=1, source_target_pairs={{0,16},{1,17},{2,18},{3,19},{4,20},{5,21},{6,22},{7,23},{8,24},{9,... | collective-permute-start | bytes 3342344 | tf_op jit(solution)/shard_map/ppermute | solution.py:64
  6.9 0.3 pack_shrinks.1
  7.2 9.8 %collective-permute-done.refs_1_.refs_3_ = bf16[2176,128]{1,0:T(8,128)(2,1)S(1)} collective-permute-done((bf16[2176,128]{1,0:T(8,128)(2,1)S(1)}, bf16[2176,128]{1,0:T(8,128)(2,1)S(1)}, u32[]{:S(2)}, u32[]{:S(2)}) %collective-permute-start) | collective-permute-done | bytes 557088 | tf_op jit(solution)/shard_map/ppermute | solution.py:64
  17.1 3.4 %collective-permute-start.3 = (bf16[2176,128]{1,0:T(8,128)(2,1)S(1)}, bf16[2176,128]{1,0:T(8,128)(2,1)S(1)}, u32[]{:S(2)}, u32[]{:S(2)}) collective-permute-start(bf16[2176,128]{1,0:T(8,128)(2,1)S(1)} %choose.2), channel_id=1, source_target_pairs={{0,4},{1,5},{2,6},{3,7},{4,0},{5,1},{6,2},{7,3},{8,12},{9,13},{10,... | collective-permute-start | bytes 1671176 | tf_op jit(solution)/shard_map/ppermute | solution.py:64
  20.5 11.7 %collective-permute-done.3.refs_4_.refs_5_.refs_2_ = bf16[2176,128]{1,0:T(8,128)(2,1)S(1)} collective-permute-done((bf16[2176,128]{1,0:T(8,128)(2,1)S(1)}, bf16[2176,128]{1,0:T(8,128)(2,1)S(1)}, u32[]{:S(2)}, u32[]{:S(2)}) %collective-permute-start.3) | collective-permute-done | bytes 557088 | tf_op jit(solution)/shard_map/ppermute | solution.py:64
  32.3 2.2 %collective-permute-start.4 = (bf16[2176,128]{1,0:T(8,128)(2,1)S(1)}, bf16[2176,128]{1,0:T(8,128)(2,1)S(1)}, u32[]{:S(2)}, u32[]{:S(2)}) collective-permute-start(bf16[2176,128]{1,0:T(8,128)(2,1)S(1)} %choose.3), channel_id=1, source_target_pairs={{0,4},{1,5},{2,6},{3,7},{4,0},{5,1},{6,2},{7,3},{8,12},{9,13},{10,... | collective-permute-start | bytes 1671176 | tf_op jit(solution)/shard_map/ppermute | solution.py:64
  34.5 1.6 %collective-permute-start.8 = (bf16[1024,128]{1,0:T(8,128)(2,1)S(1)}, bf16[1024,128]{1,0:T(8,128)(2,1)S(1)}, u32[]{:S(2)}, u32[]{:S(2)}) collective-permute-start(bf16[1024,128]{1,0:T(8,128)(2,1)S(1)} %collective-permute-done.7.refs_4_), channel_id=1, source_target_pairs={{0,16},{1,17},{2,18},{3,19},{4,20},{5,21},{6,22},{7,23},{8,24},{9,... | collective-permute-start | bytes 786440 | tf_op jit(solution)/shard_map/ppermute | solution.py:64
  36.1 5.4 %collective-permute-done.8.refs_5_ = bf16[1024,128]{1,0:T(8,128)(2,1)S(1)} collective-permute-done((bf16[1024,128]{1,0:T(8,128)(2,1)S(1)}, bf16[1024,128]{1,0:T(8,128)(2,1)S(1)}, u32[]{:S(2)}, u32[]{:S(2)}) %collective-permute-start.8) | collective-permute-done | bytes 262176 | tf_op jit(solution)/shard_map/ppermute | solution.py:64
  41.5 1.7 %collective-permute-start.11 = (bf16[1024,128]{1,0:T(8,128)(2,1)S(1)}, bf16[1024,128]{1,0:T(8,128)(2,1)S(1)}, u32[]{:S(2)}, u32[]{:S(2)}) collective-permute-start(bf16[1024,128]{1,0:T(8,128)(2,1)S(1)} %collective-permute-done.10.refs_4_), channel_id=1, source_target_pairs={{0,16},{1,17},{2,18},{3,19},{4,20},{5,21},{6,22},{7,23},{8,24},{9,... | collective-permute-start | bytes 786440 | tf_op jit(solution)/shard_map/ppermute | solution.py:64
  43.2 2.1 %early_columns.1 = (f32[1536,128]{1,0:T(8,128)S(1)}, f32[3,256,64]{2,1,0:T(8,128)S(1)}) custom-call(bf16[272,2048]{1,0:T(8,128)(2,1)S(1)} %sort_blocks.1.refs_0_, bf16[272,2048]{1,0:T(8,128)(2,1)S(1)} %collective-permute-done.6.refs_1_, bf16[2176,128]{1,0:T(8,128)(2,1)S(1)} %pad_maximum_fusion.refs_0_.refs_2_, ...), custom_call_target="tpu_custom_call" | custom-call | tf_op jit(solution)/shard_map/early_columns/pallas_call | solution.py:24
  45.3 0.8 %last_columns.1 = (f32[1024,128]{1,0:T(8,128)S(1)}, bf16[1024,128]{1,0:T(8,128)(2,1)S(1)}, f32[3,256,64]{2,1,0:T(8,128)S(1)}) custom-call(bf16[272,2048]{1,0:T(8,128)(2,1)S(1)} %sort_blocks.1.refs_0_, bf16[272,2048]{1,0:T(8,128)(2,1)S(1)} %collective-permute-done.6.refs_1_, bf16[2176,128]{1,0:T(8,128)(2,1)S(1)} %collective-permute-done.3.refs_4_.refs_5_.refs_2_, ...), custom_call_target="tpu_custom_call" | custom-call | tf_op jit(solution)/shard_map/last_columns/pallas_call | solution.py:24
  46.2 0.1 collective-permute-start.9
  46.2 1.6 %collective-permute-done.11.refs_5_ = bf16[1024,128]{1,0:T(8,128)(2,1)S(1)} collective-permute-done((bf16[1024,128]{1,0:T(8,128)(2,1)S(1)}, bf16[1024,128]{1,0:T(8,128)(2,1)S(1)}, u32[]{:S(2)}, u32[]{:S(2)}) %collective-permute-start.11) | collective-permute-done | bytes 262176 | tf_op jit(solution)/shard_map/ppermute | solution.py:64
  47.8 0.1 last_shrinks.1
  48.0 0.1 collective-permute-start.12
  48.1 1.8 %collective-permute-start.5 = (bf16[512,128]{1,0:T(8,128)(2,1)S(1)}, bf16[512,128]{1,0:T(8,128)(2,1)S(1)}, u32[]{:S(2)}, u32[]{:S(2)}) collective-permute-start(bf16[512,128]{1,0:T(8,128)(2,1)S(1)} %gather_ups.1.refs_1_), channel_id=1, source_target_pairs={{0,16},{1,17},{2,18},{3,19},{4,20},{5,21},{6,22},{7,23},{8,24},{9,... | collective-permute-start | bytes 393224 | tf_op jit(solution)/shard_map/ppermute | solution.py:64
  49.9 0.1 add_cores.1
  49.9 1.6 %collective-permute-start.13 = (bf16[384,128]{1,0:T(8,128)(2,1)S(1)}, bf16[384,128]{1,0:T(8,128)(2,1)S(1)}, u32[]{:S(2)}, u32[]{:S(2)}) collective-permute-start(bf16[384,128]{1,0:T(8,128)(2,1)S(1)} %get-tuple-element.45), channel_id=1, source_target_pairs={{0,2},{1,3},{2,0},{3,1},{4,6},{5,7},{6,4},{7,5},{8,10},{9,11},{10,... | collective-permute-start | bytes 294920 | tf_op jit(solution)/shard_map/ppermute | solution.py:64
  51.5 1.2 %collective-permute-start.14 = (bf16[384,128]{1,0:T(8,128)(2,1)S(1)}, bf16[384,128]{1,0:T(8,128)(2,1)S(1)}, u32[]{:S(2)}, u32[]{:S(2)}) collective-permute-start(bf16[384,128]{1,0:T(8,128)(2,1)S(1)} %get-tuple-element.46), channel_id=1, source_target_pairs={{0,16},{1,17},{2,18},{3,19},{4,20},{5,21},{6,22},{7,23},{8,24},{9,... | collective-permute-start | bytes 294920 | tf_op jit(solution)/shard_map/ppermute | solution.py:64
  52.7 0.8 %collective-permute-start.15 = (bf16[384,128]{1,0:T(8,128)(2,1)S(1)}, bf16[384,128]{1,0:T(8,128)(2,1)S(1)}, u32[]{:S(2)}, u32[]{:S(2)}) collective-permute-start(bf16[384,128]{1,0:T(8,128)(2,1)S(1)} %get-tuple-element.47), channel_id=1, source_target_pairs={{0,18},{1,19},{2,16},{3,17},{4,22},{5,23},{6,20},{7,21},{8,26},{9,... | collective-permute-start | bytes 294920 | tf_op jit(solution)/shard_map/ppermute | solution.py:64
  53.5 4.3 %collective-permute-start.16 = (bf16[128,128]{1,0:T(8,128)(2,1)S(1)}, bf16[128,128]{1,0:T(8,128)(2,1)S(1)}, u32[]{:S(2)}, u32[]{:S(2)}) collective-permute-start(bf16[128,128]{1,0:T(8,128)(2,1)S(1)} %get-tuple-element.48), channel_id=1, source_target_pairs={{0,4},{1,5},{2,6},{3,7},{4,0},{5,1},{6,2},{7,3},{8,12},{9,13},{10,... | collective-permute-start | bytes 98312 | tf_op jit(solution)/shard_map/ppermute | solution.py:64
  57.8 2.9 %collective-permute-start.17 = (bf16[128,128]{1,0:T(8,128)(2,1)S(1)}, bf16[128,128]{1,0:T(8,128)(2,1)S(1)}, u32[]{:S(2)}, u32[]{:S(2)}) collective-permute-start(bf16[128,128]{1,0:T(8,128)(2,1)S(1)} %get-tuple-element.48), channel_id=1, source_target_pairs={{0,6},{1,7},{2,4},{3,5},{4,2},{5,3},{6,0},{7,1},{8,14},{9,15},{10,... | collective-permute-start | bytes 98312 | tf_op jit(solution)/shard_map/ppermute | solution.py:64
  60.7 0.7 %ups.1 = (bf16[4,128,128]{2,1,0:T(8,128)(2,1)S(1)}, f32[24,128]{1,0:T(8,128)S(1)}) custom-call(s32[16]{0:T(128)S(1)} %pad_add_fusion.refs_0_, bf16[512,128]{1,0:T(8,128)(2,1)S(1)} %gather_ups.1.refs_1_, bf16[512,128]{1,0:T(8,128)(2,1)S(1)} %collective-permute-done.5.refs_2_), custom_call_target="tpu_custom_call" | custom-call | tf_op jit(solution)/shard_map/ups/pallas_call | solution.py:24
  61.4 1.2 %collective-permute-done.17.refs_7_ = bf16[128,128]{1,0:T(8,128)(2,1)S(1)} collective-permute-done((bf16[128,128]{1,0:T(8,128)(2,1)S(1)}, bf16[128,128]{1,0:T(8,128)(2,1)S(1)}, u32[]{:S(2)}, u32[]{:S(2)}) %collective-permute-start.17) | collective-permute-done | bytes 32800 | tf_op jit(solution)/shard_map/ppermute | solution.py:64
  62.6 0.9 %finish.1 = bf16[256,256]{1,0:T(8,128)(2,1)} custom-call(f32[24,128]{1,0:T(8,128)S(1)} %get-tuple-element.30.refs_0_, bf16[4,128,128]{2,1,0:T(8,128)(2,1)S(1)} %get-tuple-element.31.refs_1_, f32[384,128]{1,0:T(8,128)S(1)} %get-tuple-element.44.refs_2_, bf16[384,128]{1,0:T(8,128)(2,1)S(1)} %collective-permute-done.13.refs_3_, ...), custom_call_target="tpu_custom_call" | custom-call | tf_op jit(solution)/shard_map/finish/pallas_call | solution.py:24
  (33 shorter events, 0.3 us)
Async XLA Ops:
  0.0 1.2 %copy-start = (bf16[2048,256]{1,0:T(8,128)(2,1)S(1)}, bf16[2048,256]{1,0:T(8,128)(2,1)}, u32[]{:S(2)}) copy-start(bf16[2048,256]{1,0:T(8,128)(2,1)} %param.8) | copy-start | bytes 3145732
  0.9 3.6 %copy-start.3 = (s32[4]{0:T(128)S(1)}, s32[4]{0:T(128)}, u32[]{:S(2)}) copy-start(s32[4]{0:T(128)} %param.13) | copy-start | bytes 52
  0.9 3.6 %copy-start.4 = (s32[4]{0:T(128)S(1)}, s32[4]{0:T(128)}, u32[]{:S(2)}) copy-start(s32[4]{0:T(128)} %param.12) | copy-start | bytes 52
  0.9 3.6 %copy-start.5 = (s32[8]{0:T(128)S(1)}, s32[8]{0:T(128)}, u32[]{:S(2)}) copy-start(s32[8]{0:T(128)} %param.11) | copy-start | bytes 100
  0.9 3.7 %copy-start.1 = (bf16[256,2048]{1,0:T(8,128)(2,1)S(1)}, bf16[256,2048]{1,0:T(8,128)(2,1)}, u32[]{:S(2)}) copy-start(bf16[256,2048]{1,0:T(8,128)(2,1)} %refs_1_.1) | copy-start | bytes 3145732
  1.3 5.6 %copy-start.2 = (bf16[2,2048,64]{1,2,0:T(8,128)(2,1)S(1)}, bf16[2,2048,64]{1,2,0:T(8,128)(2,1)}, u32[]{:S(2)}) copy-start(bf16[2,2048,64]{1,2,0:T(8,128)(2,1)} %param.9) | copy-start | bytes 1572868
  1.3 15.7 %collective-permute-start = (bf16[2176,128]{1,0:T(8,128)(2,1)S(1)}, bf16[2176,128]{1,0:T(8,128)(2,1)S(1)}, u32[]{:S(2)}, u32[]{:S(2)}) collective-permute-start(bf16[2176,128]{1,0:T(8,128)(2,1)S(1)} %pad_maximum_fusion.refs_0_.refs_2_), channel_id=1, source_target_pairs={{0,4},{1,5},{2,6},{3,7},{4,0},{5,1},{6,2},{7,3},{8,12},{9,13},{10,... | collective-permute-start | bytes 1671176 | tf_op jit(solution)/shard_map/ppermute | solution.py:64
  4.4 12.6 %collective-permute-start.1 = (bf16[2176,128]{1,0:T(8,128)(2,1)S(1)}, bf16[2176,128]{1,0:T(8,128)(2,1)S(1)}, u32[]{:S(2)}, u32[]{:S(2)}) collective-permute-start(bf16[2176,128]{1,0:T(8,128)(2,1)S(1)} %pad_maximum_fusion.refs_0_.refs_2_), channel_id=1, source_target_pairs={{0,1},{1,0},{2,3},{3,2},{4,8},{5,9},{6,10},{7,11},{8,4},{9,5},{10,... | collective-permute-start | bytes 1671176 | tf_op jit(solution)/shard_map/ppermute | solution.py:64
  5.3 29.2 %collective-permute-start.6 = (bf16[272,2048]{1,0:T(8,128)(2,1)S(1)}, bf16[272,2048]{1,0:T(8,128)(2,1)S(1)}, u32[]{:S(2)}, u32[]{:S(2)}) collective-permute-start(bf16[272,2048]{1,0:T(8,128)(2,1)S(1)} %sort_blocks.1.refs_0_), channel_id=1, source_target_pairs={{0,16},{1,17},{2,18},{3,19},{4,20},{5,21},{6,22},{7,23},{8,24},{9,... | collective-permute-start | bytes 3342344 | tf_op jit(solution)/shard_map/ppermute | solution.py:64
  17.1 3.4 %collective-permute-start.2 = (bf16[2176,128]{1,0:T(8,128)(2,1)S(1)}, bf16[2176,128]{1,0:T(8,128)(2,1)S(1)}, u32[]{:S(2)}, u32[]{:S(2)}) collective-permute-start(bf16[2176,128]{1,0:T(8,128)(2,1)S(1)} %collective-permute-done.refs_1_.refs_3_), channel_id=1, source_target_pairs={{0,1},{1,0},{2,3},{3,2},{4,8},{5,9},{6,10},{7,11},{8,4},{9,5},{10,... | collective-permute-start | bytes 1671176 | tf_op jit(solution)/shard_map/ppermute | solution.py:64
  17.1 15.1 %collective-permute-start.3 = (bf16[2176,128]{1,0:T(8,128)(2,1)S(1)}, bf16[2176,128]{1,0:T(8,128)(2,1)S(1)}, u32[]{:S(2)}, u32[]{:S(2)}) collective-permute-start(bf16[2176,128]{1,0:T(8,128)(2,1)S(1)} %choose.2), channel_id=1, source_target_pairs={{0,4},{1,5},{2,6},{3,7},{4,0},{5,1},{6,2},{7,3},{8,12},{9,13},{10,... | collective-permute-start | bytes 1671176 | tf_op jit(solution)/shard_map/ppermute | solution.py:64
  20.5 14.0 %collective-permute-start.7 = (bf16[1024,128]{1,0:T(8,128)(2,1)S(1)}, bf16[1024,128]{1,0:T(8,128)(2,1)S(1)}, u32[]{:S(2)}, u32[]{:S(2)}) collective-permute-start(bf16[1024,128]{1,0:T(8,128)(2,1)S(1)} %get-tuple-element.33.refs_6_), channel_id=1, source_target_pairs={{0,1},{1,0},{2,3},{3,2},{4,8},{5,9},{6,10},{7,11},{8,4},{9,5},{10,... | collective-permute-start | bytes 786440 | tf_op jit(solution)/shard_map/ppermute | solution.py:64
  32.3 13.1 %collective-permute-start.4 = (bf16[2176,128]{1,0:T(8,128)(2,1)S(1)}, bf16[2176,128]{1,0:T(8,128)(2,1)S(1)}, u32[]{:S(2)}, u32[]{:S(2)}) collective-permute-start(bf16[2176,128]{1,0:T(8,128)(2,1)S(1)} %choose.3), channel_id=1, source_target_pairs={{0,4},{1,5},{2,6},{3,7},{4,0},{5,1},{6,2},{7,3},{8,12},{9,13},{10,... | collective-permute-start | bytes 1671176 | tf_op jit(solution)/shard_map/ppermute | solution.py:64
  34.5 7.0 %collective-permute-start.8 = (bf16[1024,128]{1,0:T(8,128)(2,1)S(1)}, bf16[1024,128]{1,0:T(8,128)(2,1)S(1)}, u32[]{:S(2)}, u32[]{:S(2)}) collective-permute-start(bf16[1024,128]{1,0:T(8,128)(2,1)S(1)} %collective-permute-done.7.refs_4_), channel_id=1, source_target_pairs={{0,16},{1,17},{2,18},{3,19},{4,20},{5,21},{6,22},{7,23},{8,24},{9,... | collective-permute-start | bytes 786440 | tf_op jit(solution)/shard_map/ppermute | solution.py:64
  36.1 5.4 %collective-permute-start.10 = (bf16[1024,128]{1,0:T(8,128)(2,1)S(1)}, bf16[1024,128]{1,0:T(8,128)(2,1)S(1)}, u32[]{:S(2)}, u32[]{:S(2)}) collective-permute-start(bf16[1024,128]{1,0:T(8,128)(2,1)S(1)} %slice.14), channel_id=1, source_target_pairs={{0,1},{1,0},{2,3},{3,2},{4,8},{5,9},{6,10},{7,11},{8,4},{9,5},{10,... | collective-permute-start | bytes 786440 | tf_op jit(solution)/shard_map/ppermute | solution.py:64
  41.5 6.4 %collective-permute-start.11 = (bf16[1024,128]{1,0:T(8,128)(2,1)S(1)}, bf16[1024,128]{1,0:T(8,128)(2,1)S(1)}, u32[]{:S(2)}, u32[]{:S(2)}) collective-permute-start(bf16[1024,128]{1,0:T(8,128)(2,1)S(1)} %collective-permute-done.10.refs_4_), channel_id=1, source_target_pairs={{0,16},{1,17},{2,18},{3,19},{4,20},{5,21},{6,22},{7,23},{8,24},{9,... | collective-permute-start | bytes 786440 | tf_op jit(solution)/shard_map/ppermute | solution.py:64
  46.2 3.7 %collective-permute-start.9 = (bf16[1024,128]{1,0:T(8,128)(2,1)S(1)}, bf16[1024,128]{1,0:T(8,128)(2,1)S(1)}, u32[]{:S(2)}, u32[]{:S(2)}) collective-permute-start(bf16[1024,128]{1,0:T(8,128)(2,1)S(1)} %get-tuple-element.39), channel_id=1, source_target_pairs={{0,1},{1,0},{2,3},{3,2},{4,5},{5,4},{6,7},{7,6},{8,9},{9,8},{10,11... | collective-permute-start | bytes 786440 | tf_op jit(solution)/shard_map/ppermute | solution.py:64
  48.0 1.9 %collective-permute-start.12 = (bf16[384,128]{1,0:T(8,128)(2,1)S(1)}, bf16[384,128]{1,0:T(8,128)(2,1)S(1)}, u32[]{:S(2)}, u32[]{:S(2)}) collective-permute-start(bf16[384,128]{1,0:T(8,128)(2,1)S(1)} %get-tuple-element.43), channel_id=1, source_target_pairs={{0,1},{1,0},{2,3},{3,2},{4,5},{5,4},{6,7},{7,6},{8,9},{9,8},{10,11... | collective-permute-start | bytes 294920 | tf_op jit(solution)/shard_map/ppermute | solution.py:64
  48.1 9.7 %collective-permute-start.5 = (bf16[512,128]{1,0:T(8,128)(2,1)S(1)}, bf16[512,128]{1,0:T(8,128)(2,1)S(1)}, u32[]{:S(2)}, u32[]{:S(2)}) collective-permute-start(bf16[512,128]{1,0:T(8,128)(2,1)S(1)} %gather_ups.1.refs_1_), channel_id=1, source_target_pairs={{0,16},{1,17},{2,18},{3,19},{4,20},{5,21},{6,22},{7,23},{8,24},{9,... | collective-permute-start | bytes 393224 | tf_op jit(solution)/shard_map/ppermute | solution.py:64
  49.9 12.7 %collective-permute-start.13 = (bf16[384,128]{1,0:T(8,128)(2,1)S(1)}, bf16[384,128]{1,0:T(8,128)(2,1)S(1)}, u32[]{:S(2)}, u32[]{:S(2)}) collective-permute-start(bf16[384,128]{1,0:T(8,128)(2,1)S(1)} %get-tuple-element.45), channel_id=1, source_target_pairs={{0,2},{1,3},{2,0},{3,1},{4,6},{5,7},{6,4},{7,5},{8,10},{9,11},{10,... | collective-permute-start | bytes 294920 | tf_op jit(solution)/shard_map/ppermute | solution.py:64
  51.5 11.1 %collective-permute-start.14 = (bf16[384,128]{1,0:T(8,128)(2,1)S(1)}, bf16[384,128]{1,0:T(8,128)(2,1)S(1)}, u32[]{:S(2)}, u32[]{:S(2)}) collective-permute-start(bf16[384,128]{1,0:T(8,128)(2,1)S(1)} %get-tuple-element.46), channel_id=1, source_target_pairs={{0,16},{1,17},{2,18},{3,19},{4,20},{5,21},{6,22},{7,23},{8,24},{9,... | collective-permute-start | bytes 294920 | tf_op jit(solution)/shard_map/ppermute | solution.py:64
  52.7 9.9 %collective-permute-start.15 = (bf16[384,128]{1,0:T(8,128)(2,1)S(1)}, bf16[384,128]{1,0:T(8,128)(2,1)S(1)}, u32[]{:S(2)}, u32[]{:S(2)}) collective-permute-start(bf16[384,128]{1,0:T(8,128)(2,1)S(1)} %get-tuple-element.47), channel_id=1, source_target_pairs={{0,18},{1,19},{2,16},{3,17},{4,22},{5,23},{6,20},{7,21},{8,26},{9,... | collective-permute-start | bytes 294920 | tf_op jit(solution)/shard_map/ppermute | solution.py:64
  53.5 7.9 %collective-permute-start.16 = (bf16[128,128]{1,0:T(8,128)(2,1)S(1)}, bf16[128,128]{1,0:T(8,128)(2,1)S(1)}, u32[]{:S(2)}, u32[]{:S(2)}) collective-permute-start(bf16[128,128]{1,0:T(8,128)(2,1)S(1)} %get-tuple-element.48), channel_id=1, source_target_pairs={{0,4},{1,5},{2,6},{3,7},{4,0},{5,1},{6,2},{7,3},{8,12},{9,13},{10,... | collective-permute-start | bytes 98312 | tf_op jit(solution)/shard_map/ppermute | solution.py:64
  57.8 4.8 %collective-permute-start.17 = (bf16[128,128]{1,0:T(8,128)(2,1)S(1)}, bf16[128,128]{1,0:T(8,128)(2,1)S(1)}, u32[]{:S(2)}, u32[]{:S(2)}) collective-permute-start(bf16[128,128]{1,0:T(8,128)(2,1)S(1)} %get-tuple-element.48), channel_id=1, source_target_pairs={{0,6},{1,7},{2,4},{3,5},{4,2},{5,3},{6,0},{7,1},{8,14},{9,15},{10,... | collective-permute-start | bytes 98312 | tf_op jit(solution)/shard_map/ppermute | solution.py:64

commit v9 on v7

--- a/solution.py
+++ b/solution.py
@@ -178,7 +178,7 @@
     others = to_group(in_order)
     two = to_neighbour(chosen(first, mid_w))
     far_w = to_middle(near_w)
-    mid_d = to_middle(tie(own_d, near_w))
+    mid_d = to_middle(tie(own_d, mid_w))
     three = to_neighbour(chosen(second, far_w))
     near_d = two[0:half]
     mid_e = to_group(tie(mid_d, others, near_d))

time: 63.7 us -> 63.7 us (level)
  no operation moved by 1% of the time
where the time goes in v9:
time: 63.7 us; the launch traced here: 63.5 us
  starting transfers between devices  36.1 us (57%)
  waiting for transfers between devices  19.8 us (31%)
  Pallas kernels  6.03 us (9%)
  local copies, waits for them, and re-layouts  1.29 us (2%)
    ppermute x18, starting transfers between devices, swap(): return lax.ppermute(x, AXES, perm)  36.1 us
    ppermute x18, waiting for transfers between devices, swap(): return lax.ppermute(x, AXES, perm)  19.8 us
    pallas_call x11, Pallas kernels, call(): pl.pallas_call(lambda *refs: body(Place(), *refs), name=name, out_shape=o...  6.03 us
  transfers between devices with their start and end apart: 18, of which 5 were waited for; matrix products, arithmetic and copies ran while one was open for 0% of the time, Pallas kernels for 8%

profile of v9, /device:TPU:0, one launch (start us, length us, event | category | flops | bytes accessed | tf_op | source)
XLA Modules:
  0.0 63.5 jit_solution(3221643879772187207)
XLA Ops:
  0.0 0.8 %dynamic-slice_bitcast_fusion = bf16[64,256]{1,0:T(8,128)(2,1)S(1)} fusion(bf16[2,64,256]{2,1,0:T(8,128)(2,1)} %param.10, s32[]{:T(128)S(6)} %select_n.8), kind=kLoop, calls=%fused_computation.1 | loop fusion | bytes 65540 | tf_op jit(solution)/shard_map/jit(dynamic_index_in_dim)/squeeze | solution.py:104
  0.9 0.0 copy-start.1
  0.9 0.4 copy-done
  1.3 3.1 %collective-permute-start = (bf16[2176,128]{1,0:T(8,128)(2,1)S(1)}, bf16[2176,128]{1,0:T(8,128)(2,1)S(1)}, u32[]{:S(2)}, u32[]{:S(2)}) collective-permute-start(bf16[2176,128]{1,0:T(8,128)(2,1)S(1)} %pad_maximum_fusion.refs_0_.refs_2_), channel_id=1, source_target_pairs={{0,4},{1,5},{2,6},{3,7},{4,0},{5,1},{6,2},{7,3},{8,12},{9,13},{10,... | collective-permute-start | bytes 1671176 | tf_op jit(solution)/shard_map/ppermute | solution.py:64
  4.4 0.1 pad_add_fusion.refs_0_
  4.5 0.8 %sort_blocks.1.refs_0_ = bf16[272,2048]{1,0:T(8,128)(2,1)S(1)} custom-call(s32[16]{0:T(128)S(1)} %pad_add_fusion.refs_0_, bf16[256,2048]{1,0:T(8,128)(2,1)S(1)} %copy-done.1), custom_call_target="tpu_custom_call" | custom-call | tf_op jit(solution)/shard_map/sort_blocks/pallas_call | solution.py:24
  5.3 1.6 %collective-permute-start.6 = (bf16[272,2048]{1,0:T(8,128)(2,1)S(1)}, bf16[272,2048]{1,0:T(8,128)(2,1)S(1)}, u32[]{:S(2)}, u32[]{:S(2)}) collective-permute-start(bf16[272,2048]{1,0:T(8,128)(2,1)S(1)} %sort_blocks.1.refs_0_), channel_id=1, source_target_pairs={{0,16},{1,17},{2,18},{3,19},{4,20},{5,21},{6,22},{7,23},{8,24},{9,... | collective-permute-start | bytes 3342344 | tf_op jit(solution)/shard_map/ppermute | solution.py:64
  6.9 10.1 %collective-permute-done.refs_1_.refs_3_ = bf16[2176,128]{1,0:T(8,128)(2,1)S(1)} collective-permute-done((bf16[2176,128]{1,0:T(8,128)(2,1)S(1)}, bf16[2176,128]{1,0:T(8,128)(2,1)S(1)}, u32[]{:S(2)}, u32[]{:S(2)}) %collective-permute-start) | collective-permute-done | bytes 557088 | tf_op jit(solution)/shard_map/ppermute | solution.py:64
  17.1 0.3 pack_shrinks.1
  17.4 0.1 choose.2
  17.4 3.4 %collective-permute-start.3 = (bf16[2176,128]{1,0:T(8,128)(2,1)S(1)}, bf16[2176,128]{1,0:T(8,128)(2,1)S(1)}, u32[]{:S(2)}, u32[]{:S(2)}) collective-permute-start(bf16[2176,128]{1,0:T(8,128)(2,1)S(1)} %choose.2), channel_id=1, source_target_pairs={{0,4},{1,5},{2,6},{3,7},{4,0},{5,1},{6,2},{7,3},{8,12},{9,13},{10,... | collective-permute-start | bytes 1671176 | tf_op jit(solution)/shard_map/ppermute | solution.py:64
  20.9 13.6 %collective-permute-start.4 = (bf16[2176,128]{1,0:T(8,128)(2,1)S(1)}, bf16[2176,128]{1,0:T(8,128)(2,1)S(1)}, u32[]{:S(2)}, u32[]{:S(2)}) collective-permute-start(bf16[2176,128]{1,0:T(8,128)(2,1)S(1)} %choose.3), channel_id=1, source_target_pairs={{0,4},{1,5},{2,6},{3,7},{4,0},{5,1},{6,2},{7,3},{8,12},{9,13},{10,... | collective-permute-start | bytes 1671176 | tf_op jit(solution)/shard_map/ppermute | solution.py:64
  34.5 1.6 %collective-permute-start.8 = (bf16[1024,128]{1,0:T(8,128)(2,1)S(1)}, bf16[1024,128]{1,0:T(8,128)(2,1)S(1)}, u32[]{:S(2)}, u32[]{:S(2)}) collective-permute-start(bf16[1024,128]{1,0:T(8,128)(2,1)S(1)} %collective-permute-done.7.refs_4_), channel_id=1, source_target_pairs={{0,16},{1,17},{2,18},{3,19},{4,20},{5,21},{6,22},{7,23},{8,24},{9,... | collective-permute-start | bytes 786440 | tf_op jit(solution)/shard_map/ppermute | solution.py:64
  36.1 5.4 %collective-permute-done.8.refs_5_ = bf16[1024,128]{1,0:T(8,128)(2,1)S(1)} collective-permute-done((bf16[1024,128]{1,0:T(8,128)(2,1)S(1)}, bf16[1024,128]{1,0:T(8,128)(2,1)S(1)}, u32[]{:S(2)}, u32[]{:S(2)}) %collective-permute-start.8) | collective-permute-done | bytes 262176 | tf_op jit(solution)/shard_map/ppermute | solution.py:64
  41.5 1.7 %collective-permute-start.11 = (bf16[1024,128]{1,0:T(8,128)(2,1)S(1)}, bf16[1024,128]{1,0:T(8,128)(2,1)S(1)}, u32[]{:S(2)}, u32[]{:S(2)}) collective-permute-start(bf16[1024,128]{1,0:T(8,128)(2,1)S(1)} %collective-permute-done.10.refs_4_), channel_id=1, source_target_pairs={{0,16},{1,17},{2,18},{3,19},{4,20},{5,21},{6,22},{7,23},{8,24},{9,... | collective-permute-start | bytes 786440 | tf_op jit(solution)/shard_map/ppermute | solution.py:64
  43.2 2.1 %early_columns.1 = (f32[1536,128]{1,0:T(8,128)S(1)}, f32[3,256,64]{2,1,0:T(8,128)S(1)}) custom-call(bf16[272,2048]{1,0:T(8,128)(2,1)S(1)} %sort_blocks.1.refs_0_, bf16[272,2048]{1,0:T(8,128)(2,1)S(1)} %collective-permute-done.6.refs_1_, bf16[2176,128]{1,0:T(8,128)(2,1)S(1)} %pad_maximum_fusion.refs_0_.refs_2_, ...), custom_call_target="tpu_custom_call" | custom-call | tf_op jit(solution)/shard_map/early_columns/pallas_call | solution.py:24
  45.3 0.8 %last_columns.1 = (f32[1024,128]{1,0:T(8,128)S(1)}, bf16[1024,128]{1,0:T(8,128)(2,1)S(1)}, f32[3,256,64]{2,1,0:T(8,128)S(1)}) custom-call(bf16[272,2048]{1,0:T(8,128)(2,1)S(1)} %sort_blocks.1.refs_0_, bf16[272,2048]{1,0:T(8,128)(2,1)S(1)} %collective-permute-done.6.refs_1_, bf16[2176,128]{1,0:T(8,128)(2,1)S(1)} %collective-permute-done.3.refs_4_.refs_5_.refs_2_, ...), custom_call_target="tpu_custom_call" | custom-call | tf_op jit(solution)/shard_map/last_columns/pallas_call | solution.py:24
  46.2 0.1 collective-permute-start.9
  46.2 1.6 %collective-permute-done.11.refs_5_ = bf16[1024,128]{1,0:T(8,128)(2,1)S(1)} collective-permute-done((bf16[1024,128]{1,0:T(8,128)(2,1)S(1)}, bf16[1024,128]{1,0:T(8,128)(2,1)S(1)}, u32[]{:S(2)}, u32[]{:S(2)}) %collective-permute-start.11) | collective-permute-done | bytes 262176 | tf_op jit(solution)/shard_map/ppermute | solution.py:64
  47.8 0.1 last_shrinks.1
  48.0 0.1 collective-permute-start.12
  48.1 1.8 %collective-permute-start.5 = (bf16[512,128]{1,0:T(8,128)(2,1)S(1)}, bf16[512,128]{1,0:T(8,128)(2,1)S(1)}, u32[]{:S(2)}, u32[]{:S(2)}) collective-permute-start(bf16[512,128]{1,0:T(8,128)(2,1)S(1)} %gather_ups.1.refs_1_), channel_id=1, source_target_pairs={{0,16},{1,17},{2,18},{3,19},{4,20},{5,21},{6,22},{7,23},{8,24},{9,... | collective-permute-start | bytes 393224 | tf_op jit(solution)/shard_map/ppermute | solution.py:64
  49.9 0.1 add_cores.1
  49.9 1.6 %collective-permute-start.13 = (bf16[384,128]{1,0:T(8,128)(2,1)S(1)}, bf16[384,128]{1,0:T(8,128)(2,1)S(1)}, u32[]{:S(2)}, u32[]{:S(2)}) collective-permute-start(bf16[384,128]{1,0:T(8,128)(2,1)S(1)} %get-tuple-element.43), channel_id=1, source_target_pairs={{0,2},{1,3},{2,0},{3,1},{4,6},{5,7},{6,4},{7,5},{8,10},{9,11},{10,... | collective-permute-start | bytes 294920 | tf_op jit(solution)/shard_map/ppermute | solution.py:64
  51.5 1.2 %collective-permute-start.14 = (bf16[384,128]{1,0:T(8,128)(2,1)S(1)}, bf16[384,128]{1,0:T(8,128)(2,1)S(1)}, u32[]{:S(2)}, u32[]{:S(2)}) collective-permute-start(bf16[384,128]{1,0:T(8,128)(2,1)S(1)} %get-tuple-element.44), channel_id=1, source_target_pairs={{0,16},{1,17},{2,18},{3,19},{4,20},{5,21},{6,22},{7,23},{8,24},{9,... | collective-permute-start | bytes 294920 | tf_op jit(solution)/shard_map/ppermute | solution.py:64
  52.7 0.8 %collective-permute-start.15 = (bf16[384,128]{1,0:T(8,128)(2,1)S(1)}, bf16[384,128]{1,0:T(8,128)(2,1)S(1)}, u32[]{:S(2)}, u32[]{:S(2)}) collective-permute-start(bf16[384,128]{1,0:T(8,128)(2,1)S(1)} %get-tuple-element.45), channel_id=1, source_target_pairs={{0,18},{1,19},{2,16},{3,17},{4,22},{5,23},{6,20},{7,21},{8,26},{9,... | collective-permute-start | bytes 294920 | tf_op jit(solution)/shard_map/ppermute | solution.py:64
  53.5 5.2 %collective-permute-start.17 = (bf16[128,128]{1,0:T(8,128)(2,1)S(1)}, bf16[128,128]{1,0:T(8,128)(2,1)S(1)}, u32[]{:S(2)}, u32[]{:S(2)}) collective-permute-start(bf16[128,128]{1,0:T(8,128)(2,1)S(1)} %get-tuple-element.46), channel_id=1, source_target_pairs={{0,6},{1,7},{2,4},{3,5},{4,2},{5,3},{6,0},{7,1},{8,14},{9,15},{10,... | collective-permute-start | bytes 98312 | tf_op jit(solution)/shard_map/ppermute | solution.py:64
  58.7 0.5 collective-permute-start.16
  59.2 0.7 %ups.1 = (bf16[4,128,128]{2,1,0:T(8,128)(2,1)S(1)}, f32[24,128]{1,0:T(8,128)S(1)}) custom-call(s32[16]{0:T(128)S(1)} %pad_add_fusion.refs_0_, bf16[512,128]{1,0:T(8,128)(2,1)S(1)} %gather_ups.1.refs_1_, bf16[512,128]{1,0:T(8,128)(2,1)S(1)} %collective-permute-done.5.refs_2_), custom_call_target="tpu_custom_call" | custom-call | tf_op jit(solution)/shard_map/ups/pallas_call | solution.py:24
  60.0 0.9 %collective-permute-done.17.refs_7_ = bf16[128,128]{1,0:T(8,128)(2,1)S(1)} collective-permute-done((bf16[128,128]{1,0:T(8,128)(2,1)S(1)}, bf16[128,128]{1,0:T(8,128)(2,1)S(1)}, u32[]{:S(2)}, u32[]{:S(2)}) %collective-permute-start.17) | collective-permute-done | bytes 32800 | tf_op jit(solution)/shard_map/ppermute | solution.py:64
  60.9 1.7 %collective-permute-done.16.refs_6_ = bf16[128,128]{1,0:T(8,128)(2,1)S(1)} collective-permute-done((bf16[128,128]{1,0:T(8,128)(2,1)S(1)}, bf16[128,128]{1,0:T(8,128)(2,1)S(1)}, u32[]{:S(2)}, u32[]{:S(2)}) %collective-permute-start.16) | collective-permute-done | bytes 32800 | tf_op jit(solution)/shard_map/ppermute | solution.py:64
  62.6 0.9 %finish.1 = bf16[256,256]{1,0:T(8,128)(2,1)} custom-call(f32[24,128]{1,0:T(8,128)S(1)} %get-tuple-element.28.refs_0_, bf16[4,128,128]{2,1,0:T(8,128)(2,1)S(1)} %get-tuple-element.29.refs_1_, f32[384,128]{1,0:T(8,128)S(1)} %get-tuple-element.42.refs_2_, bf16[384,128]{1,0:T(8,128)(2,1)S(1)} %collective-permute-done.13.refs_3_, ...), custom_call_target="tpu_custom_call" | custom-call | tf_op jit(solution)/shard_map/finish/pallas_call | solution.py:24
  (33 shorter events, 0.2 us)
Async XLA Ops:
  0.0 1.2 %copy-start = (bf16[2048,256]{1,0:T(8,128)(2,1)S(1)}, bf16[2048,256]{1,0:T(8,128)(2,1)}, u32[]{:S(2)}) copy-start(bf16[2048,256]{1,0:T(8,128)(2,1)} %param.8) | copy-start | bytes 3145732
  0.9 3.6 %copy-start.3 = (s32[4]{0:T(128)S(1)}, s32[4]{0:T(128)}, u32[]{:S(2)}) copy-start(s32[4]{0:T(128)} %param.13) | copy-start | bytes 52
  0.9 3.6 %copy-start.4 = (s32[4]{0:T(128)S(1)}, s32[4]{0:T(128)}, u32[]{:S(2)}) copy-start(s32[4]{0:T(128)} %param.12) | copy-start | bytes 52
  0.9 3.6 %copy-start.5 = (s32[8]{0:T(128)S(1)}, s32[8]{0:T(128)}, u32[]{:S(2)}) copy-start(s32[8]{0:T(128)} %param.11) | copy-start | bytes 100
  0.9 3.7 %copy-start.1 = (bf16[256,2048]{1,0:T(8,128)(2,1)S(1)}, bf16[256,2048]{1,0:T(8,128)(2,1)}, u32[]{:S(2)}) copy-start(bf16[256,2048]{1,0:T(8,128)(2,1)} %refs_1_.1) | copy-start | bytes 3145732
  1.3 15.7 %copy-start.2 = (bf16[2,2048,64]{1,2,0:T(8,128)(2,1)S(1)}, bf16[2,2048,64]{1,2,0:T(8,128)(2,1)}, u32[]{:S(2)}) copy-start(bf16[2,2048,64]{1,2,0:T(8,128)(2,1)} %param.9) | copy-start | bytes 1572868
  1.3 15.7 %collective-permute-start = (bf16[2176,128]{1,0:T(8,128)(2,1)S(1)}, bf16[2176,128]{1,0:T(8,128)(2,1)S(1)}, u32[]{:S(2)}, u32[]{:S(2)}) collective-permute-start(bf16[2176,128]{1,0:T(8,128)(2,1)S(1)} %pad_maximum_fusion.refs_0_.refs_2_), channel_id=1, source_target_pairs={{0,4},{1,5},{2,6},{3,7},{4,0},{5,1},{6,2},{7,3},{8,12},{9,13},{10,... | collective-permute-start | bytes 1671176 | tf_op jit(solution)/shard_map/ppermute | solution.py:64
  4.4 12.9 %collective-permute-start.1 = (bf16[2176,128]{1,0:T(8,128)(2,1)S(1)}, bf16[2176,128]{1,0:T(8,128)(2,1)S(1)}, u32[]{:S(2)}, u32[]{:S(2)}) collective-permute-start(bf16[2176,128]{1,0:T(8,128)(2,1)S(1)} %pad_maximum_fusion.refs_0_.refs_2_), channel_id=1, source_target_pairs={{0,1},{1,0},{2,3},{3,2},{4,8},{5,9},{6,10},{7,11},{8,4},{9,5},{10,... | collective-permute-start | bytes 1671176 | tf_op jit(solution)/shard_map/ppermute | solution.py:64
  5.3 29.2 %collective-permute-start.6 = (bf16[272,2048]{1,0:T(8,128)(2,1)S(1)}, bf16[272,2048]{1,0:T(8,128)(2,1)S(1)}, u32[]{:S(2)}, u32[]{:S(2)}) collective-permute-start(bf16[272,2048]{1,0:T(8,128)(2,1)S(1)} %sort_blocks.1.refs_0_), channel_id=1, source_target_pairs={{0,16},{1,17},{2,18},{3,19},{4,20},{5,21},{6,22},{7,23},{8,24},{9,... | collective-permute-start | bytes 3342344 | tf_op jit(solution)/shard_map/ppermute | solution.py:64
  17.1 3.8 %collective-permute-start.2 = (bf16[2176,128]{1,0:T(8,128)(2,1)S(1)}, bf16[2176,128]{1,0:T(8,128)(2,1)S(1)}, u32[]{:S(2)}, u32[]{:S(2)}) collective-permute-start(bf16[2176,128]{1,0:T(8,128)(2,1)S(1)} %collective-permute-done.refs_1_.refs_3_), channel_id=1, source_target_pairs={{0,1},{1,0},{2,3},{3,2},{4,8},{5,9},{6,10},{7,11},{8,4},{9,5},{10,... | collective-permute-start | bytes 1671176 | tf_op jit(solution)/shard_map/ppermute | solution.py:64
  17.4 17.0 %collective-permute-start.3 = (bf16[2176,128]{1,0:T(8,128)(2,1)S(1)}, bf16[2176,128]{1,0:T(8,128)(2,1)S(1)}, u32[]{:S(2)}, u32[]{:S(2)}) collective-permute-start(bf16[2176,128]{1,0:T(8,128)(2,1)S(1)} %choose.2), channel_id=1, source_target_pairs={{0,4},{1,5},{2,6},{3,7},{4,0},{5,1},{6,2},{7,3},{8,12},{9,13},{10,... | collective-permute-start | bytes 1671176 | tf_op jit(solution)/shard_map/ppermute | solution.py:64
  20.8 13.7 %collective-permute-start.7 = (bf16[1024,128]{1,0:T(8,128)(2,1)S(1)}, bf16[1024,128]{1,0:T(8,128)(2,1)S(1)}, u32[]{:S(2)}, u32[]{:S(2)}) collective-permute-start(bf16[1024,128]{1,0:T(8,128)(2,1)S(1)} %get-tuple-element.31.refs_6_), channel_id=1, source_target_pairs={{0,1},{1,0},{2,3},{3,2},{4,8},{5,9},{6,10},{7,11},{8,4},{9,5},{10,... | collective-permute-start | bytes 786440 | tf_op jit(solution)/shard_map/ppermute | solution.py:64
  20.9 24.4 %collective-permute-start.4 = (bf16[2176,128]{1,0:T(8,128)(2,1)S(1)}, bf16[2176,128]{1,0:T(8,128)(2,1)S(1)}, u32[]{:S(2)}, u32[]{:S(2)}) collective-permute-start(bf16[2176,128]{1,0:T(8,128)(2,1)S(1)} %choose.3), channel_id=1, source_target_pairs={{0,4},{1,5},{2,6},{3,7},{4,0},{5,1},{6,2},{7,3},{8,12},{9,13},{10,... | collective-permute-start | bytes 1671176 | tf_op jit(solution)/shard_map/ppermute | solution.py:64
  34.5 7.0 %collective-permute-start.8 = (bf16[1024,128]{1,0:T(8,128)(2,1)S(1)}, bf16[1024,128]{1,0:T(8,128)(2,1)S(1)}, u32[]{:S(2)}, u32[]{:S(2)}) collective-permute-start(bf16[1024,128]{1,0:T(8,128)(2,1)S(1)} %collective-permute-done.7.refs_4_), channel_id=1, source_target_pairs={{0,16},{1,17},{2,18},{3,19},{4,20},{5,21},{6,22},{7,23},{8,24},{9,... | collective-permute-start | bytes 786440 | tf_op jit(solution)/shard_map/ppermute | solution.py:64
  36.1 5.4 %collective-permute-start.10 = (bf16[1024,128]{1,0:T(8,128)(2,1)S(1)}, bf16[1024,128]{1,0:T(8,128)(2,1)S(1)}, u32[]{:S(2)}, u32[]{:S(2)}) collective-permute-start(bf16[1024,128]{1,0:T(8,128)(2,1)S(1)} %slice.14), channel_id=1, source_target_pairs={{0,1},{1,0},{2,3},{3,2},{4,8},{5,9},{6,10},{7,11},{8,4},{9,5},{10,... | collective-permute-start | bytes 786440 | tf_op jit(solution)/shard_map/ppermute | solution.py:64
  41.5 6.4 %collective-permute-start.11 = (bf16[1024,128]{1,0:T(8,128)(2,1)S(1)}, bf16[1024,128]{1,0:T(8,128)(2,1)S(1)}, u32[]{:S(2)}, u32[]{:S(2)}) collective-permute-start(bf16[1024,128]{1,0:T(8,128)(2,1)S(1)} %collective-permute-done.10.refs_4_), channel_id=1, source_target_pairs={{0,16},{1,17},{2,18},{3,19},{4,20},{5,21},{6,22},{7,23},{8,24},{9,... | collective-permute-start | bytes 786440 | tf_op jit(solution)/shard_map/ppermute | solution.py:64
  46.2 3.7 %collective-permute-start.9 = (bf16[1024,128]{1,0:T(8,128)(2,1)S(1)}, bf16[1024,128]{1,0:T(8,128)(2,1)S(1)}, u32[]{:S(2)}, u32[]{:S(2)}) collective-permute-start(bf16[1024,128]{1,0:T(8,128)(2,1)S(1)} %get-tuple-element.37), channel_id=1, source_target_pairs={{0,1},{1,0},{2,3},{3,2},{4,5},{5,4},{6,7},{7,6},{8,9},{9,8},{10,11... | collective-permute-start | bytes 786440 | tf_op jit(solution)/shard_map/ppermute | solution.py:64
  48.0 1.9 %collective-permute-start.12 = (bf16[384,128]{1,0:T(8,128)(2,1)S(1)}, bf16[384,128]{1,0:T(8,128)(2,1)S(1)}, u32[]{:S(2)}, u32[]{:S(2)}) collective-permute-start(bf16[384,128]{1,0:T(8,128)(2,1)S(1)} %get-tuple-element.41), channel_id=1, source_target_pairs={{0,1},{1,0},{2,3},{3,2},{4,5},{5,4},{6,7},{7,6},{8,9},{9,8},{10,11... | collective-permute-start | bytes 294920 | tf_op jit(solution)/shard_map/ppermute | solution.py:64
  48.1 10.6 %collective-permute-start.5 = (bf16[512,128]{1,0:T(8,128)(2,1)S(1)}, bf16[512,128]{1,0:T(8,128)(2,1)S(1)}, u32[]{:S(2)}, u32[]{:S(2)}) collective-permute-start(bf16[512,128]{1,0:T(8,128)(2,1)S(1)} %gather_ups.1.refs_1_), channel_id=1, source_target_pairs={{0,16},{1,17},{2,18},{3,19},{4,20},{5,21},{6,22},{7,23},{8,24},{9,... | collective-permute-start | bytes 393224 | tf_op jit(solution)/shard_map/ppermute | solution.py:64
  49.9 12.7 %collective-permute-start.13 = (bf16[384,128]{1,0:T(8,128)(2,1)S(1)}, bf16[384,128]{1,0:T(8,128)(2,1)S(1)}, u32[]{:S(2)}, u32[]{:S(2)}) collective-permute-start(bf16[384,128]{1,0:T(8,128)(2,1)S(1)} %get-tuple-element.43), channel_id=1, source_target_pairs={{0,2},{1,3},{2,0},{3,1},{4,6},{5,7},{6,4},{7,5},{8,10},{9,11},{10,... | collective-permute-start | bytes 294920 | tf_op jit(solution)/shard_map/ppermute | solution.py:64
  51.5 11.1 %collective-permute-start.14 = (bf16[384,128]{1,0:T(8,128)(2,1)S(1)}, bf16[384,128]{1,0:T(8,128)(2,1)S(1)}, u32[]{:S(2)}, u32[]{:S(2)}) collective-permute-start(bf16[384,128]{1,0:T(8,128)(2,1)S(1)} %get-tuple-element.44), channel_id=1, source_target_pairs={{0,16},{1,17},{2,18},{3,19},{4,20},{5,21},{6,22},{7,23},{8,24},{9,... | collective-permute-start | bytes 294920 | tf_op jit(solution)/shard_map/ppermute | solution.py:64
  52.7 10.0 %collective-permute-start.15 = (bf16[384,128]{1,0:T(8,128)(2,1)S(1)}, bf16[384,128]{1,0:T(8,128)(2,1)S(1)}, u32[]{:S(2)}, u32[]{:S(2)}) collective-permute-start(bf16[384,128]{1,0:T(8,128)(2,1)S(1)} %get-tuple-element.45), channel_id=1, source_target_pairs={{0,18},{1,19},{2,16},{3,17},{4,22},{5,23},{6,20},{7,21},{8,26},{9,... | collective-permute-start | bytes 294920 | tf_op jit(solution)/shard_map/ppermute | solution.py:64
  53.5 7.4 %collective-permute-start.17 = (bf16[128,128]{1,0:T(8,128)(2,1)S(1)}, bf16[128,128]{1,0:T(8,128)(2,1)S(1)}, u32[]{:S(2)}, u32[]{:S(2)}) collective-permute-start(bf16[128,128]{1,0:T(8,128)(2,1)S(1)} %get-tuple-element.46), channel_id=1, source_target_pairs={{0,6},{1,7},{2,4},{3,5},{4,2},{5,3},{6,0},{7,1},{8,14},{9,15},{10,... | collective-permute-start | bytes 98312 | tf_op jit(solution)/shard_map/ppermute | solution.py:64
  58.7 3.9 %collective-permute-start.16 = (bf16[128,128]{1,0:T(8,128)(2,1)S(1)}, bf16[128,128]{1,0:T(8,128)(2,1)S(1)}, u32[]{:S(2)}, u32[]{:S(2)}) collective-permute-start(bf16[128,128]{1,0:T(8,128)(2,1)S(1)} %get-tuple-element.46), channel_id=1, source_target_pairs={{0,4},{1,5},{2,6},{3,7},{4,0},{5,1},{6,2},{7,3},{8,12},{9,13},{10,... | collective-permute-start | bytes 98312 | tf_op jit(solution)/shard_map/ppermute | solution.py:64
